TPU v7x, 32 devices: a whole 2x2x4 slice. The times are simulated.
32 devices in a mesh: sector: 16 (over z, x, core), blk: 2 (over y).
Axes of the slice: x: 2, y: 2, z: 4, core: 2. Of those that a mesh axis runs over, the one named last changes fastest.
Arguments:
- signal: bfloat16 [4, 4096, 8192], P('blk', 'sector'), may hold values from -6 to 6
- offsets: int32 [4], P('blk'), may hold values from 0 to 4095
- fraction: float32 [4, 8192], P('blk'), may hold values from 0 to 1
- radius: float32 [256], replicated, may hold values from 0.2 to 0.9
- azimuth: float32 [256], replicated, may hold values from -3.140625 to 3.140625
Outputs:
- power: float32 [512, 256], P(('sector', 'blk'))
All inputs are finite; a program needn't handle non-finite values.
Results may differ from a plain program's by a relative error of at most 0.00095.
Values may be sent and summed in bfloat16 or wider, within the bound.
A program may use at most 128 MiB of HBM per device.

v0:
```python
import math

import jax
import jax.numpy as jnp
from jax import lax
from jax.sharding import PartitionSpec as P

NFFT = 1024


wavenumber = 2.0
height = 0.5


def from_behind(x, axis, by):
    size = lax.axis_size(axis)
    return lax.ppermute(x, axis, [(i, (i + by) % size) for i in range(size)])


def fourier_table(groups):
    half_bins = NFFT // 2
    per_group = half_bins // groups
    sample = lax.iota(jnp.int32, NFFT)[:, None]
    column = lax.iota(jnp.int32, 2 * half_bins)[None, :]
    group = column // (2 * per_group)
    part = column // per_group % 2
    inner = column % per_group
    frequency = group * per_group + inner
    turns = (sample * frequency % NFFT).astype(jnp.float32)
    angle = turns * (2.0 * math.pi / NFFT)
    window = 0.5 - 0.5 * jnp.cos(sample.astype(jnp.float32) * (2.0 * math.pi / NFFT))
    value = jnp.where(part == 0, jnp.cos(angle), -jnp.sin(angle))
    return (value * window / math.sqrt(3.0 * NFFT / 8.0)).astype(jnp.bfloat16)


def distances(radius, azimuth, total_mics):
    turn = lax.iota(jnp.int32, total_mics).astype(jnp.float32) * (2.0 * math.pi / total_mics)
    cycle_cos = jnp.cos(turn)[:, None]
    cycle_sin = jnp.sin(turn)[:, None]
    across = (radius * jnp.cos(azimuth))[None, :]
    along = (radius * jnp.sin(azimuth))[None, :]
    squared = (
        1.0
        + height * height
        + (radius * radius)[None, :]
        - 2.0 * (cycle_cos * across + cycle_sin * along)
    )
    return jnp.sqrt(squared)


def steering(frequency, distance):
    phase = wavenumber * frequency.astype(jnp.float32) * distance
    return jnp.concatenate([jnp.cos(phase), jnp.sin(phase)], 1).astype(jnp.bfloat16)


def interpolate(window_rows, weight):
    lower = window_rows[:, :-1].astype(jnp.float32)
    upper = window_rows[:, 1:].astype(jnp.float32)
    spread_weight = weight[:, None, :]
    return ((1.0 - spread_weight) * lower + spread_weight * upper).astype(jnp.bfloat16)


def segment_spectra(virtual, table):
    blocks, mics, length = virtual.shape
    half = NFFT // 2
    halves = virtual.reshape(blocks, mics, length // half, half)
    upper = jnp.einsum(
        "bmhn,nc->bhcm", halves[:, :, :-1], table[:half], preferred_element_type=jnp.float32
    )
    lower = jnp.einsum(
        "bmhn,nc->bhcm", halves[:, :, 1:], table[half:], preferred_element_type=jnp.float32
    )
    return (upper + lower).astype(jnp.bfloat16)


def band_power(flat, first, count, distance):
    snapshots = flat.shape[0]
    points = distance.shape[1]

    def one_bin(bin_place):
        picked = lax.dynamic_index_in_dim(flat, bin_place, 2, keepdims=False)
        stacked = jnp.concatenate([picked[:, 0], picked[:, 1]], 0)
        steer = steering(first + bin_place, distance)
        product = jnp.dot(stacked, steer, preferred_element_type=jnp.float32)
        along = product[:snapshots, :points] + product[snapshots:, points:]
        across = product[snapshots:, :points] - product[:snapshots, points:]
        return jnp.sum(along * along + across * across, 0)

    return lax.map(one_bin, jnp.arange(count, dtype=jnp.int32))


def local(signal, offsets, fraction, radius, azimuth):
    blocks, mics, length = signal.shape
    sectors = lax.axis_size("sector")
    sector_index = lax.axis_index("sector")
    total_mics = mics * sectors
    edge_row = from_behind(signal[:, :1, :], "sector", -1)
    virtual = interpolate(jnp.concatenate([signal, edge_row], 1), fraction)
    spectra = segment_spectra(virtual, fourier_table(sectors))
    banded = lax.all_to_all(spectra, "sector", split_axis=2, concat_axis=3, tiled=True)
    doubled_bands = jnp.concatenate([banded, banded], 3)
    banded = jax.vmap(lambda rows, start: lax.dynamic_slice_in_dim(rows, start, total_mics, 2))(
        doubled_bands, offsets
    )
    segments = banded.shape[1]
    per_sector = banded.shape[2] // 2
    grouped = banded.reshape(blocks, segments, 2, per_sector, total_mics)
    distance = distances(radius, azimuth, total_mics)
    scale = 1.0 / (total_mics * blocks * segments * lax.axis_size("blk"))
    flat = grouped.reshape(blocks * segments, 2, per_sector, total_mics)
    partial_power = band_power(flat, sector_index * per_sector, per_sector, distance) * scale
    return lax.psum_scatter(partial_power, "blk", scatter_dimension=0, tiled=True)


def solution(mesh):
    return jax.shard_map(
        local,
        mesh=mesh,
        in_specs=(P("blk", "sector", None), P("blk"), P("blk", None), P(), P()),
        out_specs=P(("sector", "blk"), None),
        check_vma=False,
    )
```

profile of v0, /device:TPU:0, one launch (start us, length us, event | category | flops | bytes accessed | tf_op | source)
XLA Modules:
  0.0 1411.6 jit_solution(15494116423828833752)
XLA Ops:
  7.6 5.5 collective-permute-start
  14.0 18.2 %multiply_convert_fusion = bf16[1024,1024]{0,1:T(8,128)(2,1)S(1)} fusion(f32[1024]{0:T(1024)S(1)} %multiply_subtract_fusion, s32[1024]{0:T(1024)S(1)} %fusion.40, pred[1024]{0:T(1024)(128)(4,1)S(1)} %fusion.37), kind=kLoop, calls=%fused_computation.39 | loop fusion | flops 19922944 | bytes 2106368 | tf_op jit(solution)/shard_map/convert_element_type | solution.py:33
  32.2 11.9 copy.34
  44.1 3.4 copy.37
  47.5 14.1 add_convert_fusion.1
  61.6 3.3 copy-done
  64.9 13.8 fusion.20
  78.7 22.1 %fusion.18 = bf16[2,15,1024,256]{3,2,1,0:T(8,128)(2,1)} fusion(f32[1024,2,256,15]{2,0,3,1:T(8,128)} %fusion.20, bf16[2,256,16,512]{1,3,2,0:T(8,128)(2,1)} %bitcast.45, bf16[1024,1024]{0,1:T(8,128)(2,1)S(1)} %multiply_convert_fusion), kind=kOutput, calls=%fused_computation.28 | convolution fusion | flops 8068792320 | bytes 56098816 | tf_op jit(solution)/shard_map/bmhn,nc->bhcm/dot_general | solution.py:70
  100.8 29.3 %copy.40 = bf16[2,15,1024,256]{3,0,1,2:T(2,128)(2,1)} copy(bf16[2,15,1024,256]{3,2,1,0:T(8,128)(2,1)} %fusion.18) | data formatting | bytes 31457280 | tf_op jit(solution)/shard_map/convert_element_type | solution.py:73
  130.1 5.2 all-to-all-start
  135.9 277.9 %all-to-all-done = bf16[2,15,1024,256]{3,0,1,2:T(2,128)(2,1)} async-done(((bf16[2,15,1024,256]{3,0,1,2:T(2,128)(2,1)}), bf16[2,15,1024,256]{3,0,1,2:T(2,128)(2,1)}, u32[]{:S(2)}, u32[]{:S(2)}) %all-to-all-start) | async-done | bytes 15728672 | tf_op jit(solution)/shard_map/all_to_all | solution.py:100
  413.8 15.3 %copy.41 = bf16[2,15,64,16,256]{4,3,2,1,0:T(8,128)(2,1)} copy(bf16[2,15,64,16,256]{4,0,1,2,3:T(2,128)(2,1)} %bitcast.7) | data formatting | bytes 31457280 | tf_op jit(solution)/shard_map/all_to_all | solution.py:100
  429.0 24.1 %all_to_all.16 = bf16[2,15,64,4096]{3,2,1,0:T(8,128)(2,1)} reshape(bf16[2,15,64,16,256]{4,3,2,1,0:T(8,128)(2,1)} %copy.41) | data formatting | bytes 31457280 | tf_op jit(solution)/shard_map/all_to_all | solution.py:100
  453.1 21.3 %pad_maximum_fusion = bf16[2,15,64,8192]{3,2,1,0:T(8,128)(2,1)} fusion(bf16[2,15,64,4096]{3,2,1,0:T(8,128)(2,1)} %all_to_all.16), kind=kLoop, calls=%fused_computation.25 | loop fusion | flops 62914560 | bytes 47185920 | tf_op jit(solution)/shard_map/concatenate | solution.py:101
  474.4 24.1 %while.12 = (s32[]{:T(128)}, bf16[2,15,64,8192]{3,2,1,0:T(8,128)(2,1)}, s32[2,4]{1,0:T(2,128)S(1)}, bf16[2,15,64,4096]{3,2,1,0:T(8,128)(2,1)}, s32[]{:T(128)}) while((s32[]{:T(128)}, bf16[2,15,64,8192]{3,2,1,0:T(8,128)(2,1)}, s32[2,4]{1,0:T(2,128)S(1)}, bf16[2,15,64,4096]{3,2,1,0:T(8,128)(2,1)}, s32[]{:T(128)}) %tuple.55), condition=%wide.while_cond, body=%wide.while_body.sunk | while | flops 2 | bytes 15730289 | solution.py:102
  475.1 11.3 dynamic-slice_dynamic-update-slice_fusion.2
  487.1 11.4 dynamic-slice_dynamic-update-slice_fusion.2
  498.5 29.3 %copy.43 = bf16[30,2,32,4096]{3,1,0,2:T(2,128)(2,1)} copy(bf16[30,2,32,4096]{3,2,1,0:T(8,128)(2,1)} %bitcast.43) | data formatting | bytes 31457280
  527.8 805.0 %while.13 = (s32[]{:T(128)}, f32[32,256]{1,0:T(8,128)S(1)}, s32[32]{0:T(128)S(1)}, bf16[30,2,32,4096]{3,1,0,2:T(2,128)(2,1)}, s32[]{:T(128)}, /*index=5*/f32[256...) while((s32[]{:T(128)}, f32[32,256]{1,0:T(8,128)S(1)}, ...), condition=%wide.region_2.3_spmd.clone, body=%wide.region_0.2_spmd.clone.sunk | while | flops 269464320 | bytes 12114143 | solution.py:89
  530.1 1.4 dynamic-slice_bitcast_fusion.2
  533.8 18.4 %fusion.56 = (bf16[4096,256]{1,0:T(8,128)(2,1)S(1)}, bf16[4096,256]{1,0:T(8,128)(2,1)S(1)}) fusion(f32[256]{0:T(256)S(1)} %get-tuple-element.316, f32[4096]{0:T(1024)S(1)} %get-tuple-element.317, f32[256]{0:T(256)S(1)} %get-tuple-element.314, f32[4096]{0:T(1024)S(1)} %get-tuple-element.315, f32[256]{0:T(256)S(1)} %get-tuple-element.318, f32[]{:T(128)S(6)} %mul.373), kind=kLoop, calls=%fused_computation.10.clone.1 | loop fusion | flops 8388608 | bytes 4230148 | tf_op jit(solution)/shard_map/convert
  555.2 1.4 dynamic-slice_bitcast_fusion.2
  558.9 18.4 %fusion.56 = (bf16[4096,256]{1,0:T(8,128)(2,1)S(1)}, bf16[4096,256]{1,0:T(8,128)(2,1)S(1)}) fusion(f32[256]{0:T(256)S(1)} %get-tuple-element.316, f32[4096]{0:T(1024)S(1)} %get-tuple-element.317, f32[256]{0:T(256)S(1)} %get-tuple-element.314, f32[4096]{0:T(1024)S(1)} %get-tuple-element.315, f32[256]{0:T(256)S(1)} %get-tuple-element.318, f32[]{:T(128)S(6)} %mul.373), kind=kLoop, calls=%fused_computation.10.clone.1 | loop fusion | flops 8388608 | bytes 4230148 | tf_op jit(solution)/shard_map/convert
  580.4 1.4 dynamic-slice_bitcast_fusion.2
  584.1 18.4 %fusion.56 = (bf16[4096,256]{1,0:T(8,128)(2,1)S(1)}, bf16[4096,256]{1,0:T(8,128)(2,1)S(1)}) fusion(f32[256]{0:T(256)S(1)} %get-tuple-element.316, f32[4096]{0:T(1024)S(1)} %get-tuple-element.317, f32[256]{0:T(256)S(1)} %get-tuple-element.314, f32[4096]{0:T(1024)S(1)} %get-tuple-element.315, f32[256]{0:T(256)S(1)} %get-tuple-element.318, f32[]{:T(128)S(6)} %mul.373), kind=kLoop, calls=%fused_computation.10.clone.1 | loop fusion | flops 8388608 | bytes 4230148 | tf_op jit(solution)/shard_map/convert
  605.6 1.4 dynamic-slice_bitcast_fusion.2
  609.2 18.4 %fusion.56 = (bf16[4096,256]{1,0:T(8,128)(2,1)S(1)}, bf16[4096,256]{1,0:T(8,128)(2,1)S(1)}) fusion(f32[256]{0:T(256)S(1)} %get-tuple-element.316, f32[4096]{0:T(1024)S(1)} %get-tuple-element.317, f32[256]{0:T(256)S(1)} %get-tuple-element.314, f32[4096]{0:T(1024)S(1)} %get-tuple-element.315, f32[256]{0:T(256)S(1)} %get-tuple-element.318, f32[]{:T(128)S(6)} %mul.373), kind=kLoop, calls=%fused_computation.10.clone.1 | loop fusion | flops 8388608 | bytes 4230148 | tf_op jit(solution)/shard_map/convert
  630.7 1.4 dynamic-slice_bitcast_fusion.2
  634.4 18.4 %fusion.56 = (bf16[4096,256]{1,0:T(8,128)(2,1)S(1)}, bf16[4096,256]{1,0:T(8,128)(2,1)S(1)}) fusion(f32[256]{0:T(256)S(1)} %get-tuple-element.316, f32[4096]{0:T(1024)S(1)} %get-tuple-element.317, f32[256]{0:T(256)S(1)} %get-tuple-element.314, f32[4096]{0:T(1024)S(1)} %get-tuple-element.315, f32[256]{0:T(256)S(1)} %get-tuple-element.318, f32[]{:T(128)S(6)} %mul.373), kind=kLoop, calls=%fused_computation.10.clone.1 | loop fusion | flops 8388608 | bytes 4230148 | tf_op jit(solution)/shard_map/convert
  655.9 1.4 dynamic-slice_bitcast_fusion.2
  659.6 18.4 %fusion.56 = (bf16[4096,256]{1,0:T(8,128)(2,1)S(1)}, bf16[4096,256]{1,0:T(8,128)(2,1)S(1)}) fusion(f32[256]{0:T(256)S(1)} %get-tuple-element.316, f32[4096]{0:T(1024)S(1)} %get-tuple-element.317, f32[256]{0:T(256)S(1)} %get-tuple-element.314, f32[4096]{0:T(1024)S(1)} %get-tuple-element.315, f32[256]{0:T(256)S(1)} %get-tuple-element.318, f32[]{:T(128)S(6)} %mul.373), kind=kLoop, calls=%fused_computation.10.clone.1 | loop fusion | flops 8388608 | bytes 4230148 | tf_op jit(solution)/shard_map/convert
  681.0 1.4 dynamic-slice_bitcast_fusion.2
  684.7 18.4 %fusion.56 = (bf16[4096,256]{1,0:T(8,128)(2,1)S(1)}, bf16[4096,256]{1,0:T(8,128)(2,1)S(1)}) fusion(f32[256]{0:T(256)S(1)} %get-tuple-element.316, f32[4096]{0:T(1024)S(1)} %get-tuple-element.317, f32[256]{0:T(256)S(1)} %get-tuple-element.314, f32[4096]{0:T(1024)S(1)} %get-tuple-element.315, f32[256]{0:T(256)S(1)} %get-tuple-element.318, f32[]{:T(128)S(6)} %mul.373), kind=kLoop, calls=%fused_computation.10.clone.1 | loop fusion | flops 8388608 | bytes 4230148 | tf_op jit(solution)/shard_map/convert
  706.2 1.4 dynamic-slice_bitcast_fusion.2
  709.9 18.4 %fusion.56 = (bf16[4096,256]{1,0:T(8,128)(2,1)S(1)}, bf16[4096,256]{1,0:T(8,128)(2,1)S(1)}) fusion(f32[256]{0:T(256)S(1)} %get-tuple-element.316, f32[4096]{0:T(1024)S(1)} %get-tuple-element.317, f32[256]{0:T(256)S(1)} %get-tuple-element.314, f32[4096]{0:T(1024)S(1)} %get-tuple-element.315, f32[256]{0:T(256)S(1)} %get-tuple-element.318, f32[]{:T(128)S(6)} %mul.373), kind=kLoop, calls=%fused_computation.10.clone.1 | loop fusion | flops 8388608 | bytes 4230148 | tf_op jit(solution)/shard_map/convert
  731.3 1.4 dynamic-slice_bitcast_fusion.2
  735.0 18.4 %fusion.56 = (bf16[4096,256]{1,0:T(8,128)(2,1)S(1)}, bf16[4096,256]{1,0:T(8,128)(2,1)S(1)}) fusion(f32[256]{0:T(256)S(1)} %get-tuple-element.316, f32[4096]{0:T(1024)S(1)} %get-tuple-element.317, f32[256]{0:T(256)S(1)} %get-tuple-element.314, f32[4096]{0:T(1024)S(1)} %get-tuple-element.315, f32[256]{0:T(256)S(1)} %get-tuple-element.318, f32[]{:T(128)S(6)} %mul.373), kind=kLoop, calls=%fused_computation.10.clone.1 | loop fusion | flops 8388608 | bytes 4230148 | tf_op jit(solution)/shard_map/convert
  756.5 1.4 dynamic-slice_bitcast_fusion.2
  760.2 18.4 %fusion.56 = (bf16[4096,256]{1,0:T(8,128)(2,1)S(1)}, bf16[4096,256]{1,0:T(8,128)(2,1)S(1)}) fusion(f32[256]{0:T(256)S(1)} %get-tuple-element.316, f32[4096]{0:T(1024)S(1)} %get-tuple-element.317, f32[256]{0:T(256)S(1)} %get-tuple-element.314, f32[4096]{0:T(1024)S(1)} %get-tuple-element.315, f32[256]{0:T(256)S(1)} %get-tuple-element.318, f32[]{:T(128)S(6)} %mul.373), kind=kLoop, calls=%fused_computation.10.clone.1 | loop fusion | flops 8388608 | bytes 4230148 | tf_op jit(solution)/shard_map/convert
  785.3 18.4 %fusion.56 = (bf16[4096,256]{1,0:T(8,128)(2,1)S(1)}, bf16[4096,256]{1,0:T(8,128)(2,1)S(1)}) fusion(f32[256]{0:T(256)S(1)} %get-tuple-element.316, f32[4096]{0:T(1024)S(1)} %get-tuple-element.317, f32[256]{0:T(256)S(1)} %get-tuple-element.314, f32[4096]{0:T(1024)S(1)} %get-tuple-element.315, f32[256]{0:T(256)S(1)} %get-tuple-element.318, f32[]{:T(128)S(6)} %mul.373), kind=kLoop, calls=%fused_computation.10.clone.1 | loop fusion | flops 8388608 | bytes 4230148 | tf_op jit(solution)/shard_map/convert
  810.5 18.4 %fusion.56 = (bf16[4096,256]{1,0:T(8,128)(2,1)S(1)}, bf16[4096,256]{1,0:T(8,128)(2,1)S(1)}) fusion(f32[256]{0:T(256)S(1)} %get-tuple-element.316, f32[4096]{0:T(1024)S(1)} %get-tuple-element.317, f32[256]{0:T(256)S(1)} %get-tuple-element.314, f32[4096]{0:T(1024)S(1)} %get-tuple-element.315, f32[256]{0:T(256)S(1)} %get-tuple-element.318, f32[]{:T(128)S(6)} %mul.373), kind=kLoop, calls=%fused_computation.10.clone.1 | loop fusion | flops 8388608 | bytes 4230148 | tf_op jit(solution)/shard_map/convert
  835.7 18.4 %fusion.56 = (bf16[4096,256]{1,0:T(8,128)(2,1)S(1)}, bf16[4096,256]{1,0:T(8,128)(2,1)S(1)}) fusion(f32[256]{0:T(256)S(1)} %get-tuple-element.316, f32[4096]{0:T(1024)S(1)} %get-tuple-element.317, f32[256]{0:T(256)S(1)} %get-tuple-element.314, f32[4096]{0:T(1024)S(1)} %get-tuple-element.315, f32[256]{0:T(256)S(1)} %get-tuple-element.318, f32[]{:T(128)S(6)} %mul.373), kind=kLoop, calls=%fused_computation.10.clone.1 | loop fusion | flops 8388608 | bytes 4230148 | tf_op jit(solution)/shard_map/convert
  860.8 18.4 %fusion.56 = (bf16[4096,256]{1,0:T(8,128)(2,1)S(1)}, bf16[4096,256]{1,0:T(8,128)(2,1)S(1)}) fusion(f32[256]{0:T(256)S(1)} %get-tuple-element.316, f32[4096]{0:T(1024)S(1)} %get-tuple-element.317, f32[256]{0:T(256)S(1)} %get-tuple-element.314, f32[4096]{0:T(1024)S(1)} %get-tuple-element.315, f32[256]{0:T(256)S(1)} %get-tuple-element.318, f32[]{:T(128)S(6)} %mul.373), kind=kLoop, calls=%fused_computation.10.clone.1 | loop fusion | flops 8388608 | bytes 4230148 | tf_op jit(solution)/shard_map/convert
  886.0 18.4 %fusion.56 = (bf16[4096,256]{1,0:T(8,128)(2,1)S(1)}, bf16[4096,256]{1,0:T(8,128)(2,1)S(1)}) fusion(f32[256]{0:T(256)S(1)} %get-tuple-element.316, f32[4096]{0:T(1024)S(1)} %get-tuple-element.317, f32[256]{0:T(256)S(1)} %get-tuple-element.314, f32[4096]{0:T(1024)S(1)} %get-tuple-element.315, f32[256]{0:T(256)S(1)} %get-tuple-element.318, f32[]{:T(128)S(6)} %mul.373), kind=kLoop, calls=%fused_computation.10.clone.1 | loop fusion | flops 8388608 | bytes 4230148 | tf_op jit(solution)/shard_map/convert
  911.1 18.4 %fusion.56 = (bf16[4096,256]{1,0:T(8,128)(2,1)S(1)}, bf16[4096,256]{1,0:T(8,128)(2,1)S(1)}) fusion(f32[256]{0:T(256)S(1)} %get-tuple-element.316, f32[4096]{0:T(1024)S(1)} %get-tuple-element.317, f32[256]{0:T(256)S(1)} %get-tuple-element.314, f32[4096]{0:T(1024)S(1)} %get-tuple-element.315, f32[256]{0:T(256)S(1)} %get-tuple-element.318, f32[]{:T(128)S(6)} %mul.373), kind=kLoop, calls=%fused_computation.10.clone.1 | loop fusion | flops 8388608 | bytes 4230148 | tf_op jit(solution)/shard_map/convert
  936.3 18.4 %fusion.56 = (bf16[4096,256]{1,0:T(8,128)(2,1)S(1)}, bf16[4096,256]{1,0:T(8,128)(2,1)S(1)}) fusion(f32[256]{0:T(256)S(1)} %get-tuple-element.316, f32[4096]{0:T(1024)S(1)} %get-tuple-element.317, f32[256]{0:T(256)S(1)} %get-tuple-element.314, f32[4096]{0:T(1024)S(1)} %get-tuple-element.315, f32[256]{0:T(256)S(1)} %get-tuple-element.318, f32[]{:T(128)S(6)} %mul.373), kind=kLoop, calls=%fused_computation.10.clone.1 | loop fusion | flops 8388608 | bytes 4230148 | tf_op jit(solution)/shard_map/convert
  957.8 1.4 dynamic-slice_bitcast_fusion.2
  961.5 18.4 %fusion.56 = (bf16[4096,256]{1,0:T(8,128)(2,1)S(1)}, bf16[4096,256]{1,0:T(8,128)(2,1)S(1)}) fusion(f32[256]{0:T(256)S(1)} %get-tuple-element.316, f32[4096]{0:T(1024)S(1)} %get-tuple-element.317, f32[256]{0:T(256)S(1)} %get-tuple-element.314, f32[4096]{0:T(1024)S(1)} %get-tuple-element.315, f32[256]{0:T(256)S(1)} %get-tuple-element.318, f32[]{:T(128)S(6)} %mul.373), kind=kLoop, calls=%fused_computation.10.clone.1 | loop fusion | flops 8388608 | bytes 4230148 | tf_op jit(solution)/shard_map/convert
  986.6 18.4 %fusion.56 = (bf16[4096,256]{1,0:T(8,128)(2,1)S(1)}, bf16[4096,256]{1,0:T(8,128)(2,1)S(1)}) fusion(f32[256]{0:T(256)S(1)} %get-tuple-element.316, f32[4096]{0:T(1024)S(1)} %get-tuple-element.317, f32[256]{0:T(256)S(1)} %get-tuple-element.314, f32[4096]{0:T(1024)S(1)} %get-tuple-element.315, f32[256]{0:T(256)S(1)} %get-tuple-element.318, f32[]{:T(128)S(6)} %mul.373), kind=kLoop, calls=%fused_computation.10.clone.1 | loop fusion | flops 8388608 | bytes 4230148 | tf_op jit(solution)/shard_map/convert
  1011.8 18.4 %fusion.56 = (bf16[4096,256]{1,0:T(8,128)(2,1)S(1)}, bf16[4096,256]{1,0:T(8,128)(2,1)S(1)}) fusion(f32[256]{0:T(256)S(1)} %get-tuple-element.316, f32[4096]{0:T(1024)S(1)} %get-tuple-element.317, f32[256]{0:T(256)S(1)} %get-tuple-element.314, f32[4096]{0:T(1024)S(1)} %get-tuple-element.315, f32[256]{0:T(256)S(1)} %get-tuple-element.318, f32[]{:T(128)S(6)} %mul.373), kind=kLoop, calls=%fused_computation.10.clone.1 | loop fusion | flops 8388608 | bytes 4230148 | tf_op jit(solution)/shard_map/convert
  1036.9 18.4 %fusion.56 = (bf16[4096,256]{1,0:T(8,128)(2,1)S(1)}, bf16[4096,256]{1,0:T(8,128)(2,1)S(1)}) fusion(f32[256]{0:T(256)S(1)} %get-tuple-element.316, f32[4096]{0:T(1024)S(1)} %get-tuple-element.317, f32[256]{0:T(256)S(1)} %get-tuple-element.314, f32[4096]{0:T(1024)S(1)} %get-tuple-element.315, f32[256]{0:T(256)S(1)} %get-tuple-element.318, f32[]{:T(128)S(6)} %mul.373), kind=kLoop, calls=%fused_computation.10.clone.1 | loop fusion | flops 8388608 | bytes 4230148 | tf_op jit(solution)/shard_map/convert
  1062.1 18.4 %fusion.56 = (bf16[4096,256]{1,0:T(8,128)(2,1)S(1)}, bf16[4096,256]{1,0:T(8,128)(2,1)S(1)}) fusion(f32[256]{0:T(256)S(1)} %get-tuple-element.316, f32[4096]{0:T(1024)S(1)} %get-tuple-element.317, f32[256]{0:T(256)S(1)} %get-tuple-element.314, f32[4096]{0:T(1024)S(1)} %get-tuple-element.315, f32[256]{0:T(256)S(1)} %get-tuple-element.318, f32[]{:T(128)S(6)} %mul.373), kind=kLoop, calls=%fused_computation.10.clone.1 | loop fusion | flops 8388608 | bytes 4230148 | tf_op jit(solution)/shard_map/convert
  1083.6 1.4 dynamic-slice_bitcast_fusion.2
  1087.2 18.4 %fusion.56 = (bf16[4096,256]{1,0:T(8,128)(2,1)S(1)}, bf16[4096,256]{1,0:T(8,128)(2,1)S(1)}) fusion(f32[256]{0:T(256)S(1)} %get-tuple-element.316, f32[4096]{0:T(1024)S(1)} %get-tuple-element.317, f32[256]{0:T(256)S(1)} %get-tuple-element.314, f32[4096]{0:T(1024)S(1)} %get-tuple-element.315, f32[256]{0:T(256)S(1)} %get-tuple-element.318, f32[]{:T(128)S(6)} %mul.373), kind=kLoop, calls=%fused_computation.10.clone.1 | loop fusion | flops 8388608 | bytes 4230148 | tf_op jit(solution)/shard_map/convert
  1112.4 18.4 %fusion.56 = (bf16[4096,256]{1,0:T(8,128)(2,1)S(1)}, bf16[4096,256]{1,0:T(8,128)(2,1)S(1)}) fusion(f32[256]{0:T(256)S(1)} %get-tuple-element.316, f32[4096]{0:T(1024)S(1)} %get-tuple-element.317, f32[256]{0:T(256)S(1)} %get-tuple-element.314, f32[4096]{0:T(1024)S(1)} %get-tuple-element.315, f32[256]{0:T(256)S(1)} %get-tuple-element.318, f32[]{:T(128)S(6)} %mul.373), kind=kLoop, calls=%fused_computation.10.clone.1 | loop fusion | flops 8388608 | bytes 4230148 | tf_op jit(solution)/shard_map/convert
  1137.6 18.4 %fusion.56 = (bf16[4096,256]{1,0:T(8,128)(2,1)S(1)}, bf16[4096,256]{1,0:T(8,128)(2,1)S(1)}) fusion(f32[256]{0:T(256)S(1)} %get-tuple-element.316, f32[4096]{0:T(1024)S(1)} %get-tuple-element.317, f32[256]{0:T(256)S(1)} %get-tuple-element.314, f32[4096]{0:T(1024)S(1)} %get-tuple-element.315, f32[256]{0:T(256)S(1)} %get-tuple-element.318, f32[]{:T(128)S(6)} %mul.373), kind=kLoop, calls=%fused_computation.10.clone.1 | loop fusion | flops 8388608 | bytes 4230148 | tf_op jit(solution)/shard_map/convert
  1162.7 18.4 %fusion.56 = (bf16[4096,256]{1,0:T(8,128)(2,1)S(1)}, bf16[4096,256]{1,0:T(8,128)(2,1)S(1)}) fusion(f32[256]{0:T(256)S(1)} %get-tuple-element.316, f32[4096]{0:T(1024)S(1)} %get-tuple-element.317, f32[256]{0:T(256)S(1)} %get-tuple-element.314, f32[4096]{0:T(1024)S(1)} %get-tuple-element.315, f32[256]{0:T(256)S(1)} %get-tuple-element.318, f32[]{:T(128)S(6)} %mul.373), kind=kLoop, calls=%fused_computation.10.clone.1 | loop fusion | flops 8388608 | bytes 4230148 | tf_op jit(solution)/shard_map/convert
  1187.9 18.4 %fusion.56 = (bf16[4096,256]{1,0:T(8,128)(2,1)S(1)}, bf16[4096,256]{1,0:T(8,128)(2,1)S(1)}) fusion(f32[256]{0:T(256)S(1)} %get-tuple-element.316, f32[4096]{0:T(1024)S(1)} %get-tuple-element.317, f32[256]{0:T(256)S(1)} %get-tuple-element.314, f32[4096]{0:T(1024)S(1)} %get-tuple-element.315, f32[256]{0:T(256)S(1)} %get-tuple-element.318, f32[]{:T(128)S(6)} %mul.373), kind=kLoop, calls=%fused_computation.10.clone.1 | loop fusion | flops 8388608 | bytes 4230148 | tf_op jit(solution)/shard_map/convert
  1213.0 18.4 %fusion.56 = (bf16[4096,256]{1,0:T(8,128)(2,1)S(1)}, bf16[4096,256]{1,0:T(8,128)(2,1)S(1)}) fusion(f32[256]{0:T(256)S(1)} %get-tuple-element.316, f32[4096]{0:T(1024)S(1)} %get-tuple-element.317, f32[256]{0:T(256)S(1)} %get-tuple-element.314, f32[4096]{0:T(1024)S(1)} %get-tuple-element.315, f32[256]{0:T(256)S(1)} %get-tuple-element.318, f32[]{:T(128)S(6)} %mul.373), kind=kLoop, calls=%fused_computation.10.clone.1 | loop fusion | flops 8388608 | bytes 4230148 | tf_op jit(solution)/shard_map/convert
  1238.2 18.4 %fusion.56 = (bf16[4096,256]{1,0:T(8,128)(2,1)S(1)}, bf16[4096,256]{1,0:T(8,128)(2,1)S(1)}) fusion(f32[256]{0:T(256)S(1)} %get-tuple-element.316, f32[4096]{0:T(1024)S(1)} %get-tuple-element.317, f32[256]{0:T(256)S(1)} %get-tuple-element.314, f32[4096]{0:T(1024)S(1)} %get-tuple-element.315, f32[256]{0:T(256)S(1)} %get-tuple-element.318, f32[]{:T(128)S(6)} %mul.373), kind=kLoop, calls=%fused_computation.10.clone.1 | loop fusion | flops 8388608 | bytes 4230148 | tf_op jit(solution)/shard_map/convert
  1263.3 18.4 %fusion.56 = (bf16[4096,256]{1,0:T(8,128)(2,1)S(1)}, bf16[4096,256]{1,0:T(8,128)(2,1)S(1)}) fusion(f32[256]{0:T(256)S(1)} %get-tuple-element.316, f32[4096]{0:T(1024)S(1)} %get-tuple-element.317, f32[256]{0:T(256)S(1)} %get-tuple-element.314, f32[4096]{0:T(1024)S(1)} %get-tuple-element.315, f32[256]{0:T(256)S(1)} %get-tuple-element.318, f32[]{:T(128)S(6)} %mul.373), kind=kLoop, calls=%fused_computation.10.clone.1 | loop fusion | flops 8388608 | bytes 4230148 | tf_op jit(solution)/shard_map/convert
  1288.5 18.4 %fusion.56 = (bf16[4096,256]{1,0:T(8,128)(2,1)S(1)}, bf16[4096,256]{1,0:T(8,128)(2,1)S(1)}) fusion(f32[256]{0:T(256)S(1)} %get-tuple-element.316, f32[4096]{0:T(1024)S(1)} %get-tuple-element.317, f32[256]{0:T(256)S(1)} %get-tuple-element.314, f32[4096]{0:T(1024)S(1)} %get-tuple-element.315, f32[256]{0:T(256)S(1)} %get-tuple-element.318, f32[]{:T(128)S(6)} %mul.373), kind=kLoop, calls=%fused_computation.10.clone.1 | loop fusion | flops 8388608 | bytes 4230148 | tf_op jit(solution)/shard_map/convert
  1313.7 18.4 %fusion.56 = (bf16[4096,256]{1,0:T(8,128)(2,1)S(1)}, bf16[4096,256]{1,0:T(8,128)(2,1)S(1)}) fusion(f32[256]{0:T(256)S(1)} %get-tuple-element.316, f32[4096]{0:T(1024)S(1)} %get-tuple-element.317, f32[256]{0:T(256)S(1)} %get-tuple-element.314, f32[4096]{0:T(1024)S(1)} %get-tuple-element.315, f32[256]{0:T(256)S(1)} %get-tuple-element.318, f32[]{:T(128)S(6)} %mul.373), kind=kLoop, calls=%fused_computation.10.clone.1 | loop fusion | flops 8388608 | bytes 4230148 | tf_op jit(solution)/shard_map/convert
  1333.5 71.3 %reduce-scatter.2.cloned.1.call-done = f32[16,256]{1,0:T(8,128)} async-done(((f32[32,256]{1,0:T(8,128)}), f32[16,256]{1,0:T(8,128)}) %reduce-scatter.2.cloned.1.call-update) | async-done | bytes 16400 | tf_op jit(solution)/shard_map/reduce_scatter | solution.py:112
  (244 shorter events, 130.7 us)
Async XLA Ops:
  7.6 36.5 %collective-permute-start = (bf16[2,1,8192]{2,0,1:T(2,128)(2,1)S(1)}, bf16[2,1,8192]{2,0,1:T(2,128)(2,1)S(1)}, u32[]{:S(2)}, u32[]{:S(2)}) collective-permute-start(bf16[2,1,8192]{2,0,1:T(2,128)(2,1)S(1)} %copy.48), channel_id=1, source_target_pairs={{0,30},{2,0},{4,2},{6,4},{8,6},{10,8},{12,10},{14,12},{16,14},{18,... | collective-permute-start | bytes 98312 | tf_op jit(solution)/shard_map/ppermute | solution.py:17
  44.1 3.4 copy-start.1
  61.6 3.3 copy-start
  130.1 5.5 copy-start.4
  130.1 5.7 copy-start.2
  130.1 5.7 copy-start.3
  130.1 283.7 %all-to-all-start = ((bf16[2,15,1024,256]{3,0,1,2:T(2,128)(2,1)}), bf16[2,15,1024,256]{3,0,1,2:T(2,128)(2,1)}, u32[]{:S(2)}, u32[]{:S(2)}) async-start(bf16[2,15,1024,256]{3,0,1,2:T(2,128)(2,1)} %copy.40), calls=%async_computation | async-start | bytes 31457280 | tf_op jit(solution)/shard_map/all_to_all | solution.py:100
  135.4 1269.4 %reduce-scatter.2.cloned.1.call-start = ((), (), s32[]{:S(2)}) async-start(), calls=%async_computation.2 | async-start | bytes 49152 | tf_op jit(solution)/shard_map/reduce_scatter | solution.py:112
Sparse Core Ops, SparseCore 0:
  1333.6 71.0 reduce-scatter.1
where the time goes:
time: 1420 us; the launch traced here: 1410 us
  other arithmetic  644 us (45%)
  waiting for transfers between devices  349 us (25%)
  local copies, waits for them, and re-layouts  261 us (18%)
  loops' own time  73.7 us (5%)
  matrix products  59.5 us (4%)
    another operation x32, other arithmetic  588 us
    all_to_all x1, waiting for transfers between devices, local(): lax.all_to_all(spectra, 'sector', split_axis=2, concat_axis=3, tiled=True)  278 us
    another operation x1, loops' own time, band_power(): return lax.map(one_bin, jnp.arange(count, dtype=jnp.int32))  73.7 us
    reduce_scatter x1, waiting for transfers between devices, local(): lax.psum_scatter(partial_power, 'blk', scatter_dimension=0, tiled=True)  71.3 us
    squeeze x32, local copies, waits for them, and re-layouts, one_bin(): picked = lax.dynamic_index_in_dim(flat, bin_place, 2, keepdims=False)  46 us
    unnamed x15, local copies, waits for them, and re-layouts  44.8 us
    all_to_all x2, local copies, waits for them, and re-layouts, local(): lax.all_to_all(spectra, 'sector', split_axis=2, concat_axis=3, tiled=True)  39.3 us
    slice x32, local copies, waits for them, and re-layouts, one_bin(): stacked = jnp.concatenate([picked[:, 0], picked[:, 1]], 0)  35.7 us
  transfers between devices with their start and end apart: 3, of which 2 were waited for; matrix products, arithmetic and copies ran while one was open for 2% of the time, Pallas kernels for 0%

commit v1 on v0

v1 whole, which is shorter than its diff:
```python
import functools
import math

import jax
import jax.numpy as jnp
from jax import lax
from jax.experimental import pallas as pl
from jax.experimental.pallas import tpu as pltpu
from jax.sharding import PartitionSpec as P

NFFT = 1024
HALF = NFFT // 2
PARTS = 4
ROWS = 16

wavenumber = 2.0
height = 0.5


def fourier_table():
    fine_count = 32
    coarse_count = HALF // fine_count
    sample = lax.iota(jnp.int32, NFFT)
    unit = 2.0 * math.pi / NFFT

    def turns(frequency):
        angle = (frequency[:, None] * sample[None, :] % NFFT).astype(jnp.float32) * unit
        return lax.optimization_barrier((jnp.cos(angle), jnp.sin(angle)))

    coarse_cos, coarse_sin = turns(lax.iota(jnp.int32, coarse_count) * fine_count)
    fine_cos, fine_sin = turns(lax.iota(jnp.int32, fine_count))
    window = 0.5 - 0.5 * jnp.cos(sample.astype(jnp.float32) * unit)
    window = lax.optimization_barrier(window)
    coarse_cos, coarse_sin = coarse_cos[:, None, None, :], coarse_sin[:, None, None, :]
    fine_cos, fine_sin = fine_cos[None, :, None, :], fine_sin[None, :, None, :]
    part = lax.broadcasted_iota(jnp.int32, (1, 1, 2, 1), 2)
    real = coarse_cos * fine_cos - coarse_sin * fine_sin
    imag = -(coarse_sin * fine_cos + coarse_cos * fine_sin)
    value = jnp.where(part == 0, real, imag)
    table = (value * window / math.sqrt(3.0 * NFFT / 8.0)).astype(jnp.bfloat16)
    return table.reshape(2 * HALF, NFFT)


def distances(index, radius, azimuth, total_mics):
    turn = index.astype(jnp.float32) * (2.0 * math.pi / total_mics)
    cycle_cos = jnp.cos(turn)[..., None]
    cycle_sin = jnp.sin(turn)[..., None]
    across = (radius * jnp.cos(azimuth))[None, None, :]
    along = (radius * jnp.sin(azimuth))[None, None, :]
    squared = (
        1.0
        + height * height
        + (radius * radius)[None, None, :]
        - 2.0 * (cycle_cos * across + cycle_sin * along)
    )
    return jnp.sqrt(squared)


def spectra_kernel(segments, virtual_ref, table_ref, out_ref, spread):
    columns = table_ref.shape[0]
    halves, _, lanes = spread.shape
    mics = halves * lanes

    @pl.loop(0, segments)
    def _(segment):
        start = pl.multiple_of(segment * HALF, HALF)
        piece = virtual_ref[0, :, pl.ds(start, NFFT)]
        product = lax.dot_general(
            table_ref[...], piece, (((1,), (1,)), ((), ())), preferred_element_type=jnp.float32
        )
        for half in range(halves):
            spread[half, pl.ds(segment, columns, stride=ROWS), :] = product[
                :, half * lanes : (half + 1) * lanes
            ]

    for half in range(halves):
        for pad in range(segments, ROWS):
            spread[half, pl.ds(pad, columns, stride=ROWS), :] = jnp.zeros(
                (columns, lanes), jnp.float32
            )
        out_ref[0, :, half * lanes : (half + 1) * lanes] = spread[half].astype(jnp.bfloat16)


def spectra_of(virtual, table):
    blocks, mics, length = virtual.shape
    segments = length // HALF - 1
    tile = HALF
    lanes = min(mics, 128)
    return pl.pallas_call(
        functools.partial(spectra_kernel, segments),
        grid=(blocks, 2 * HALF // tile),
        in_specs=[
            pl.BlockSpec((1, mics, length), lambda b, c: (b, 0, 0)),
            pl.BlockSpec((tile, NFFT), lambda b, c: (c, 0)),
        ],
        out_specs=pl.BlockSpec((1, tile * ROWS, mics), lambda b, c: (b, c, 0)),
        out_shape=jax.ShapeDtypeStruct((blocks, 2 * HALF * ROWS, mics), jnp.bfloat16),
        scratch_shapes=[pltpu.VMEM((mics // lanes, tile * ROWS, lanes), jnp.float32)],
        compiler_params=pltpu.CompilerParams(vmem_limit_bytes=50 << 20),
        name="welch",
    )(virtual, table)


def beam_kernel(spectra_ref, one_ref, step_ref, first_ref, out_ref, now, steer):
    _, mics, points = one_ref.shape[1:]
    bins = spectra_ref.shape[3]

    @pl.when(pl.program_id(1) == 0)
    def _():
        now[...] = first_ref[0]

    @pl.loop(0, mics // ROWS)
    def _(tile):
        rows = pl.ds(pl.multiple_of(tile * ROWS, ROWS), ROWS)
        cos0, sin0 = now[0, rows], now[1, rows]
        cos1, sin1 = one_ref[0, 0, rows], one_ref[0, 1, rows]
        next_cos = cos0 * cos1 - sin0 * sin1
        next_sin = sin0 * cos1 + cos0 * sin1
        double = cos1 + cos1
        step_cos, step_sin = step_ref[0, 0, rows], step_ref[0, 1, rows]
        now[0, rows] = cos0 * step_cos - sin0 * step_sin
        now[1, rows] = sin0 * step_cos + cos0 * step_sin
        for place in range(bins):
            steer[place, 0, rows] = cos0.astype(jnp.bfloat16)
            steer[place, 1, rows] = sin0.astype(jnp.bfloat16)
            cos0, next_cos = next_cos, double * next_cos - cos0
            sin0, next_sin = next_sin, double * next_sin - sin0

    for place in range(bins):
        rows = spectra_ref[0, 0, 0, place]
        turned = jnp.concatenate([rows[ROWS:], -rows[:ROWS]], 0)
        product = jnp.dot(rows, steer[place, 0], preferred_element_type=jnp.float32)
        product += jnp.dot(turned, steer[place, 1], preferred_element_type=jnp.float32)
        out_ref[0, place] = product.astype(jnp.bfloat16)


def beams(spectra, one, step, first, part):
    blocks, groups, _, bins, rows, mics = spectra.shape
    points = one.shape[-1]
    wave = pl.BlockSpec((1, 2, mics, points), lambda b, o: (b, 0, 0, 0))
    return pl.pallas_call(
        beam_kernel,
        grid=(blocks, groups),
        in_specs=[
            pl.BlockSpec((1, 1, 1, bins, rows, mics), lambda b, o: (b, o, part, 0, 0, 0)),
            wave,
            wave,
            wave,
        ],
        out_specs=pl.BlockSpec((1, bins, rows, points), lambda b, o: (o, 0, b, 0)),
        out_shape=jax.ShapeDtypeStruct((groups, bins, blocks * rows, points), jnp.bfloat16),
        scratch_shapes=[
            pltpu.VMEM((2, mics, points), jnp.float32),
            pltpu.VMEM((bins, 2, mics, points), jnp.bfloat16),
        ],
        compiler_params=pltpu.CompilerParams(vmem_limit_bytes=40 << 20),
        cost_estimate=pl.CostEstimate(
            flops=4 * blocks * groups * bins * rows * mics * points * 4,
            bytes_accessed=blocks * groups * bins * rows * (mics + points) * 2,
            transcendentals=0,
        ),
        name="beams",
    )(spectra, one, step, first)


def add(a, b):
    return (a.astype(jnp.float32) + b.astype(jnp.float32)).astype(jnp.bfloat16)


def fold_pair(x, bit):
    sectors = lax.axis_size("sector")
    mine = lax.axis_index("sector") // bit % 2
    halves = x.reshape((x.shape[0] // 2, 2) + x.shape[1:])
    sent = lax.dynamic_index_in_dim(halves, 1 - mine, 1, keepdims=False)
    kept = lax.dynamic_index_in_dim(halves, mine, 1, keepdims=False)
    got = lax.ppermute(sent, "sector", [(i, i ^ bit) for i in range(sectors)])
    return add(kept, got)


def fold_line(x, stride):
    length = x.shape[0]
    place = lax.axis_index("sector") // stride

    def entry(i):
        return lax.dynamic_index_in_dim(x, jnp.clip(i, 0, length - 1), 0, keepdims=False)

    right = left = None
    for step in range(1, length):
        send_right = entry(length - step + place)
        send_left = entry(place + step - length)
        if right is not None:
            send_right, send_left = add(send_right, right), add(send_left, left)
        movers = [i for i in range(length - 1) if i < step]
        pairs = [(i * stride + j, (i + 1) * stride + j) for i in movers for j in range(stride)]
        last = stride * length - 1
        right = lax.ppermute(send_right, "sector", pairs)
        left = lax.ppermute(send_left, "sector", [(last - a, last - b) for a, b in pairs])
    total = entry(place).astype(jnp.float32)
    for got in (right, left):
        if got is not None:
            total = total + got.astype(jnp.float32)
    return total


def fold(x):
    sectors = lax.axis_size("sector")
    stride = 1
    while stride < 4 and sectors // stride % 2 == 0:
        x = fold_pair(x, stride)
        stride *= 2
    return fold_line(x, stride)


def local(signal, offsets, fraction, radius, azimuth):
    blocks, mics, length = signal.shape
    sectors = lax.axis_size("sector")
    sector = lax.axis_index("sector")
    total_mics = mics * sectors
    segments = length // HALF - 1
    edge = lax.ppermute(
        signal[:, :1, :], "sector", [(i, (i - 1) % sectors) for i in range(sectors)]
    )
    upper = jnp.concatenate([signal[:, 1:], edge], 1).astype(jnp.float32)
    weight = fraction[:, None, :]
    virtual = ((1.0 - weight) * signal.astype(jnp.float32) + weight * upper).astype(jnp.bfloat16)
    spectra = spectra_of(virtual, fourier_table())

    band = HALF // sectors
    bins = band // PARTS
    spectra = spectra.reshape(blocks, sectors, PARTS, bins, 2 * ROWS, mics)
    index = (sector * mics + lax.iota(jnp.int32, mics)[None, :] - offsets[:, None]) % total_mics
    distance = lax.optimization_barrier(distances(index, radius, azimuth, total_mics))

    def wave(frequency):
        phase = wavenumber * frequency * distance
        return jnp.stack([jnp.cos(phase), jnp.sin(phase)], 1)

    one, step = wave(1.0), wave(float(band))
    powers = []
    for part in range(PARTS):
        partial = beams(spectra, one, step, wave(float(part * bins)), part)
        total = fold(partial)
        powers.append(jnp.sum(total * total, 1))
    scale = 1.0 / (total_mics * blocks * segments * lax.axis_size("blk"))
    power = jnp.concatenate(powers, 0) * scale
    return lax.psum_scatter(power, "blk", scatter_dimension=0, tiled=True)


def solution(mesh):
    return jax.shard_map(
        local,
        mesh=mesh,
        in_specs=(P("blk", "sector", None), P("blk"), P("blk", None), P(), P()),
        out_specs=P(("sector", "blk"), None),
        check_vma=False,
    )
```

time: 1420 us -> 452 us (0.32)
  other arithmetic: 644 us -> 42.8 us
  waiting for transfers between devices: 349 us -> 101 us
  local copies, waits for them, and re-layouts: 261 us -> 48.6 us
  Pallas kernels: 0 us -> 173 us
  loops' own time: 73.7 us -> 0 us
  matrix products: 59.5 us -> 0 us
  starting transfers between devices: 10.9 us -> 70.2 us
    another operation x32 -> x5, other arithmetic: 588 us -> 15.3 us  [wave(): return jnp.stack([jnp.cos(phase), jnp.sin(phase)], 1)]
    all_to_all x1 -> x0, waiting for transfers between devices: 278 us -> none  [local(): lax.all_to_all(spectra, 'sector', split_axis=2, concat_axis=3, tiled=True)]
    pallas_call x0 -> x5, Pallas kernels: none -> 173 us  [the longest x4 128 us: beams(): pl.pallas_call(beam_kernel, grid=(blocks, groups), in_specs=[pl.BlockSpec...]
    ppermute x1 -> x33, waiting for transfers between devices: 0.01 us -> 91.4 us  [the longest x8 76.4 us: fold_pair(): got = lax.ppermute(sent, 'sector', [(i, i ^ bit) for i in range(sectors)])]
    another operation x2 -> x0, loops' own time: 73.7 us -> none  [the longest x1 73.7 us: band_power(): return lax.map(one_bin, jnp.arange(count, dtype=jnp.int32))]
    ppermute x1 -> x33, starting transfers between devices: 5.47 us -> 70.2 us  [the longest x12 48.9 us: fold_line(): right = lax.ppermute(send_right, 'sector', pairs)]
    reduce_scatter x1, waiting for transfers between devices: 71.3 us -> 9.52 us  [local(): return lax.psum_scatter(power, 'blk', scatter_dimension=0, tiled=True)]
    dot_general x34 -> x0, matrix products: 59.5 us -> none  [the longest x32 23.6 us: one_bin(): product = jnp.dot(stacked, steer, preferred_element_type=jnp.float32)]
  transfers between devices with their start and end apart: 3 -> 34, of which waited for: 2 -> 11; matrix products, arithmetic and copies ran while one was open for 2% -> 16% of each run, Pallas kernels for 0% -> 21%
where the time goes in v1:
time: 452 us; the launch traced here: 450 us
  Pallas kernels  173 us (38%)
  waiting for transfers between devices  101 us (22%)
  starting transfers between devices  70.2 us (16%)
  local copies, waits for them, and re-layouts  48.6 us (11%)
  other arithmetic  42.8 us (9%)
  between operations  14.2 us (3%)
    pallas_call x4, Pallas kernels, beams(): pl.pallas_call(beam_kernel, grid=(blocks, groups), in_specs=[pl.BlockSpec...  128 us
    ppermute x8, waiting for transfers between devices, fold_pair(): got = lax.ppermute(sent, 'sector', [(i, i ^ bit) for i in range(sectors)])  76.4 us
    ppermute x12, starting transfers between devices, fold_line(): right = lax.ppermute(send_right, 'sector', pairs)  48.9 us
    pallas_call x1, Pallas kernels, spectra_of(): pl.pallas_call(functools.partial(spectra_kernel, segments), grid=(blocks,...  45.7 us
    broadcast_in_dim x6, local copies, waits for them, and re-layouts, fourier_table(): value = jnp.where(part == 0, real, imag)  19.4 us
    another operation x5, other arithmetic, wave(): return jnp.stack([jnp.cos(phase), jnp.sin(phase)], 1)  15.3 us
    convert_element_type x20, other arithmetic, add(): return (a.astype(jnp.float32) + b.astype(jnp.float32)).astype(jnp.bfloat16)  12 us
    convert_element_type x1, other arithmetic, local(): ((1.0 - weight) * signal.astype(jnp.float32) + weight * upper).astype(jnp...  10.9 us
  transfers between devices with their start and end apart: 34, of which 11 were waited for; matrix products, arithmetic and copies ran while one was open for 16% of the time, Pallas kernels for 21%

profile of v1, /device:TPU:0, one launch (start us, length us, event | category | flops | bytes accessed | tf_op | source)
XLA Modules:
  0.0 450.2 jit_solution(3682294154702655690)
XLA Ops:
  6.5 1.0 slice.7
  7.5 5.5 %collective-permute-start = (bf16[2,1,8192]{2,1,0:T(2,128)(2,1)S(1)}, bf16[2,1,8192]{2,1,0:T(2,128)(2,1)S(1)}, u32[]{:S(2)}, u32[]{:S(2)}) collective-permute-start(bf16[2,1,8192]{2,1,0:T(2,128)(2,1)S(1)} %slice.7), channel_id=1, source_target_pairs={{0,30},{2,0},{4,2},{6,4},{8,6},{10,8},{12,10},{14,12},{16,14},{18,... | collective-permute-start | bytes 98312 | tf_op jit(solution)/shard_map/ppermute | solution.py:220
  13.6 0.9 broadcast_subtract_fusion
  15.3 3.5 broadcast_in_dim.52
  18.8 6.0 %broadcast_in_dim.53 = f32[1024,1024]{1,0:T(8,128)} reshape(f32[16,32,2,1024]{3,2,1,0:T(2,128)} %broadcast_in_dim.52) | data formatting | bytes 8388608 | tf_op jit(solution)/shard_map/jit(_where)/broadcast_in_dim | solution.py:39
  24.8 3.5 broadcast_in_dim.54
  28.4 6.2 %broadcast_in_dim.55 = f32[1024,1024]{1,0:T(8,128)} reshape(f32[16,32,2,1024]{3,2,1,0:T(2,128)} %broadcast_in_dim.54) | data formatting | bytes 8388608 | tf_op jit(solution)/shard_map/jit(_where)/broadcast_in_dim | solution.py:39
  35.3 11.1 %cosine_bitcast_fusion.3 = (f32[2,1,256,256]{3,2,0,1:T(8,128)S(1)}, f32[2,1,256,256]{3,2,0,1:T(8,128)S(1)}, f32[2,1,256,256]{3,2,0,1:T(8,128)S(1)}, f32[2,1,256,...) fusion(f32[2,256,256]{2,1,0:T(8,128)S(1)} %subtract_sqrt_fusion), kind=kLoop, calls=%fused_computation.89 | loop fusion | flops 786432 | bytes 6815744 | tf_op jit(solution)/shard_map/stack | solution.py:236
  47.1 1.6 pad_maximum_fusion
  48.7 1.5 pad_maximum_fusion.2
  50.1 1.0 pad_maximum_fusion.4
  51.2 8.9 %slice.6 = bf16[2,255,8192]{2,1,0:T(8,128)(2,1)} slice(bf16[2,256,8192]{2,1,0:T(8,128)(2,1)} %param.5), slice={[0:2], [1:256], [0:8192]} | slice | bytes 16711680 | tf_op jit(solution)/shard_map/slice | solution.py:223
  60.1 2.4 copy.18.one_ref
  62.4 1.1 copy.19.step_ref
  63.5 2.4 copy.26.first_ref
  66.0 1.0 copy.23.first_ref
  67.0 1.1 copy.20.first_ref
  68.1 10.9 %add_convert_fusion.virtual_ref = bf16[2,256,8192]{2,1,0:T(8,128)(2,1)} fusion(bf16[2,256,8192]{2,1,0:T(8,128)(2,1)} %param.5, bf16[2,1,8192]{2,1,0:T(2,128)(2,1)S(1)} %collective-permute-done, bf16[2,255,8192]{2,1,0:T(8,128)(2,1)} %slice.6, f32[2,8192]{1,0:T(2,128)S(1)} %copy-done.17, f32[2,8192]{1,0:T(2,128)S(1)} %broadcast_subtract_fusion), kind=kLoop, calls=%fused_computation | loop fusion | flops 37748736 | bytes 25296896 | tf_op jit(solution)/shard_map/convert_element_type | solution.py:225
  79.1 45.7 %welch.1 = bf16[2,16384,256]{2,1,0:T(8,128)(2,1)} custom-call(bf16[2,256,8192]{2,1,0:T(8,128)(2,1)} %add_convert_fusion.virtual_ref, bf16[1024,1024]{1,0:T(8,128)(2,1)S(1)} %multiply_convert_fusion.table_ref), custom_call_target="tpu_custom_call" | custom-call | tf_op jit(solution)/shard_map/welch/pallas_call | solution.py:89
  124.8 31.9 %beams.7 = bf16[16,8,64,256]{3,2,1,0:T(8,128)(2,1)S(1)} custom-call(bf16[2,16,4,8,32,256]{5,4,3,2,1,0:T(8,128)(2,1)} %bitcast.159, f32[2,2,256,256]{3,2,1,0:T(8,128)S(1)} %copy-done.7, f32[2,2,256,256]{3,2,1,0:T(8,128)S(1)} %copy-done.8, f32[2,2,256,256]{3,2,1,0:T(8,128)S(1)} %pad_maximum_fusion.5.first_ref), custom_call_target="tpu_custom_call" | custom-call | flops 8589934592 | bytes 8388608 | tf_op jit(solution)/shard_map/beams/pallas_call | solution.py:141
  156.7 1.6 dynamic-slice_bitcast_fusion
  158.3 1.0 copy-done.6
  159.3 31.9 %beams.6 = bf16[16,8,64,256]{3,2,1,0:T(8,128)(2,1)S(1)} custom-call(bf16[2,16,4,8,32,256]{5,4,3,2,1,0:T(8,128)(2,1)} %bitcast.160, f32[2,2,256,256]{3,2,1,0:T(8,128)S(1)} %copy-done.7, f32[2,2,256,256]{3,2,1,0:T(8,128)S(1)} %copy-done.8, f32[2,2,256,256]{3,2,1,0:T(8,128)S(1)} %copy-done.11), custom_call_target="tpu_custom_call" | custom-call | flops 8589934592 | bytes 8388608 | tf_op jit(solution)/shard_map/beams/pallas_call | solution.py:141
  191.2 1.6 dynamic-slice_bitcast_fusion.1
  192.9 1.0 copy-done.4
  194.4 31.9 %beams.5 = bf16[16,8,64,256]{3,2,1,0:T(8,128)(2,1)S(1)} custom-call(bf16[2,16,4,8,32,256]{5,4,3,2,1,0:T(8,128)(2,1)} %bitcast.161, f32[2,2,256,256]{3,2,1,0:T(8,128)S(1)} %copy-done.7, f32[2,2,256,256]{3,2,1,0:T(8,128)S(1)} %copy-done.8, f32[2,2,256,256]{3,2,1,0:T(8,128)S(1)} %copy-done.10), custom_call_target="tpu_custom_call" | custom-call | flops 8589934592 | bytes 8388608 | tf_op jit(solution)/shard_map/beams/pallas_call | solution.py:141
  226.2 1.6 dynamic-slice_bitcast_fusion.2
  227.9 1.1 copy-done.2
  228.9 32.1 %beams.4 = bf16[16,8,64,256]{3,2,1,0:T(8,128)(2,1)S(1)} custom-call(bf16[2,16,4,8,32,256]{5,4,3,2,1,0:T(8,128)(2,1)} %bitcast.162, f32[2,2,256,256]{3,2,1,0:T(8,128)S(1)} %copy-done.7, f32[2,2,256,256]{3,2,1,0:T(8,128)S(1)} %copy-done.8, f32[2,2,256,256]{3,2,1,0:T(8,128)S(1)} %copy-done.9), custom_call_target="tpu_custom_call" | custom-call | flops 8589934592 | bytes 8388608 | tf_op jit(solution)/shard_map/beams/pallas_call | solution.py:141
  261.1 1.8 dynamic-slice_bitcast_fusion.3
  262.9 0.9 copy-done
  264.2 3.2 fusion
  267.7 2.6 fusion.1
  270.4 2.0 collective-permute-start.18
  272.4 2.6 fusion.2
  275.2 0.9 fusion.3
  276.3 2.0 collective-permute-start.2
  278.3 15.3 %collective-permute-done.26 = bf16[4,8,64,256]{3,2,1,0:T(8,128)(2,1)S(1)} collective-permute-done((bf16[4,8,64,256]{3,2,1,0:T(8,128)(2,1)S(1)}, bf16[4,8,64,256]{3,2,1,0:T(8,128)(2,1)S(1)}, u32[]{:S(2)}, u32[]{:S(2)}) %collective-permute-start.26) | collective-permute-done | bytes 1048608 | tf_op jit(solution)/shard_map/ppermute | solution.py:176
  294.1 1.3 collective-permute-start.27
  295.4 0.7 collective-permute-start.30
  296.1 20.0 %collective-permute-done.18 = bf16[4,8,64,256]{3,2,1,0:T(8,128)(2,1)S(1)} collective-permute-done((bf16[4,8,64,256]{3,2,1,0:T(8,128)(2,1)S(1)}, bf16[4,8,64,256]{3,2,1,0:T(8,128)(2,1)S(1)}, u32[]{:S(2)}, u32[]{:S(2)}) %collective-permute-start.18) | collective-permute-done | bytes 1048608 | tf_op jit(solution)/shard_map/ppermute | solution.py:176
  316.6 1.3 collective-permute-start.19
  317.9 20.7 %collective-permute-done.10 = bf16[4,8,64,256]{3,2,1,0:T(8,128)(2,1)S(1)} collective-permute-done((bf16[4,8,64,256]{3,2,1,0:T(8,128)(2,1)S(1)}, bf16[4,8,64,256]{3,2,1,0:T(8,128)(2,1)S(1)}, u32[]{:S(2)}, u32[]{:S(2)}) %collective-permute-start.10) | collective-permute-done | bytes 1048608 | tf_op jit(solution)/shard_map/ppermute | solution.py:176
  339.7 20.4 %collective-permute-done.2 = bf16[4,8,64,256]{3,2,1,0:T(8,128)(2,1)S(1)} collective-permute-done((bf16[4,8,64,256]{3,2,1,0:T(8,128)(2,1)S(1)}, bf16[4,8,64,256]{3,2,1,0:T(8,128)(2,1)S(1)}, u32[]{:S(2)}, u32[]{:S(2)}) %collective-permute-start.2) | collective-permute-done | bytes 1048608 | tf_op jit(solution)/shard_map/ppermute | solution.py:176
  360.1 1.3 collective-permute-start.11
  362.6 1.3 collective-permute-start.3
  364.0 4.1 collective-permute-done.11
  368.1 4.4 collective-permute-start.28
  372.6 1.1 collective-permute-done.3
  373.8 4.4 collective-permute-start.20
  379.4 4.4 collective-permute-start.12
  383.9 1.9 collective-permute-start.4
  386.7 4.1 collective-permute-start.29
  391.7 5.2 %collective-permute-start.21 = (bf16[8,64,256]{2,1,0:T(8,128)(2,1)S(1)}, bf16[8,64,256]{2,1,0:T(8,128)(2,1)S(1)}, u32[]{:S(2)}, u32[]{:S(2)}) collective-permute-start(bf16[8,64,256]{2,1,0:T(8,128)(2,1)S(1)} %get-tuple-element.21), channel_id=1, source_target_pairs={{0,8},{2,10},{4,12},{6,14},{8,16},{10,18},{12,20},{14,22},{16,24},... | collective-permute-start | bytes 786440 | tf_op jit(solution)/shard_map/ppermute | solution.py:196
  397.8 5.2 %collective-permute-start.13 = (bf16[8,64,256]{2,1,0:T(8,128)(2,1)S(1)}, bf16[8,64,256]{2,1,0:T(8,128)(2,1)S(1)}, u32[]{:S(2)}, u32[]{:S(2)}) collective-permute-start(bf16[8,64,256]{2,1,0:T(8,128)(2,1)S(1)} %get-tuple-element.17), channel_id=1, source_target_pairs={{0,8},{2,10},{4,12},{6,14},{8,16},{10,18},{12,20},{14,22},{16,24},... | collective-permute-start | bytes 786440 | tf_op jit(solution)/shard_map/ppermute | solution.py:196
  403.8 1.3 collective-permute-start.32
  405.2 1.3 collective-permute-start.24
  406.6 14.1 %collective-permute-start.5 = (bf16[8,64,256]{2,1,0:T(8,128)(2,1)S(1)}, bf16[8,64,256]{2,1,0:T(8,128)(2,1)S(1)}, u32[]{:S(2)}, u32[]{:S(2)}) collective-permute-start(bf16[8,64,256]{2,1,0:T(8,128)(2,1)S(1)} %get-tuple-element.13), channel_id=1, source_target_pairs={{0,8},{2,10},{4,12},{6,14},{8,16},{10,18},{12,20},{14,22},{16,24},... | collective-permute-start | bytes 786440 | tf_op jit(solution)/shard_map/ppermute | solution.py:196
  420.7 1.3 collective-permute-start.16
  422.2 1.3 collective-permute-start.8
  423.5 2.4 collective-permute-done.24
  426.1 4.2 collective-permute-done.16
  430.4 2.6 collective-permute-done.8
  433.8 9.5 %reduce-scatter.2.cloned.1.call-done = f32[16,256]{1,0:T(8,128)} async-done(((f32[32,256]{1,0:T(8,128)}), f32[16,256]{1,0:T(8,128)}) %reduce-scatter.2.cloned.1.call-update) | async-done | bytes 16400 | tf_op jit(solution)/shard_map/reduce_scatter | solution.py:246
  (120 shorter events, 13.9 us)
Async XLA Ops:
  6.5 436.8 %reduce-scatter.2.cloned.1.call-start = ((), (), s32[]{:S(2)}) async-start(), calls=%async_computation.1 | async-start | bytes 49152 | tf_op jit(solution)/shard_map/reduce_scatter | solution.py:246
  7.5 60.6 %collective-permute-start = (bf16[2,1,8192]{2,1,0:T(2,128)(2,1)S(1)}, bf16[2,1,8192]{2,1,0:T(2,128)(2,1)S(1)}, u32[]{:S(2)}, u32[]{:S(2)}) collective-permute-start(bf16[2,1,8192]{2,1,0:T(2,128)(2,1)S(1)} %slice.7), channel_id=1, source_target_pairs={{0,30},{2,0},{4,2},{6,4},{8,6},{10,8},{12,10},{14,12},{16,14},{18,... | collective-permute-start | bytes 98312 | tf_op jit(solution)/shard_map/ppermute | solution.py:220
  28.4 6.4 %copy-start.18 = (f32[256]{0:T(256)S(1)}, f32[256]{0:T(256)}, u32[]{:S(2)}) copy-start(f32[256]{0:T(256)} %param.8) | copy-start | bytes 3076
  28.4 6.4 %copy-start.19 = (f32[256]{0:T(256)S(1)}, f32[256]{0:T(256)}, u32[]{:S(2)}) copy-start(f32[256]{0:T(256)} %param.9) | copy-start | bytes 3076
  28.4 6.4 %copy-start.20 = (s32[2]{0:T(128)S(1)}, s32[2]{0:T(128)}, u32[]{:S(2)}) copy-start(s32[2]{0:T(128)} %param.6) | copy-start | bytes 28
  35.2 11.2 %copy-start.12 = (f32[1024,1024]{1,0:T(8,128)S(1)}, f32[1024,1024]{1,0:T(8,128)}, u32[]{:S(2)}) copy-start(f32[1024,1024]{1,0:T(8,128)} %broadcast_in_dim.53) | copy-start | bytes 12582916
  35.3 11.2 %copy-start.13 = (f32[1024,1024]{1,0:T(8,128)S(1)}, f32[1024,1024]{1,0:T(8,128)}, u32[]{:S(2)}) copy-start(f32[1024,1024]{1,0:T(8,128)} %broadcast_in_dim.55) | copy-start | bytes 12582916
  60.1 2.4 copy-start.16
  63.5 2.4 copy-start.15
  63.5 3.5 copy-start.14
  66.0 2.1 copy-start.17
  79.1 45.7 %copy-start.7 = (f32[2,2,256,256]{3,2,1,0:T(8,128)S(1)}, f32[2,2,256,256]{3,2,1,0:T(8,128)}, u32[]{:S(2)}) copy-start(f32[2,2,256,256]{3,2,1,0:T(8,128)} %copy.18.one_ref) | copy-start | bytes 3145732
  79.1 45.7 %copy-start.8 = (f32[2,2,256,256]{3,2,1,0:T(8,128)S(1)}, f32[2,2,256,256]{3,2,1,0:T(8,128)}, u32[]{:S(2)}) copy-start(f32[2,2,256,256]{3,2,1,0:T(8,128)} %copy.19.step_ref) | copy-start | bytes 3145732
  156.7 2.6 copy-start.6
  156.7 2.6 copy-start.11
  159.3 104.9 %collective-permute-start.25 = (bf16[8,8,64,256]{3,2,1,0:T(8,128)(2,1)}, bf16[8,8,64,256]{3,2,1,0:T(8,128)(2,1)}, u32[]{:S(2)}, u32[]{:S(2)}) collective-permute-start(bf16[8,8,64,256]{3,2,1,0:T(8,128)(2,1)} %dynamic-slice_bitcast_fusion), channel_id=1, source_target_pairs={{0,2},{2,0},{4,6},{6,4},{8,10},{10,8},{12,14},{14,12},{16,18},{18,... | collective-permute-start | bytes 6291464 | tf_op jit(solution)/shard_map/ppermute | solution.py:176
  191.2 2.6 copy-start.4
  191.2 3.1 copy-start.10
  193.8 73.8 %collective-permute-start.17 = (bf16[8,8,64,256]{3,2,1,0:T(8,128)(2,1)}, bf16[8,8,64,256]{3,2,1,0:T(8,128)(2,1)}, u32[]{:S(2)}, u32[]{:S(2)}) collective-permute-start(bf16[8,8,64,256]{3,2,1,0:T(8,128)(2,1)} %dynamic-slice_bitcast_fusion.1), channel_id=1, source_target_pairs={{0,2},{2,0},{4,6},{6,4},{8,10},{10,8},{12,14},{14,12},{16,18},{18,... | collective-permute-start | bytes 6291464 | tf_op jit(solution)/shard_map/ppermute | solution.py:176
  226.2 2.7 copy-start.2
  226.2 2.7 copy-start.9
  228.9 43.5 %collective-permute-start.9 = (bf16[8,8,64,256]{3,2,1,0:T(8,128)(2,1)}, bf16[8,8,64,256]{3,2,1,0:T(8,128)(2,1)}, u32[]{:S(2)}, u32[]{:S(2)}) collective-permute-start(bf16[8,8,64,256]{3,2,1,0:T(8,128)(2,1)} %dynamic-slice_bitcast_fusion.2), channel_id=1, source_target_pairs={{0,2},{2,0},{4,6},{6,4},{8,10},{10,8},{12,14},{14,12},{16,18},{18,... | collective-permute-start | bytes 6291464 | tf_op jit(solution)/shard_map/ppermute | solution.py:176
  261.1 2.7 copy-start
  263.7 11.5 %collective-permute-start.1 = (bf16[8,8,64,256]{3,2,1,0:T(8,128)(2,1)}, bf16[8,8,64,256]{3,2,1,0:T(8,128)(2,1)S(1)}, u32[]{:S(2)}, u32[]{:S(2)}) collective-permute-start(bf16[8,8,64,256]{3,2,1,0:T(8,128)(2,1)} %dynamic-slice_bitcast_fusion.3), channel_id=1, source_target_pairs={{0,2},{2,0},{4,6},{6,4},{8,10},{10,8},{12,14},{14,12},{16,18},{18,... | collective-permute-start | bytes 6291464 | tf_op jit(solution)/shard_map/ppermute | solution.py:176
  264.2 3.5 copy-start.5
  267.5 26.1 %collective-permute-start.26 = (bf16[4,8,64,256]{3,2,1,0:T(8,128)(2,1)S(1)}, bf16[4,8,64,256]{3,2,1,0:T(8,128)(2,1)S(1)}, u32[]{:S(2)}, u32[]{:S(2)}) collective-permute-start(bf16[4,8,64,256]{3,2,1,0:T(8,128)(2,1)S(1)} %dynamic-slice_bitcast_fusion.4), channel_id=1, source_target_pairs={{0,4},{2,6},{4,0},{6,2},{8,12},{10,14},{12,8},{14,10},{16,20},{18,... | collective-permute-start | bytes 3145736 | tf_op jit(solution)/shard_map/ppermute | solution.py:176
  267.7 4.7 %copy-start.3 = (bf16[16,8,64,256]{3,2,1,0:T(8,128)(2,1)S(1)}, bf16[16,8,64,256]{3,2,1,0:T(8,128)(2,1)}, u32[]{:S(2)}) copy-start(bf16[16,8,64,256]{3,2,1,0:T(8,128)(2,1)} %copy-done.2) | copy-start | bytes 12582916
  270.4 45.7 %collective-permute-start.18 = (bf16[4,8,64,256]{3,2,1,0:T(8,128)(2,1)S(1)}, bf16[4,8,64,256]{3,2,1,0:T(8,128)(2,1)S(1)}, u32[]{:S(2)}, u32[]{:S(2)}) collective-permute-start(bf16[4,8,64,256]{3,2,1,0:T(8,128)(2,1)S(1)} %dynamic-slice_bitcast_fusion.5), channel_id=1, source_target_pairs={{0,4},{2,6},{4,0},{6,2},{8,12},{10,14},{12,8},{14,10},{16,20},{18,... | collective-permute-start | bytes 3145736 | tf_op jit(solution)/shard_map/ppermute | solution.py:176
  272.4 2.8 copy-start.1
  275.1 63.5 %collective-permute-start.10 = (bf16[4,8,64,256]{3,2,1,0:T(8,128)(2,1)S(1)}, bf16[4,8,64,256]{3,2,1,0:T(8,128)(2,1)S(1)}, u32[]{:S(2)}, u32[]{:S(2)}) collective-permute-start(bf16[4,8,64,256]{3,2,1,0:T(8,128)(2,1)S(1)} %dynamic-slice_bitcast_fusion.6), channel_id=1, source_target_pairs={{0,4},{2,6},{4,0},{6,2},{8,12},{10,14},{12,8},{14,10},{16,20},{18,... | collective-permute-start | bytes 3145736 | tf_op jit(solution)/shard_map/ppermute | solution.py:176
  276.3 83.8 %collective-permute-start.2 = (bf16[4,8,64,256]{3,2,1,0:T(8,128)(2,1)S(1)}, bf16[4,8,64,256]{3,2,1,0:T(8,128)(2,1)S(1)}, u32[]{:S(2)}, u32[]{:S(2)}) collective-permute-start(bf16[4,8,64,256]{3,2,1,0:T(8,128)(2,1)S(1)} %dynamic-slice_bitcast_fusion.7), channel_id=1, source_target_pairs={{0,4},{2,6},{4,0},{6,2},{8,12},{10,14},{12,8},{14,10},{16,20},{18,... | collective-permute-start | bytes 3145736 | tf_op jit(solution)/shard_map/ppermute | solution.py:176
  294.1 67.7 %collective-permute-start.27 = (bf16[8,64,256]{2,1,0:T(8,128)(2,1)S(1)}, bf16[8,64,256]{2,1,0:T(8,128)(2,1)S(1)}, u32[]{:S(2)}, u32[]{:S(2)}) collective-permute-start(bf16[8,64,256]{2,1,0:T(8,128)(2,1)S(1)} %get-tuple-element.27), channel_id=1, source_target_pairs={{0,8},{2,10},{4,12},{6,14},{1,9},{3,11},{5,13},{7,15}} | collective-permute-start | bytes 786440 | tf_op jit(solution)/shard_map/ppermute | solution.py:196
  295.4 82.8 %collective-permute-start.30 = (bf16[8,64,256]{2,1,0:T(8,128)(2,1)S(1)}, bf16[8,64,256]{2,1,0:T(8,128)(2,1)S(1)}, u32[]{:S(2)}, u32[]{:S(2)}) collective-permute-start(bf16[8,64,256]{2,1,0:T(8,128)(2,1)S(1)} %get-tuple-element.28), channel_id=1, source_target_pairs={{30,22},{28,20},{26,18},{24,16},{31,23},{29,21},{27,19},{25,17}} | collective-permute-start | bytes 786440 | tf_op jit(solution)/shard_map/ppermute | solution.py:197
  316.6 46.0 %collective-permute-start.19 = (bf16[8,64,256]{2,1,0:T(8,128)(2,1)S(1)}, bf16[8,64,256]{2,1,0:T(8,128)(2,1)S(1)}, u32[]{:S(2)}, u32[]{:S(2)}) collective-permute-start(bf16[8,64,256]{2,1,0:T(8,128)(2,1)S(1)} %get-tuple-element.23), channel_id=1, source_target_pairs={{0,8},{2,10},{4,12},{6,14},{1,9},{3,11},{5,13},{7,15}} | collective-permute-start | bytes 786440 | tf_op jit(solution)/shard_map/ppermute | solution.py:196
  338.6 45.4 %collective-permute-start.22 = (bf16[8,64,256]{2,1,0:T(8,128)(2,1)S(1)}, bf16[8,64,256]{2,1,0:T(8,128)(2,1)S(1)}, u32[]{:S(2)}, u32[]{:S(2)}) collective-permute-start(bf16[8,64,256]{2,1,0:T(8,128)(2,1)S(1)} %get-tuple-element.24), channel_id=1, source_target_pairs={{30,22},{28,20},{26,18},{24,16},{31,23},{29,21},{27,19},{25,17}} | collective-permute-start | bytes 786440 | tf_op jit(solution)/shard_map/ppermute | solution.py:197
  360.1 8.0 %collective-permute-start.11 = (bf16[8,64,256]{2,1,0:T(8,128)(2,1)S(1)}, bf16[8,64,256]{2,1,0:T(8,128)(2,1)S(1)}, u32[]{:S(2)}, u32[]{:S(2)}) collective-permute-start(bf16[8,64,256]{2,1,0:T(8,128)(2,1)S(1)} %get-tuple-element.19), channel_id=1, source_target_pairs={{0,8},{2,10},{4,12},{6,14},{1,9},{3,11},{5,13},{7,15}} | collective-permute-start | bytes 786440 | tf_op jit(solution)/shard_map/ppermute | solution.py:196
  361.9 24.9 %collective-permute-start.14 = (bf16[8,64,256]{2,1,0:T(8,128)(2,1)S(1)}, bf16[8,64,256]{2,1,0:T(8,128)(2,1)S(1)}, u32[]{:S(2)}, u32[]{:S(2)}) collective-permute-start(bf16[8,64,256]{2,1,0:T(8,128)(2,1)S(1)} %get-tuple-element.20), channel_id=1, source_target_pairs={{30,22},{28,20},{26,18},{24,16},{31,23},{29,21},{27,19},{25,17}} | collective-permute-start | bytes 786440 | tf_op jit(solution)/shard_map/ppermute | solution.py:197
  362.6 11.1 %collective-permute-start.3 = (bf16[8,64,256]{2,1,0:T(8,128)(2,1)S(1)}, bf16[8,64,256]{2,1,0:T(8,128)(2,1)S(1)}, u32[]{:S(2)}, u32[]{:S(2)}) collective-permute-start(bf16[8,64,256]{2,1,0:T(8,128)(2,1)S(1)} %get-tuple-element.15), channel_id=1, source_target_pairs={{0,8},{2,10},{4,12},{6,14},{1,9},{3,11},{5,13},{7,15}} | collective-permute-start | bytes 786440 | tf_op jit(solution)/shard_map/ppermute | solution.py:196
  368.1 11.2 %collective-permute-start.28 = (bf16[8,64,256]{2,1,0:T(8,128)(2,1)S(1)}, bf16[8,64,256]{2,1,0:T(8,128)(2,1)S(1)}, u32[]{:S(2)}, u32[]{:S(2)}) collective-permute-start(bf16[8,64,256]{2,1,0:T(8,128)(2,1)S(1)} %fusion.10), channel_id=1, source_target_pairs={{0,8},{2,10},{4,12},{6,14},{8,16},{10,18},{12,20},{14,22},{1,9},{3... | collective-permute-start | bytes 786440 | tf_op jit(solution)/shard_map/ppermute | solution.py:196
  373.8 12.1 %collective-permute-start.20 = (bf16[8,64,256]{2,1,0:T(8,128)(2,1)S(1)}, bf16[8,64,256]{2,1,0:T(8,128)(2,1)S(1)}, u32[]{:S(2)}, u32[]{:S(2)}) collective-permute-start(bf16[8,64,256]{2,1,0:T(8,128)(2,1)S(1)} %fusion.17), channel_id=1, source_target_pairs={{0,8},{2,10},{4,12},{6,14},{8,16},{10,18},{12,20},{14,22},{1,9},{3... | collective-permute-start | bytes 786440 | tf_op jit(solution)/shard_map/ppermute | solution.py:196
  378.2 13.5 %collective-permute-start.6 = (bf16[8,64,256]{2,1,0:T(8,128)(2,1)S(1)}, bf16[8,64,256]{2,1,0:T(8,128)(2,1)S(1)}, u32[]{:S(2)}, u32[]{:S(2)}) collective-permute-start(bf16[8,64,256]{2,1,0:T(8,128)(2,1)S(1)} %get-tuple-element.16), channel_id=1, source_target_pairs={{30,22},{28,20},{26,18},{24,16},{31,23},{29,21},{27,19},{25,17}} | collective-permute-start | bytes 786440 | tf_op jit(solution)/shard_map/ppermute | solution.py:197
  379.4 11.5 %collective-permute-start.12 = (bf16[8,64,256]{2,1,0:T(8,128)(2,1)S(1)}, bf16[8,64,256]{2,1,0:T(8,128)(2,1)S(1)}, u32[]{:S(2)}, u32[]{:S(2)}) collective-permute-start(bf16[8,64,256]{2,1,0:T(8,128)(2,1)S(1)} %fusion.24), channel_id=1, source_target_pairs={{0,8},{2,10},{4,12},{6,14},{8,16},{10,18},{12,20},{14,22},{1,9},{3... | collective-permute-start | bytes 786440 | tf_op jit(solution)/shard_map/ppermute | solution.py:196
  383.9 13.0 %collective-permute-start.4 = (bf16[8,64,256]{2,1,0:T(8,128)(2,1)S(1)}, bf16[8,64,256]{2,1,0:T(8,128)(2,1)S(1)}, u32[]{:S(2)}, u32[]{:S(2)}) collective-permute-start(bf16[8,64,256]{2,1,0:T(8,128)(2,1)S(1)} %fusion.31), channel_id=1, source_target_pairs={{0,8},{2,10},{4,12},{6,14},{8,16},{10,18},{12,20},{14,22},{1,9},{3... | collective-permute-start | bytes 786440 | tf_op jit(solution)/shard_map/ppermute | solution.py:196
  385.9 11.9 %collective-permute-start.31 = (bf16[8,64,256]{2,1,0:T(8,128)(2,1)S(1)}, bf16[8,64,256]{2,1,0:T(8,128)(2,1)S(1)}, u32[]{:S(2)}, u32[]{:S(2)}) collective-permute-start(bf16[8,64,256]{2,1,0:T(8,128)(2,1)S(1)} %get-tuple-element.26), channel_id=1, source_target_pairs={{30,22},{28,20},{26,18},{24,16},{22,14},{20,12},{18,10},{16,8},{31... | collective-permute-start | bytes 786440 | tf_op jit(solution)/shard_map/ppermute | solution.py:197
  386.7 19.8 %collective-permute-start.29 = (bf16[8,64,256]{2,1,0:T(8,128)(2,1)S(1)}, bf16[8,64,256]{2,1,0:T(8,128)(2,1)S(1)}, u32[]{:S(2)}, u32[]{:S(2)}) collective-permute-start(bf16[8,64,256]{2,1,0:T(8,128)(2,1)S(1)} %get-tuple-element.25), channel_id=1, source_target_pairs={{0,8},{2,10},{4,12},{6,14},{8,16},{10,18},{12,20},{14,22},{16,24},... | collective-permute-start | bytes 786440 | tf_op jit(solution)/shard_map/ppermute | solution.py:196
  390.9 12.2 %collective-permute-start.23 = (bf16[8,64,256]{2,1,0:T(8,128)(2,1)S(1)}, bf16[8,64,256]{2,1,0:T(8,128)(2,1)S(1)}, u32[]{:S(2)}, u32[]{:S(2)}) collective-permute-start(bf16[8,64,256]{2,1,0:T(8,128)(2,1)S(1)} %get-tuple-element.22), channel_id=1, source_target_pairs={{30,22},{28,20},{26,18},{24,16},{22,14},{20,12},{18,10},{16,8},{31... | collective-permute-start | bytes 786440 | tf_op jit(solution)/shard_map/ppermute | solution.py:197
  391.7 30.5 %collective-permute-start.21 = (bf16[8,64,256]{2,1,0:T(8,128)(2,1)S(1)}, bf16[8,64,256]{2,1,0:T(8,128)(2,1)S(1)}, u32[]{:S(2)}, u32[]{:S(2)}) collective-permute-start(bf16[8,64,256]{2,1,0:T(8,128)(2,1)S(1)} %get-tuple-element.21), channel_id=1, source_target_pairs={{0,8},{2,10},{4,12},{6,14},{8,16},{10,18},{12,20},{14,22},{16,24},... | collective-permute-start | bytes 786440 | tf_op jit(solution)/shard_map/ppermute | solution.py:196
  396.9 6.9 %collective-permute-start.15 = (bf16[8,64,256]{2,1,0:T(8,128)(2,1)S(1)}, bf16[8,64,256]{2,1,0:T(8,128)(2,1)S(1)}, u32[]{:S(2)}, u32[]{:S(2)}) collective-permute-start(bf16[8,64,256]{2,1,0:T(8,128)(2,1)S(1)} %get-tuple-element.18), channel_id=1, source_target_pairs={{30,22},{28,20},{26,18},{24,16},{22,14},{20,12},{18,10},{16,8},{31... | collective-permute-start | bytes 786440 | tf_op jit(solution)/shard_map/ppermute | solution.py:197
  397.8 28.3 %collective-permute-start.13 = (bf16[8,64,256]{2,1,0:T(8,128)(2,1)S(1)}, bf16[8,64,256]{2,1,0:T(8,128)(2,1)S(1)}, u32[]{:S(2)}, u32[]{:S(2)}) collective-permute-start(bf16[8,64,256]{2,1,0:T(8,128)(2,1)S(1)} %get-tuple-element.17), channel_id=1, source_target_pairs={{0,8},{2,10},{4,12},{6,14},{8,16},{10,18},{12,20},{14,22},{16,24},... | collective-permute-start | bytes 786440 | tf_op jit(solution)/shard_map/ppermute | solution.py:196
  403.0 2.2 collective-permute-start.7
  403.8 16.9 %collective-permute-start.32 = (bf16[8,64,256]{2,1,0:T(8,128)(2,1)S(1)}, bf16[8,64,256]{2,1,0:T(8,128)(2,1)S(1)}, u32[]{:S(2)}, u32[]{:S(2)}) collective-permute-start(bf16[8,64,256]{2,1,0:T(8,128)(2,1)S(1)} %fusion.9), channel_id=1, source_target_pairs={{30,22},{28,20},{26,18},{24,16},{22,14},{20,12},{18,10},{16,8},{14... | collective-permute-start | bytes 786440 | tf_op jit(solution)/shard_map/ppermute | solution.py:197
  405.2 20.7 %collective-permute-start.24 = (bf16[8,64,256]{2,1,0:T(8,128)(2,1)S(1)}, bf16[8,64,256]{2,1,0:T(8,128)(2,1)S(1)}, u32[]{:S(2)}, u32[]{:S(2)}) collective-permute-start(bf16[8,64,256]{2,1,0:T(8,128)(2,1)S(1)} %fusion.16), channel_id=1, source_target_pairs={{30,22},{28,20},{26,18},{24,16},{22,14},{20,12},{18,10},{16,8},{14... | collective-permute-start | bytes 786440 | tf_op jit(solution)/shard_map/ppermute | solution.py:197
  406.6 23.8 %collective-permute-start.5 = (bf16[8,64,256]{2,1,0:T(8,128)(2,1)S(1)}, bf16[8,64,256]{2,1,0:T(8,128)(2,1)S(1)}, u32[]{:S(2)}, u32[]{:S(2)}) collective-permute-start(bf16[8,64,256]{2,1,0:T(8,128)(2,1)S(1)} %get-tuple-element.13), channel_id=1, source_target_pairs={{0,8},{2,10},{4,12},{6,14},{8,16},{10,18},{12,20},{14,22},{16,24},... | collective-permute-start | bytes 786440 | tf_op jit(solution)/shard_map/ppermute | solution.py:196
  420.7 9.5 %collective-permute-start.16 = (bf16[8,64,256]{2,1,0:T(8,128)(2,1)S(1)}, bf16[8,64,256]{2,1,0:T(8,128)(2,1)S(1)}, u32[]{:S(2)}, u32[]{:S(2)}) collective-permute-start(bf16[8,64,256]{2,1,0:T(8,128)(2,1)S(1)} %fusion.23), channel_id=1, source_target_pairs={{30,22},{28,20},{26,18},{24,16},{22,14},{20,12},{18,10},{16,8},{14... | collective-permute-start | bytes 786440 | tf_op jit(solution)/shard_map/ppermute | solution.py:197
  422.2 10.9 %collective-permute-start.8 = (bf16[8,64,256]{2,1,0:T(8,128)(2,1)S(1)}, bf16[8,64,256]{2,1,0:T(8,128)(2,1)S(1)}, u32[]{:S(2)}, u32[]{:S(2)}) collective-permute-start(bf16[8,64,256]{2,1,0:T(8,128)(2,1)S(1)} %fusion.30), channel_id=1, source_target_pairs={{30,22},{28,20},{26,18},{24,16},{22,14},{20,12},{18,10},{16,8},{14... | collective-permute-start | bytes 786440 | tf_op jit(solution)/shard_map/ppermute | solution.py:197
Sparse Core Ops, SparseCore 0:
  434.0 9.3 reduce-scatter.1

commit v2 on v1

v2 whole, which is shorter than its diff:
```python
import functools
import math

import jax
import jax.numpy as jnp
from jax import lax
from jax.experimental import pallas as pl
from jax.experimental.pallas import tpu as pltpu
from jax.sharding import PartitionSpec as P

NFFT = 1024
HALF = NFFT // 2
PARTS = 4
ROWS = 16

wavenumber = 2.0
height = 0.5


def cos_of_turns(count):
    quarter = NFFT // 4
    quadrant = (count + quarter // 2) // quarter
    angle = (count - quadrant * quarter).astype(jnp.float32) * (2.0 * math.pi / NFFT)
    square = angle * angle
    sine = 1.0 / math.factorial(9)
    cosine = 1.0 / math.factorial(8) - square * (1.0 / math.factorial(10))
    cosine = 1.0 + square * (
        -1.0 / 2 + square * (1.0 / 24 + square * (-1.0 / 720 + square * cosine))
    )
    sine = angle * (
        1.0
        + square * (-1.0 / 6 + square * (1.0 / 120 + square * (-1.0 / 5040 + square * sine)))
    )
    value = jnp.where(quadrant % 2 == 0, cosine, sine)
    turned = quadrant % 4
    return jnp.where((turned == 1) | (turned == 2), -value, value)


def fourier_table():
    row = lax.broadcasted_iota(jnp.int32, (2 * HALF, NFFT), 0)
    sample = lax.broadcasted_iota(jnp.int32, (2 * HALF, NFFT), 1)
    turns = (row // 2 * sample + row % 2 * (NFFT // 4)) % NFFT
    window = 0.5 - 0.5 * cos_of_turns(lax.broadcasted_iota(jnp.int32, (1, NFFT), 1))
    value = cos_of_turns(turns) * window
    return (value / math.sqrt(3.0 * NFFT / 8.0)).astype(jnp.bfloat16)


def distances(index, radius, azimuth, total_mics):
    turn = index.astype(jnp.float32) * (2.0 * math.pi / total_mics)
    cycle_cos = jnp.cos(turn)[..., None]
    cycle_sin = jnp.sin(turn)[..., None]
    across = (radius * jnp.cos(azimuth))[None, None, :]
    along = (radius * jnp.sin(azimuth))[None, None, :]
    squared = (
        1.0
        + height * height
        + (radius * radius)[None, None, :]
        - 2.0 * (cycle_cos * across + cycle_sin * along)
    )
    return jnp.sqrt(squared)


def spectra_kernel(segments, signal_ref, edge_ref, weight_ref, table_ref, out_ref, virtual, spread):
    columns = table_ref.shape[0]
    halves, _, lanes = spread.shape
    mics, length = signal_ref.shape[1:]
    chunk = min(256, HALF)

    @pl.when(pl.program_id(1) == 0)
    def _():
        @pl.loop(0, length // chunk)
        def _(place):
            where = pl.ds(pl.multiple_of(place * chunk, chunk), chunk)
            lower = signal_ref[0, :, where].astype(jnp.float32)
            edge = edge_ref[0, :, where].astype(jnp.float32)
            weight = weight_ref[0, :, where]
            row = lax.broadcasted_iota(jnp.int32, lower.shape, 0)
            upper = jnp.where(row == mics - 1, edge, pltpu.roll(lower, mics - 1, 0))
            mixed = (1.0 - weight) * lower + weight * upper
            virtual[where, :] = mixed.T.astype(jnp.bfloat16)

    @pl.loop(0, segments)
    def _(segment):
        start = pl.multiple_of(segment * HALF, HALF)
        product = jnp.dot(
            table_ref[...], virtual[pl.ds(start, NFFT), :], preferred_element_type=jnp.float32
        )
        for half in range(halves):
            spread[half, pl.ds(segment, columns, stride=ROWS), :] = product[
                :, half * lanes : (half + 1) * lanes
            ]

    for half in range(halves):
        for pad in range(segments, ROWS):
            spread[half, pl.ds(pad, columns, stride=ROWS), :] = jnp.zeros(
                (columns, lanes), jnp.float32
            )
        out_ref[0, :, half * lanes : (half + 1) * lanes] = spread[half].astype(jnp.bfloat16)


def spectra_of(signal, edge, weight, table):
    blocks, mics, length = signal.shape
    segments = length // HALF - 1
    tile = HALF
    lanes = min(mics, 128)
    return pl.pallas_call(
        functools.partial(spectra_kernel, segments),
        grid=(blocks, 2 * HALF // tile),
        in_specs=[
            pl.BlockSpec((1, mics, length), lambda b, c: (b, 0, 0)),
            pl.BlockSpec((1, 1, length), lambda b, c: (b, 0, 0)),
            pl.BlockSpec((1, 1, length), lambda b, c: (b, 0, 0)),
            pl.BlockSpec((tile, NFFT), lambda b, c: (c, 0)),
        ],
        out_specs=pl.BlockSpec((1, tile * ROWS, mics), lambda b, c: (b, c, 0)),
        out_shape=jax.ShapeDtypeStruct((blocks, 2 * HALF * ROWS, mics), jnp.bfloat16),
        scratch_shapes=[
            pltpu.VMEM((length, mics), jnp.bfloat16),
            pltpu.VMEM((mics // lanes, tile * ROWS, lanes), jnp.float32),
        ],
        compiler_params=pltpu.CompilerParams(vmem_limit_bytes=50 << 20),
        name="welch",
    )(signal, edge, weight, table)


def beam_kernel(*refs):
    spectra_ref, one_cos, one_sin, step_cos, step_sin, *firsts = refs[:-4]
    out_ref, now, even, odd = refs[-4:]
    blocks, groups, _, bins = spectra_ref.shape[:4]
    mics = one_cos.shape[1]
    units = blocks * groups

    def generate(unit, steer):
        block = unit // groups
        for tile in range(mics // ROWS):
            rows = pl.ds(tile * ROWS, ROWS)
            cos0, sin0 = now[0, rows], now[1, rows]
            cos1, sin1 = one_cos[block, rows], one_sin[block, rows]
            next_cos = cos0 * cos1 - sin0 * sin1
            next_sin = sin0 * cos1 + cos0 * sin1
            double = cos1 + cos1
            turn_cos, turn_sin = step_cos[block, rows], step_sin[block, rows]
            now[0, rows] = cos0 * turn_cos - sin0 * turn_sin
            now[1, rows] = sin0 * turn_cos + cos0 * turn_sin
            for place in range(bins):
                steer[place, 0, rows] = cos0.astype(jnp.bfloat16)
                steer[place, 1, rows] = sin0.astype(jnp.bfloat16)
                cos0, next_cos = next_cos, double * next_cos - cos0
                sin0, next_sin = next_sin, double * next_sin - sin0

    def multiply(unit, steer):
        block, group = unit // groups, unit % groups
        for place in range(bins):
            rows = spectra_ref[block, group, 0, place]
            turned = jnp.concatenate([rows[ROWS:], -rows[:ROWS]], 0)
            product = jnp.dot(rows, steer[place, 0], preferred_element_type=jnp.float32)
            product += jnp.dot(turned, steer[place, 1], preferred_element_type=jnp.float32)
            out_ref[group, place, block] = product.astype(jnp.bfloat16)

    @pl.loop(0, units // 2)
    def _(pair):
        @pl.when(2 * pair % groups == 0)
        def _():
            if firsts:
                now[0] = firsts[0][2 * pair // groups]
                now[1] = firsts[1][2 * pair // groups]
            else:
                now[0] = jnp.ones(now.shape[1:], jnp.float32)
                now[1] = jnp.zeros(now.shape[1:], jnp.float32)

        multiply(jnp.maximum(2 * pair - 1, 0), odd)
        generate(2 * pair, even)
        multiply(2 * pair, even)
        generate(2 * pair + 1, odd)

    multiply(units - 1, odd)


def beams(spectra, waves, part):
    blocks, groups, _, bins, rows, mics = spectra.shape
    points = waves[0].shape[-1]
    wave = pl.BlockSpec((blocks, mics, points), lambda i: (0, 0, 0))
    out = pl.pallas_call(
        beam_kernel,
        grid=(1,),
        in_specs=[
            pl.BlockSpec((blocks, groups, 1, bins, rows, mics), lambda i: (0, 0, part, 0, 0, 0))
        ]
        + [wave] * len(waves),
        out_specs=pl.BlockSpec((groups, bins, blocks, rows, points), lambda i: (0, 0, 0, 0, 0)),
        out_shape=jax.ShapeDtypeStruct((groups, bins, blocks, rows, points), jnp.bfloat16),
        scratch_shapes=[
            pltpu.VMEM((2, mics, points), jnp.float32),
            pltpu.VMEM((bins, 2, mics, points), jnp.bfloat16),
            pltpu.VMEM((bins, 2, mics, points), jnp.bfloat16),
        ],
        compiler_params=pltpu.CompilerParams(vmem_limit_bytes=48 << 20),
        cost_estimate=pl.CostEstimate(
            flops=32 * blocks * groups * bins * rows * mics * points,
            bytes_accessed=blocks * groups * bins * rows * (mics + points) * 2,
            transcendentals=0,
        ),
        name="beams",
    )(spectra, *waves)
    return out.reshape(groups, bins, blocks * rows, points)


def fold_pair(x, bit):
    sectors = lax.axis_size("sector")
    mine = lax.axis_index("sector") // bit % 2
    halves = x.reshape((x.shape[0] // 2, 2) + x.shape[1:])
    sent = lax.dynamic_index_in_dim(halves, 1 - mine, 1, keepdims=False).astype(jnp.bfloat16)
    kept = lax.dynamic_index_in_dim(halves, mine, 1, keepdims=False)
    got = lax.ppermute(sent, "sector", [(i, i ^ bit) for i in range(sectors)])
    return kept.astype(jnp.float32) + got.astype(jnp.float32)


def fold_line(state, stride, step):
    x, right, left = state
    length = x.shape[0]
    place = lax.axis_index("sector") // stride

    def entry(i):
        return lax.dynamic_index_in_dim(x, jnp.clip(i, 0, length - 1), 0, keepdims=False)

    def joined(entry, got):
        return entry if got is None else entry + got.astype(jnp.float32)

    if step == length:
        return joined(joined(entry(place), right), left)
    send_right = joined(entry(length - step + place), right).astype(jnp.bfloat16)
    send_left = joined(entry(place + step - length), left).astype(jnp.bfloat16)
    movers = [i for i in range(length - 1) if i < step]
    pairs = [(i * stride + j, (i + 1) * stride + j) for i in movers for j in range(stride)]
    last = stride * length - 1
    right = lax.ppermute(send_right, "sector", pairs)
    left = lax.ppermute(send_left, "sector", [(last - a, last - b) for a, b in pairs])
    return x, right, left


def fold_stages(sectors):
    stages = []
    stride = 1
    while stride < 4 and sectors // stride % 2 == 0:
        stages.append(functools.partial(fold_pair, bit=stride))
        stride *= 2
    length = sectors // stride
    for step in range(1, length):
        if step == 1:
            stages.append(lambda x: fold_line((x, None, None), stride, 1))
        else:
            stages.append(functools.partial(fold_line, stride=stride, step=step))
    if length > 1:
        final = functools.partial(fold_line, stride=stride, step=length)
    else:
        final = lambda x: x[0]
    return stages, final


def add_over_blk(power):
    devices = lax.axis_size("blk")
    mine = lax.axis_index("blk")
    parts = power.reshape((devices, power.shape[0] // devices) + power.shape[1:])
    total = lax.dynamic_index_in_dim(parts, mine, 0, keepdims=False)
    for shift in range(1, devices):
        sent = lax.dynamic_index_in_dim(parts, (mine + shift) % devices, 0, keepdims=False)
        total += lax.ppermute(sent, "blk", [(i, (i + shift) % devices) for i in range(devices)])
    return total


def local(signal, offsets, fraction, radius, azimuth):
    blocks, mics, length = signal.shape
    sectors = lax.axis_size("sector")
    sector = lax.axis_index("sector")
    total_mics = mics * sectors
    segments = length // HALF - 1
    edge = lax.ppermute(
        signal[:, :1, :], "sector", [(i, (i - 1) % sectors) for i in range(sectors)]
    )
    spectra = spectra_of(signal, edge, fraction[:, None, :], fourier_table())

    band = HALF // sectors
    bins = band // PARTS
    spectra = spectra.reshape(blocks, sectors, PARTS, bins, 2 * ROWS, mics)
    index = (sector * mics + lax.iota(jnp.int32, mics)[None, :] - offsets[:, None]) % total_mics
    phase = wavenumber * distances(index, radius, azimuth, total_mics)
    one = lax.optimization_barrier((jnp.cos(phase), jnp.sin(phase)))

    def joint(a, b):
        return a[0] * b[0] - a[1] * b[1], a[1] * b[0] + a[0] * b[1]

    def power_of(count):
        total, factor = None, one
        while count:
            if count % 2:
                total = factor if total is None else joint(total, factor)
            factor = joint(factor, factor)
            count //= 2
        return total

    step = power_of(band)
    stages, final = fold_stages(sectors)
    states = [None] * PARTS
    for tick in range(PARTS + len(stages)):
        for part in range(PARTS):
            stage = tick - part
            if stage == 0:
                first = power_of(part * bins) if part else ()
                states[part] = beams(spectra, one + step + first, part)
            elif 0 < stage <= len(stages):
                states[part] = stages[stage - 1](states[part])
        states, spectra = lax.optimization_barrier((states, spectra))
    powers = []
    for state in states:
        total = final(state)
        powers.append(jnp.sum(total * total, 1))
    scale = 1.0 / (total_mics * blocks * segments * lax.axis_size("blk"))
    return add_over_blk(jnp.concatenate(powers, 0) * scale)


def solution(mesh):
    return jax.shard_map(
        local,
        mesh=mesh,
        in_specs=(P("blk", "sector", None), P("blk"), P("blk", None), P(), P()),
        out_specs=P(("sector", "blk"), None),
        check_vma=False,
    )
```

time: 452 us -> 332 us (0.73)
  waiting for transfers between devices: 101 us -> 42.1 us
  local copies, waits for them, and re-layouts: 48.6 us -> 17.4 us
  Pallas kernels: 173 us -> 150 us
  between operations: 14.2 us -> 0.93 us
  other arithmetic: 42.8 us -> 47.7 us
    ppermute x8, waiting for transfers between devices: 76.4 us -> 25.9 us  [fold_pair(): got = lax.ppermute(sent, 'sector', [(i, i ^ bit) for i in range(sectors)])]
    pallas_call x4, Pallas kernels: 128 us -> 97.7 us  [beams(): pl.pallas_call(beam_kernel, grid=(1,), in_specs=[pl.BlockSpec((blocks, gr...]
    add x0 -> x11, other arithmetic: none -> 20.4 us  [the longest x8 18.6 us: fold_pair(): return kept.astype(jnp.float32) + got.astype(jnp.float32)]
    broadcast_in_dim x6 -> x1, local copies, waits for them, and re-layouts: 19.4 us -> 0.05 us  [local(): spectra = spectra_of(signal, edge, fraction[:, None, :], fourier_table())]
    another operation x5 -> x0, other arithmetic: 15.3 us -> none  [wave(): return jnp.stack([jnp.cos(phase), jnp.sin(phase)], 1)]
    reduce_scatter x1 -> x0, waiting for transfers between devices: 9.52 us -> none  [local(): return lax.psum_scatter(power, 'blk', scatter_dimension=0, tiled=True)]
    slice x1 -> x0, local copies, waits for them, and re-layouts: 8.89 us -> none  [local(): upper = jnp.concatenate([signal[:, 1:], edge], 1).astype(jnp.float32)]
    another operation x5 -> x0, local copies, waits for them, and re-layouts: 8.04 us -> none  [wave(): return jnp.stack([jnp.cos(phase), jnp.sin(phase)], 1)]
  transfers between devices with their start and end apart: 34 -> 34, of which waited for: 11 -> 10; matrix products, arithmetic and copies ran while one was open for 16% -> 12% of each run, Pallas kernels for 21% -> 22%
where the time goes in v2:
time: 332 us; the launch traced here: 331 us
  Pallas kernels  150 us (45%)
  starting transfers between devices  73 us (22%)
  other arithmetic  47.7 us (14%)
  waiting for transfers between devices  42.1 us (13%)
  local copies, waits for them, and re-layouts  17.4 us (5%)
    pallas_call x4, Pallas kernels, beams(): pl.pallas_call(beam_kernel, grid=(1,), in_specs=[pl.BlockSpec((blocks, gr...  97.7 us
    pallas_call x1, Pallas kernels, spectra_of(): pl.pallas_call(functools.partial(spectra_kernel, segments), grid=(blocks,...  51.9 us
    ppermute x12, starting transfers between devices, fold_line(): right = lax.ppermute(send_right, 'sector', pairs)  49.3 us
    ppermute x8, waiting for transfers between devices, fold_pair(): got = lax.ppermute(sent, 'sector', [(i, i ^ bit) for i in range(sectors)])  25.9 us
    add x8, other arithmetic, fold_pair(): return kept.astype(jnp.float32) + got.astype(jnp.float32)  18.6 us
    convert_element_type x1, other arithmetic, fourier_table(): return (value / math.sqrt(3.0 * NFFT / 8.0)).astype(jnp.bfloat16)  12.4 us
    ppermute x12, starting transfers between devices, fold_line(): lax.ppermute(send_left, 'sector', [(last - a, last - b) for a, b in pairs])  10.7 us
    ppermute x12, waiting for transfers between devices, fold_line(): right = lax.ppermute(send_right, 'sector', pairs)  7.45 us
  transfers between devices with their start and end apart: 34, of which 10 were waited for; matrix products, arithmetic and copies ran while one was open for 12% of the time, Pallas kernels for 22%

profile of v2, /device:TPU:0, one launch (start us, length us, event | category | flops | bytes accessed | tf_op | source)
XLA Modules:
  0.0 330.6 jit_solution(5691700526305608627)
XLA Ops:
  0.0 1.0 slice.3
  1.0 5.5 %collective-permute-start = (bf16[2,1,8192]{2,1,0:T(2,128)(2,1)S(1)}, bf16[2,1,8192]{2,1,0:T(2,128)(2,1)S(1)}, u32[]{:S(2)}, u32[]{:S(2)}) collective-permute-start(bf16[2,1,8192]{2,1,0:T(2,128)(2,1)S(1)} %slice.3), channel_id=1, source_target_pairs={{0,30},{2,0},{4,2},{6,4},{8,6},{10,8},{12,10},{14,12},{16,14},{18,... | collective-permute-start | bytes 98312 | tf_op jit(solution)/shard_map/ppermute | solution.py:277
  6.5 0.7 cosine_multiply_fusion
  7.3 0.8 fusion.87
  8.1 2.3 fusion.47
  10.4 1.2 multiply_add_fusion
  11.6 12.4 %fusion.5.table_ref = bf16[1024,1024]{1,0:T(8,128)(2,1)S(1)} fusion(f32[1024]{0:T(1024)S(1)} %fusion.72, s32[1024]{0:T(1024)S(1)} %get-tuple-element.189, s32[1024]{0:T(1024)S(1)} %get-tuple-element.190, s32[1024]{0:T(1024)S(1)} %get-tuple-element.188, s32[1024]{0:T(1024)S(1)} %get-tuple-element.191, pred[1024]{0:T(1024)(128)(4,1)S(1)} %get-tuple-element.186, ...), kind=kLoop, calls=%fused_computation.18 | loop fusion | flops 89128960 | bytes 2119680 | tf_op jit(solution)/shard_map/convert_element_type | solution.py:45
  24.1 1.5 multiply_subtract_fusion
  25.6 51.9 %welch.1 = bf16[2,16384,256]{2,1,0:T(8,128)(2,1)} custom-call(bf16[2,256,8192]{2,1,0:T(8,128)(2,1)} %signal_ref.1, bf16[2,1,8192]{2,1,0:T(2,128)(2,1)S(1)} %collective-permute-done.edge_ref, f32[2,1,8192]{2,1,0:T(1,128)S(1)} %broadcast_in_dim.2.weight_ref, bf16[1024,1024]{1,0:T(8,128)(2,1)S(1)} %fusion.5.table_ref), custom_call_target="tpu_custom_call" | custom-call | tf_op jit(solution)/shard_map/welch/pallas_call | solution.py:106
  77.5 24.4 %beams.4 = bf16[16,8,2,32,256]{4,3,2,1,0:T(8,128)(2,1)} custom-call(bf16[2,16,4,8,32,256]{5,4,3,2,1,0:T(8,128)(2,1)} %bitcast.166, f32[2,256,256]{2,1,0:T(8,128)S(1)} %get-tuple-element.76.refs_1_, f32[2,256,256]{2,1,0:T(8,128)S(1)} %get-tuple-element.77.refs_2_, f32[2,256,256]{2,1,0:T(8,128)S(1)} %copy-done.9, f32[2,256,256]{2,1,0:T(8,128)S(1)} %copy-done.7), custom_call_target="tpu_custom_call" | custom-call | flops 17179869184 | bytes 8388608 | tf_op jit(solution)/shard_map/beams/pallas_call | solution.py:183
  101.9 3.3 %dynamic-slice_bitcast_fusion.3 = bf16[8,8,64,256]{3,2,1,0:T(8,128)(2,1)} fusion(bf16[8,2,8,64,256]{4,3,2,1,0:T(8,128)(2,1)} %bitcast.184, s32[]{:T(128)S(6)} %select_n.227), kind=kLoop, calls=%fused_computation.51 | loop fusion | bytes 4194308 | tf_op jit(solution)/shard_map/jit(dynamic_index_in_dim)/squeeze | solution.py:212
  105.2 24.5 %beams.5 = bf16[16,8,2,32,256]{4,3,2,1,0:T(8,128)(2,1)} custom-call(bf16[2,16,4,8,32,256]{5,4,3,2,1,0:T(8,128)(2,1)} %bitcast.167, f32[2,256,256]{2,1,0:T(8,128)S(1)} %get-tuple-element.76.refs_1_, f32[2,256,256]{2,1,0:T(8,128)S(1)} %get-tuple-element.77.refs_2_, f32[2,256,256]{2,1,0:T(8,128)S(1)} %copy-done.10, f32[2,256,256]{2,1,0:T(8,128)S(1)} %copy-done.8, ...), custom_call_target="tpu_custom_call" | custom-call | flops 17179869184 | bytes 8388608 | tf_op jit(solution)/shard_map/beams/pallas_call | solution.py:183
  129.7 4.7 %convert_add_fusion.3 = f32[8,8,64,256]{3,2,1,0:T(8,128)} fusion(bf16[8,8,64,256]{3,2,1,0:T(8,128)(2,1)} %collective-permute-done.1, bf16[8,2,8,64,256]{4,3,2,1,0:T(8,128)(2,1)S(1)} %bitcast.185, s32[]{:T(128)S(6)} %select_n.226), kind=kLoop, calls=%fused_computation.22 | loop fusion | flops 3145728 | bytes 8388612 | tf_op jit(solution)/shard_map/add | solution.py:215
  134.4 1.4 dynamic-slice_bitcast_fusion.2
  136.4 1.7 fusion.15
  138.2 24.5 %beams.6 = bf16[16,8,2,32,256]{4,3,2,1,0:T(8,128)(2,1)} custom-call(bf16[2,16,4,8,32,256]{5,4,3,2,1,0:T(8,128)(2,1)} %bitcast.168, f32[2,256,256]{2,1,0:T(8,128)S(1)} %get-tuple-element.76.refs_1_, f32[2,256,256]{2,1,0:T(8,128)S(1)} %get-tuple-element.77.refs_2_, f32[2,256,256]{2,1,0:T(8,128)S(1)} %copy-done.10, f32[2,256,256]{2,1,0:T(8,128)S(1)} %copy-done.8, ...), custom_call_target="tpu_custom_call" | custom-call | flops 17179869184 | bytes 8388608 | tf_op jit(solution)/shard_map/beams/pallas_call | solution.py:183
  163.7 2.0 copy-done.22
  165.7 2.7 convert_add_fusion.2
  168.7 1.3 collective-permute-start.4
  170.9 2.1 collective-permute-start.6
  172.9 24.3 %beams.7 = bf16[16,8,2,32,256]{4,3,2,1,0:T(8,128)(2,1)} custom-call(bf16[2,16,4,8,32,256]{5,4,3,2,1,0:T(8,128)(2,1)} %bitcast.169, f32[2,256,256]{2,1,0:T(8,128)S(1)} %get-tuple-element.76.refs_1_, f32[2,256,256]{2,1,0:T(8,128)S(1)} %get-tuple-element.77.refs_2_, f32[2,256,256]{2,1,0:T(8,128)S(1)} %copy-done.10, f32[2,256,256]{2,1,0:T(8,128)S(1)} %copy-done.8, ...), custom_call_target="tpu_custom_call" | custom-call | flops 17179869184 | bytes 8388608 | tf_op jit(solution)/shard_map/beams/pallas_call | solution.py:183
  197.3 1.8 bitcast_add_fusion.2
  199.0 1.2 copy-done.26
  200.2 0.8 convert_add_fusion.1
  201.7 1.5 dynamic-slice_bitcast_fusion
  203.9 1.4 collective-permute-start.12
  205.3 1.2 fusion.45
  206.5 1.4 collective-permute-start.8
  208.7 1.3 fusion.52
  209.9 2.7 collective-permute-start.10
  212.6 16.7 %collective-permute-done.12 = bf16[4,8,64,256]{3,2,1,0:T(8,128)(2,1)} collective-permute-done((bf16[4,8,64,256]{3,2,1,0:T(8,128)(2,1)S(1)}, bf16[4,8,64,256]{3,2,1,0:T(8,128)(2,1)}, u32[]{:S(2)}, u32[]{:S(2)}) %collective-permute-start.12) | collective-permute-done | bytes 1048608 | tf_op jit(solution)/shard_map/ppermute | solution.py:214
  230.0 3.7 %bitcast_add_fusion.1 = f32[4,8,64,256]{3,2,1,0:T(8,128)} fusion(bf16[4,8,64,256]{3,2,1,0:T(8,128)(2,1)} %collective-permute-done.12, f32[4,2,8,64,256]{4,3,2,1,0:T(8,128)} %bitcast.175, s32[]{:T(128)S(6)} %select_n.230), kind=kLoop, calls=%fused_computation.41 | loop fusion | flops 1048576 | bytes 5242884 | tf_op jit(solution)/shard_map/add | solution.py:215
  233.7 2.3 convert_add_fusion
  236.2 0.8 copy-done.34
  237.0 1.2 copy-done.19
  238.3 1.7 collective-permute-start.20
  240.0 1.2 fusion.43
  241.3 1.3 collective-permute-start.14
  242.6 1.4 collective-permute-start.15
  244.0 1.5 fusion.41
  245.5 4.6 %collective-permute-start.16 = (bf16[8,64,256]{2,1,0:T(8,128)(2,1)S(1)}, bf16[8,64,256]{2,1,0:T(8,128)(2,1)S(1)}, u32[]{:S(2)}, u32[]{:S(2)}) collective-permute-start(bf16[8,64,256]{2,1,0:T(8,128)(2,1)S(1)} %get-tuple-element.166), channel_id=1, source_target_pairs={{0,8},{2,10},{4,12},{6,14},{8,16},{10,18},{12,20},{14,22},{1,9},{3... | collective-permute-start | bytes 786440 | tf_op jit(solution)/shard_map/ppermute | solution.py:236
  250.9 3.6 %collective-permute-start.18 = (bf16[8,64,256]{2,1,0:T(8,128)(2,1)S(1)}, bf16[8,64,256]{2,1,0:T(8,128)(2,1)S(1)}, u32[]{:S(2)}, u32[]{:S(2)}) collective-permute-start(bf16[8,64,256]{2,1,0:T(8,128)(2,1)S(1)} %get-tuple-element.164), channel_id=1, source_target_pairs={{0,8},{2,10},{4,12},{6,14},{1,9},{3,11},{5,13},{7,15}} | collective-permute-start | bytes 786440 | tf_op jit(solution)/shard_map/ppermute | solution.py:236
  254.5 8.7 %collective-permute-done.20 = bf16[4,8,64,256]{3,2,1,0:T(8,128)(2,1)} collective-permute-done((bf16[4,8,64,256]{3,2,1,0:T(8,128)(2,1)S(1)}, bf16[4,8,64,256]{3,2,1,0:T(8,128)(2,1)}, u32[]{:S(2)}, u32[]{:S(2)}) %collective-permute-start.20) | collective-permute-done | bytes 1048608 | tf_op jit(solution)/shard_map/ppermute | solution.py:214
  263.9 2.2 bitcast_add_fusion
  266.4 1.3 collective-permute-start.21
  267.7 1.3 collective-permute-start.22
  269.1 9.0 %collective-permute-start.23 = (bf16[8,64,256]{2,1,0:T(8,128)(2,1)S(1)}, bf16[8,64,256]{2,1,0:T(8,128)(2,1)S(1)}, u32[]{:S(2)}, u32[]{:S(2)}) collective-permute-start(bf16[8,64,256]{2,1,0:T(8,128)(2,1)S(1)} %get-tuple-element.160), channel_id=1, source_target_pairs={{0,8},{2,10},{4,12},{6,14},{8,16},{10,18},{12,20},{14,22},{1,9},{3... | collective-permute-start | bytes 786440 | tf_op jit(solution)/shard_map/ppermute | solution.py:236
  278.9 4.5 %collective-permute-start.25 = (bf16[8,64,256]{2,1,0:T(8,128)(2,1)S(1)}, bf16[8,64,256]{2,1,0:T(8,128)(2,1)S(1)}, u32[]{:S(2)}, u32[]{:S(2)}) collective-permute-start(bf16[8,64,256]{2,1,0:T(8,128)(2,1)S(1)} %get-tuple-element.158), channel_id=1, source_target_pairs={{0,8},{2,10},{4,12},{6,14},{1,9},{3,11},{5,13},{7,15}} | collective-permute-start | bytes 786440 | tf_op jit(solution)/shard_map/ppermute | solution.py:236
  284.4 3.1 collective-permute-done.25
  287.8 4.4 %collective-permute-start.27 = (bf16[8,64,256]{2,1,0:T(8,128)(2,1)S(1)}, bf16[8,64,256]{2,1,0:T(8,128)(2,1)S(1)}, u32[]{:S(2)}, u32[]{:S(2)}) collective-permute-start(bf16[8,64,256]{2,1,0:T(8,128)(2,1)S(1)} %get-tuple-element.156), channel_id=1, source_target_pairs={{0,8},{2,10},{4,12},{6,14},{8,16},{10,18},{12,20},{14,22},{16,24},... | collective-permute-start | bytes 786440 | tf_op jit(solution)/shard_map/ppermute | solution.py:236
  292.2 1.3 collective-permute-start.28
  293.7 6.2 %collective-permute-start.29 = (bf16[8,64,256]{2,1,0:T(8,128)(2,1)S(1)}, bf16[8,64,256]{2,1,0:T(8,128)(2,1)S(1)}, u32[]{:S(2)}, u32[]{:S(2)}) collective-permute-start(bf16[8,64,256]{2,1,0:T(8,128)(2,1)S(1)} %get-tuple-element.154), channel_id=1, source_target_pairs={{0,8},{2,10},{4,12},{6,14},{8,16},{10,18},{12,20},{14,22},{1,9},{3... | collective-permute-start | bytes 786440 | tf_op jit(solution)/shard_map/ppermute | solution.py:236
  300.6 1.4 collective-permute-done.28
  301.9 1.8 collective-permute-done.29
  303.7 1.0 fusion.31
  304.7 9.0 %collective-permute-start.31 = (bf16[8,64,256]{2,1,0:T(8,128)(2,1)}, bf16[8,64,256]{2,1,0:T(8,128)(2,1)}, u32[]{:S(2)}, u32[]{:S(2)}) collective-permute-start(bf16[8,64,256]{2,1,0:T(8,128)(2,1)} %get-tuple-element.152), channel_id=1, source_target_pairs={{0,8},{2,10},{4,12},{6,14},{8,16},{10,18},{12,20},{14,22},{16,24},... | collective-permute-start | bytes 786440 | tf_op jit(solution)/shard_map/ppermute | solution.py:236
  313.7 1.3 collective-permute-start.32
  315.0 2.2 collective-permute-done.31
  317.2 5.1 %collective-permute-done.32 = bf16[8,64,256]{2,1,0:T(8,128)(2,1)} collective-permute-done((bf16[8,64,256]{2,1,0:T(8,128)(2,1)}, bf16[8,64,256]{2,1,0:T(8,128)(2,1)}, u32[]{:S(2)}, u32[]{:S(2)}) %collective-permute-start.32) | collective-permute-done | bytes 262176 | tf_op jit(solution)/shard_map/ppermute | solution.py:237
  322.3 1.3 fusion.21
  323.6 1.3 fusion.24
  324.9 1.2 fusion.27
  326.2 1.6 collective-permute-start.33
  327.8 2.2 collective-permute-done.33
  (129 shorter events, 10.9 us)
Async XLA Ops:
  1.0 24.6 %collective-permute-start = (bf16[2,1,8192]{2,1,0:T(2,128)(2,1)S(1)}, bf16[2,1,8192]{2,1,0:T(2,128)(2,1)S(1)}, u32[]{:S(2)}, u32[]{:S(2)}) collective-permute-start(bf16[2,1,8192]{2,1,0:T(2,128)(2,1)S(1)} %slice.3), channel_id=1, source_target_pairs={{0,30},{2,0},{4,2},{6,4},{8,6},{10,8},{12,10},{14,12},{16,14},{18,... | collective-permute-start | bytes 98312 | tf_op jit(solution)/shard_map/ppermute | solution.py:277
  10.3 15.2 %copy-start.35 = (f32[2,8192]{1,0:T(2,128)S(1)}, f32[2,8192]{1,0:T(2,128)}, u32[]{:S(2)}) copy-start(f32[2,8192]{1,0:T(2,128)} %param.7) | copy-start | bytes 196612
  11.6 12.5 %copy-start = (f32[2,256,256]{2,1,0:T(8,128)}, f32[2,256,256]{2,1,0:T(8,128)S(1)}, u32[]{:S(2)}) copy-start(f32[2,256,256]{2,1,0:T(8,128)S(1)} %get-tuple-element.148.refs_6_) | copy-start | bytes 1572868
  11.6 12.5 %copy-start.2 = (f32[2,256,256]{2,1,0:T(8,128)}, f32[2,256,256]{2,1,0:T(8,128)S(1)}, u32[]{:S(2)}) copy-start(f32[2,256,256]{2,1,0:T(8,128)S(1)} %get-tuple-element.149.refs_6_) | copy-start | bytes 1572868
  11.6 12.5 %copy-start.4 = (f32[2,256,256]{2,1,0:T(8,128)}, f32[2,256,256]{2,1,0:T(8,128)S(1)}, u32[]{:S(2)}) copy-start(f32[2,256,256]{2,1,0:T(8,128)S(1)} %get-tuple-element.150.refs_5_) | copy-start | bytes 1572868
  25.6 51.9 %copy-start.7 = (f32[2,256,256]{2,1,0:T(8,128)S(1)}, f32[2,256,256]{2,1,0:T(8,128)}, u32[]{:S(2)}) copy-start(f32[2,256,256]{2,1,0:T(8,128)} %get-tuple-element.176.refs_4_) | copy-start | bytes 1572868
  25.6 51.9 %copy-start.9 = (f32[2,256,256]{2,1,0:T(8,128)S(1)}, f32[2,256,256]{2,1,0:T(8,128)}, u32[]{:S(2)}) copy-start(f32[2,256,256]{2,1,0:T(8,128)} %get-tuple-element.177.refs_3_) | copy-start | bytes 1572868
  101.9 3.3 %copy-start.3 = (f32[2,256,256]{2,1,0:T(8,128)S(1)}, f32[2,256,256]{2,1,0:T(8,128)}, u32[]{:S(2)}) copy-start(f32[2,256,256]{2,1,0:T(8,128)} %copy-done.2) | copy-start | bytes 1572868
  101.9 3.3 %copy-start.5 = (f32[2,256,256]{2,1,0:T(8,128)S(1)}, f32[2,256,256]{2,1,0:T(8,128)}, u32[]{:S(2)}) copy-start(f32[2,256,256]{2,1,0:T(8,128)} %copy-done.4) | copy-start | bytes 1572868
  101.9 3.3 %copy-start.8 = (f32[2,256,256]{2,1,0:T(8,128)S(1)}, f32[2,256,256]{2,1,0:T(8,128)}, u32[]{:S(2)}) copy-start(f32[2,256,256]{2,1,0:T(8,128)} %get-tuple-element.176.refs_4_) | copy-start | bytes 1572868
  101.9 3.3 %copy-start.10 = (f32[2,256,256]{2,1,0:T(8,128)S(1)}, f32[2,256,256]{2,1,0:T(8,128)}, u32[]{:S(2)}) copy-start(f32[2,256,256]{2,1,0:T(8,128)} %get-tuple-element.177.refs_3_) | copy-start | bytes 1572868
  105.2 24.5 %collective-permute-start.1 = (bf16[8,8,64,256]{3,2,1,0:T(8,128)(2,1)}, bf16[8,8,64,256]{3,2,1,0:T(8,128)(2,1)}, u32[]{:S(2)}, u32[]{:S(2)}) collective-permute-start(bf16[8,8,64,256]{3,2,1,0:T(8,128)(2,1)} %dynamic-slice_bitcast_fusion.3), channel_id=1, source_target_pairs={{0,2},{2,0},{4,6},{6,4},{8,10},{10,8},{12,14},{14,12},{16,18},{18,... | collective-permute-start | bytes 6291464 | tf_op jit(solution)/shard_map/ppermute | solution.py:214
  105.2 24.5 %copy-start.27 = (bf16[16,8,2,32,256]{4,3,2,1,0:T(8,128)(2,1)S(1)}, bf16[16,8,2,32,256]{4,3,2,1,0:T(8,128)(2,1)}, u32[]{:S(2)}) copy-start(bf16[16,8,2,32,256]{4,3,2,1,0:T(8,128)(2,1)} %beams.4) | copy-start | bytes 12582916
  129.7 4.7 %copy-start.21 = (bf16[16,8,2,32,256]{4,3,2,1,0:T(8,128)(2,1)S(1)}, bf16[16,8,2,32,256]{4,3,2,1,0:T(8,128)(2,1)}, u32[]{:S(2)}) copy-start(bf16[16,8,2,32,256]{4,3,2,1,0:T(8,128)(2,1)} %beams.5) | copy-start | bytes 12582916
  134.4 3.8 %copy-start.1 = (f32[2,256,256]{2,1,0:T(8,128)S(1)}, f32[2,256,256]{2,1,0:T(8,128)}, u32[]{:S(2)}) copy-start(f32[2,256,256]{2,1,0:T(8,128)} %copy-done) | copy-start | bytes 1572868
  134.4 3.8 %copy-start.11 = (f32[2,256,256]{2,1,0:T(8,128)S(1)}, f32[2,256,256]{2,1,0:T(8,128)}, u32[]{:S(2)}) copy-start(f32[2,256,256]{2,1,0:T(8,128)} %get-tuple-element.178.refs_5_) | copy-start | bytes 1572868
  135.9 27.8 %collective-permute-start.3 = (bf16[8,8,64,256]{3,2,1,0:T(8,128)(2,1)}, bf16[8,8,64,256]{3,2,1,0:T(8,128)(2,1)}, u32[]{:S(2)}, u32[]{:S(2)}) collective-permute-start(bf16[8,8,64,256]{3,2,1,0:T(8,128)(2,1)} %dynamic-slice_bitcast_fusion.2), channel_id=1, source_target_pairs={{0,2},{2,0},{4,6},{6,4},{8,10},{10,8},{12,14},{14,12},{16,18},{18,... | collective-permute-start | bytes 6291464 | tf_op jit(solution)/shard_map/ppermute | solution.py:214
  138.1 25.1 %collective-permute-start.2 = (bf16[4,8,64,256]{3,2,1,0:T(8,128)(2,1)S(1)}, bf16[4,8,64,256]{3,2,1,0:T(8,128)(2,1)S(1)}, u32[]{:S(2)}, u32[]{:S(2)}) collective-permute-start(bf16[4,8,64,256]{3,2,1,0:T(8,128)(2,1)S(1)} %fusion.15), channel_id=1, source_target_pairs={{0,4},{2,6},{4,0},{6,2},{8,12},{10,14},{12,8},{14,10},{16,20},{18,... | collective-permute-start | bytes 3145736 | tf_op jit(solution)/shard_map/ppermute | solution.py:214
  138.2 25.1 %copy-start.18 = (f32[8,8,64,256]{3,2,1,0:T(8,128)S(1)}, f32[8,8,64,256]{3,2,1,0:T(8,128)}, u32[]{:S(2)}) copy-start(f32[8,8,64,256]{3,2,1,0:T(8,128)} %convert_add_fusion.3) | copy-start | bytes 12582916
  162.7 2.9 copy-start.22
  163.6 5.0 %copy-start.13 = (f32[4,8,64,256]{3,2,1,0:T(8,128)}, f32[4,8,64,256]{3,2,1,0:T(8,128)S(1)}, u32[]{:S(2)}) copy-start(f32[4,8,64,256]{3,2,1,0:T(8,128)S(1)} %bitcast_add_fusion.3) | copy-start | bytes 6291460
  163.7 4.7 %copy-start.25 = (bf16[16,8,2,32,256]{4,3,2,1,0:T(8,128)(2,1)S(1)}, bf16[16,8,2,32,256]{4,3,2,1,0:T(8,128)(2,1)}, u32[]{:S(2)}) copy-start(bf16[16,8,2,32,256]{4,3,2,1,0:T(8,128)(2,1)} %beams.6) | copy-start | bytes 12582916
  168.4 4.6 %copy-start.6 = (f32[2,256,256]{2,1,0:T(8,128)S(1)}, f32[2,256,256]{2,1,0:T(8,128)}, u32[]{:S(2)}) copy-start(f32[2,256,256]{2,1,0:T(8,128)} %get-tuple-element.175.refs_5_) | copy-start | bytes 1572868
  168.4 4.6 %copy-start.12 = (f32[2,256,256]{2,1,0:T(8,128)S(1)}, f32[2,256,256]{2,1,0:T(8,128)}, u32[]{:S(2)}) copy-start(f32[2,256,256]{2,1,0:T(8,128)} %get-tuple-element.147.refs_6_) | copy-start | bytes 1572868
  168.5 30.5 %collective-permute-start.7 = (bf16[8,8,64,256]{3,2,1,0:T(8,128)(2,1)S(1)}, bf16[8,8,64,256]{3,2,1,0:T(8,128)(2,1)S(1)}, u32[]{:S(2)}, u32[]{:S(2)}) collective-permute-start(bf16[8,8,64,256]{3,2,1,0:T(8,128)(2,1)S(1)} %dynamic-slice_bitcast_fusion.1), channel_id=1, source_target_pairs={{0,2},{2,0},{4,6},{6,4},{8,10},{10,8},{12,14},{14,12},{16,18},{18,... | collective-permute-start | bytes 6291464 | tf_op jit(solution)/shard_map/ppermute | solution.py:214
  168.7 32.3 %collective-permute-start.4 = (bf16[8,64,256]{2,1,0:T(8,128)(2,1)S(1)}, bf16[8,64,256]{2,1,0:T(8,128)(2,1)S(1)}, u32[]{:S(2)}, u32[]{:S(2)}) collective-permute-start(bf16[8,64,256]{2,1,0:T(8,128)(2,1)S(1)} %get-tuple-element.174), channel_id=1, source_target_pairs={{0,8},{2,10},{4,12},{6,14},{1,9},{3,11},{5,13},{7,15}} | collective-permute-start | bytes 786440 | tf_op jit(solution)/shard_map/ppermute | solution.py:236
  170.0 31.0 %collective-permute-start.5 = (bf16[8,64,256]{2,1,0:T(8,128)(2,1)S(1)}, bf16[8,64,256]{2,1,0:T(8,128)(2,1)S(1)}, u32[]{:S(2)}, u32[]{:S(2)}) collective-permute-start(bf16[8,64,256]{2,1,0:T(8,128)(2,1)S(1)} %get-tuple-element.173), channel_id=1, source_target_pairs={{30,22},{28,20},{26,18},{24,16},{31,23},{29,21},{27,19},{25,17}} | collective-permute-start | bytes 786440 | tf_op jit(solution)/shard_map/ppermute | solution.py:237
  170.9 26.4 %collective-permute-start.6 = (bf16[4,8,64,256]{3,2,1,0:T(8,128)(2,1)S(1)}, bf16[4,8,64,256]{3,2,1,0:T(8,128)(2,1)S(1)}, u32[]{:S(2)}, u32[]{:S(2)}) collective-permute-start(bf16[4,8,64,256]{3,2,1,0:T(8,128)(2,1)S(1)} %fusion.16), channel_id=1, source_target_pairs={{0,4},{2,6},{4,0},{6,2},{8,12},{10,14},{12,8},{14,10},{16,20},{18,... | collective-permute-start | bytes 3145736 | tf_op jit(solution)/shard_map/ppermute | solution.py:214
  197.2 2.9 copy-start.26
  201.0 4.3 %copy-start.14 = (f32[4,8,64,256]{3,2,1,0:T(8,128)S(1)}, f32[4,8,64,256]{3,2,1,0:T(8,128)}, u32[]{:S(2)}) copy-start(f32[4,8,64,256]{3,2,1,0:T(8,128)} %copy-done.13) | copy-start | bytes 6291460
  201.0 2.9 copy-start.33
  203.2 30.5 %collective-permute-start.13 = (bf16[8,8,64,256]{3,2,1,0:T(8,128)(2,1)}, bf16[8,8,64,256]{3,2,1,0:T(8,128)(2,1)}, u32[]{:S(2)}, u32[]{:S(2)}) collective-permute-start(bf16[8,8,64,256]{3,2,1,0:T(8,128)(2,1)} %dynamic-slice_bitcast_fusion), channel_id=1, source_target_pairs={{0,2},{2,0},{4,6},{6,4},{8,10},{10,8},{12,14},{14,12},{16,18},{18,... | collective-permute-start | bytes 6291464 | tf_op jit(solution)/shard_map/ppermute | solution.py:214
  203.9 25.4 %collective-permute-start.12 = (bf16[4,8,64,256]{3,2,1,0:T(8,128)(2,1)S(1)}, bf16[4,8,64,256]{3,2,1,0:T(8,128)(2,1)}, u32[]{:S(2)}, u32[]{:S(2)}) collective-permute-start(bf16[4,8,64,256]{3,2,1,0:T(8,128)(2,1)S(1)} %fusion.17), channel_id=1, source_target_pairs={{0,4},{2,6},{4,0},{6,2},{8,12},{10,14},{12,8},{14,10},{16,20},{18,... | collective-permute-start | bytes 3145736 | tf_op jit(solution)/shard_map/ppermute | solution.py:214
  205.3 28.4 %copy-start.24 = (bf16[16,8,2,32,256]{4,3,2,1,0:T(8,128)(2,1)S(1)}, bf16[16,8,2,32,256]{4,3,2,1,0:T(8,128)(2,1)}, u32[]{:S(2)}) copy-start(bf16[16,8,2,32,256]{4,3,2,1,0:T(8,128)(2,1)} %beams.7) | copy-start | bytes 12582916
  206.5 29.6 %collective-permute-start.8 = (bf16[8,64,256]{2,1,0:T(8,128)(2,1)S(1)}, bf16[8,64,256]{2,1,0:T(8,128)(2,1)S(1)}, u32[]{:S(2)}, u32[]{:S(2)}) collective-permute-start(bf16[8,64,256]{2,1,0:T(8,128)(2,1)S(1)} %get-tuple-element.172), channel_id=1, source_target_pairs={{0,8},{2,10},{4,12},{6,14},{8,16},{10,18},{12,20},{14,22},{1,9},{3... | collective-permute-start | bytes 786440 | tf_op jit(solution)/shard_map/ppermute | solution.py:236
  208.0 28.1 %collective-permute-start.9 = (bf16[8,64,256]{2,1,0:T(8,128)(2,1)S(1)}, bf16[8,64,256]{2,1,0:T(8,128)(2,1)S(1)}, u32[]{:S(2)}, u32[]{:S(2)}) collective-permute-start(bf16[8,64,256]{2,1,0:T(8,128)(2,1)S(1)} %get-tuple-element.171), channel_id=1, source_target_pairs={{30,22},{28,20},{26,18},{24,16},{22,14},{20,12},{18,10},{16,8},{31... | collective-permute-start | bytes 786440 | tf_op jit(solution)/shard_map/ppermute | solution.py:237
  209.9 26.2 %collective-permute-start.10 = (bf16[8,64,256]{2,1,0:T(8,128)(2,1)S(1)}, bf16[8,64,256]{2,1,0:T(8,128)(2,1)S(1)}, u32[]{:S(2)}, u32[]{:S(2)}) collective-permute-start(bf16[8,64,256]{2,1,0:T(8,128)(2,1)S(1)} %get-tuple-element.170), channel_id=1, source_target_pairs={{0,8},{2,10},{4,12},{6,14},{1,9},{3,11},{5,13},{7,15}} | collective-permute-start | bytes 786440 | tf_op jit(solution)/shard_map/ppermute | solution.py:236
  229.3 6.8 %collective-permute-start.11 = (bf16[8,64,256]{2,1,0:T(8,128)(2,1)S(1)}, bf16[8,64,256]{2,1,0:T(8,128)(2,1)S(1)}, u32[]{:S(2)}, u32[]{:S(2)}) collective-permute-start(bf16[8,64,256]{2,1,0:T(8,128)(2,1)S(1)} %get-tuple-element.169), channel_id=1, source_target_pairs={{30,22},{28,20},{26,18},{24,16},{31,23},{29,21},{27,19},{25,17}} | collective-permute-start | bytes 786440 | tf_op jit(solution)/shard_map/ppermute | solution.py:237
  238.3 24.8 %collective-permute-start.20 = (bf16[4,8,64,256]{3,2,1,0:T(8,128)(2,1)S(1)}, bf16[4,8,64,256]{3,2,1,0:T(8,128)(2,1)}, u32[]{:S(2)}, u32[]{:S(2)}) collective-permute-start(bf16[4,8,64,256]{3,2,1,0:T(8,128)(2,1)S(1)} %fusion.18), channel_id=1, source_target_pairs={{0,4},{2,6},{4,0},{6,2},{8,12},{10,14},{12,8},{14,10},{16,20},{18,... | collective-permute-start | bytes 3145736 | tf_op jit(solution)/shard_map/ppermute | solution.py:214
  240.0 10.8 %copy-start.16 = (f32[4,8,64,256]{3,2,1,0:T(8,128)S(1)}, f32[4,8,64,256]{3,2,1,0:T(8,128)}, u32[]{:S(2)}) copy-start(f32[4,8,64,256]{3,2,1,0:T(8,128)} %bitcast_add_fusion.1) | copy-start | bytes 6291460
  241.3 9.6 %collective-permute-start.14 = (bf16[8,64,256]{2,1,0:T(8,128)(2,1)S(1)}, bf16[8,64,256]{2,1,0:T(8,128)(2,1)S(1)}, u32[]{:S(2)}, u32[]{:S(2)}) collective-permute-start(bf16[8,64,256]{2,1,0:T(8,128)(2,1)S(1)} %get-tuple-element.168), channel_id=1, source_target_pairs={{0,8},{2,10},{4,12},{6,14},{8,16},{10,18},{12,20},{14,22},{16,24},... | collective-permute-start | bytes 786440 | tf_op jit(solution)/shard_map/ppermute | solution.py:236
  242.6 23.6 %copy-start.15 = (f32[4,8,64,256]{3,2,1,0:T(8,128)S(1)}, f32[4,8,64,256]{3,2,1,0:T(8,128)}, u32[]{:S(2)}) copy-start(f32[4,8,64,256]{3,2,1,0:T(8,128)} %bitcast_add_fusion.2) | copy-start | bytes 6291460
  242.6 23.5 %collective-permute-start.15 = (bf16[8,64,256]{2,1,0:T(8,128)(2,1)S(1)}, bf16[8,64,256]{2,1,0:T(8,128)(2,1)S(1)}, u32[]{:S(2)}, u32[]{:S(2)}) collective-permute-start(bf16[8,64,256]{2,1,0:T(8,128)(2,1)S(1)} %get-tuple-element.167), channel_id=1, source_target_pairs={{30,22},{28,20},{26,18},{24,16},{22,14},{20,12},{18,10},{16,8},{14... | collective-permute-start | bytes 786440 | tf_op jit(solution)/shard_map/ppermute | solution.py:237
  245.5 20.6 %collective-permute-start.16 = (bf16[8,64,256]{2,1,0:T(8,128)(2,1)S(1)}, bf16[8,64,256]{2,1,0:T(8,128)(2,1)S(1)}, u32[]{:S(2)}, u32[]{:S(2)}) collective-permute-start(bf16[8,64,256]{2,1,0:T(8,128)(2,1)S(1)} %get-tuple-element.166), channel_id=1, source_target_pairs={{0,8},{2,10},{4,12},{6,14},{8,16},{10,18},{12,20},{14,22},{1,9},{3... | collective-permute-start | bytes 786440 | tf_op jit(solution)/shard_map/ppermute | solution.py:236
  250.1 16.0 %collective-permute-start.17 = (bf16[8,64,256]{2,1,0:T(8,128)(2,1)S(1)}, bf16[8,64,256]{2,1,0:T(8,128)(2,1)S(1)}, u32[]{:S(2)}, u32[]{:S(2)}) collective-permute-start(bf16[8,64,256]{2,1,0:T(8,128)(2,1)S(1)} %get-tuple-element.165), channel_id=1, source_target_pairs={{30,22},{28,20},{26,18},{24,16},{22,14},{20,12},{18,10},{16,8},{31... | collective-permute-start | bytes 786440 | tf_op jit(solution)/shard_map/ppermute | solution.py:237
  250.9 15.3 %collective-permute-start.18 = (bf16[8,64,256]{2,1,0:T(8,128)(2,1)S(1)}, bf16[8,64,256]{2,1,0:T(8,128)(2,1)S(1)}, u32[]{:S(2)}, u32[]{:S(2)}) collective-permute-start(bf16[8,64,256]{2,1,0:T(8,128)(2,1)S(1)} %get-tuple-element.164), channel_id=1, source_target_pairs={{0,8},{2,10},{4,12},{6,14},{1,9},{3,11},{5,13},{7,15}} | collective-permute-start | bytes 786440 | tf_op jit(solution)/shard_map/ppermute | solution.py:236
  263.2 3.0 collective-permute-start.19
  266.1 37.6 %copy-start.17 = (f32[4,8,64,256]{3,2,1,0:T(8,128)}, f32[4,8,64,256]{3,2,1,0:T(8,128)S(1)}, u32[]{:S(2)}) copy-start(f32[4,8,64,256]{3,2,1,0:T(8,128)S(1)} %bitcast_add_fusion) | copy-start | bytes 6291460
  266.1 27.5 %copy-start.28 = (bf16[8,64,256]{2,1,0:T(8,128)(2,1)}, bf16[8,64,256]{2,1,0:T(8,128)(2,1)S(1)}, u32[]{:S(2)}) copy-start(bf16[8,64,256]{2,1,0:T(8,128)(2,1)S(1)} %collective-permute-done.15) | copy-start | bytes 786436
  266.4 17.1 %collective-permute-start.21 = (bf16[8,64,256]{2,1,0:T(8,128)(2,1)S(1)}, bf16[8,64,256]{2,1,0:T(8,128)(2,1)S(1)}, u32[]{:S(2)}, u32[]{:S(2)}) collective-permute-start(bf16[8,64,256]{2,1,0:T(8,128)(2,1)S(1)} %get-tuple-element.162), channel_id=1, source_target_pairs={{0,8},{2,10},{4,12},{6,14},{8,16},{10,18},{12,20},{14,22},{16,24},... | collective-permute-start | bytes 786440 | tf_op jit(solution)/shard_map/ppermute | solution.py:236
  267.7 16.4 %collective-permute-start.22 = (bf16[8,64,256]{2,1,0:T(8,128)(2,1)S(1)}, bf16[8,64,256]{2,1,0:T(8,128)(2,1)S(1)}, u32[]{:S(2)}, u32[]{:S(2)}) collective-permute-start(bf16[8,64,256]{2,1,0:T(8,128)(2,1)S(1)} %get-tuple-element.161), channel_id=1, source_target_pairs={{30,22},{28,20},{26,18},{24,16},{22,14},{20,12},{18,10},{16,8},{14... | collective-permute-start | bytes 786440 | tf_op jit(solution)/shard_map/ppermute | solution.py:237
  269.1 15.3 %collective-permute-start.23 = (bf16[8,64,256]{2,1,0:T(8,128)(2,1)S(1)}, bf16[8,64,256]{2,1,0:T(8,128)(2,1)S(1)}, u32[]{:S(2)}, u32[]{:S(2)}) collective-permute-start(bf16[8,64,256]{2,1,0:T(8,128)(2,1)S(1)} %get-tuple-element.160), channel_id=1, source_target_pairs={{0,8},{2,10},{4,12},{6,14},{8,16},{10,18},{12,20},{14,22},{1,9},{3... | collective-permute-start | bytes 786440 | tf_op jit(solution)/shard_map/ppermute | solution.py:236
  278.1 6.3 %collective-permute-start.24 = (bf16[8,64,256]{2,1,0:T(8,128)(2,1)S(1)}, bf16[8,64,256]{2,1,0:T(8,128)(2,1)S(1)}, u32[]{:S(2)}, u32[]{:S(2)}) collective-permute-start(bf16[8,64,256]{2,1,0:T(8,128)(2,1)S(1)} %get-tuple-element.159), channel_id=1, source_target_pairs={{30,22},{28,20},{26,18},{24,16},{22,14},{20,12},{18,10},{16,8},{31... | collective-permute-start | bytes 786440 | tf_op jit(solution)/shard_map/ppermute | solution.py:237
  278.9 8.7 %collective-permute-start.25 = (bf16[8,64,256]{2,1,0:T(8,128)(2,1)S(1)}, bf16[8,64,256]{2,1,0:T(8,128)(2,1)S(1)}, u32[]{:S(2)}, u32[]{:S(2)}) collective-permute-start(bf16[8,64,256]{2,1,0:T(8,128)(2,1)S(1)} %get-tuple-element.158), channel_id=1, source_target_pairs={{0,8},{2,10},{4,12},{6,14},{1,9},{3,11},{5,13},{7,15}} | collective-permute-start | bytes 786440 | tf_op jit(solution)/shard_map/ppermute | solution.py:236
  283.4 4.2 %collective-permute-start.26 = (bf16[8,64,256]{2,1,0:T(8,128)(2,1)S(1)}, bf16[8,64,256]{2,1,0:T(8,128)(2,1)S(1)}, u32[]{:S(2)}, u32[]{:S(2)}) collective-permute-start(bf16[8,64,256]{2,1,0:T(8,128)(2,1)S(1)} %get-tuple-element.157), channel_id=1, source_target_pairs={{30,22},{28,20},{26,18},{24,16},{31,23},{29,21},{27,19},{25,17}} | collective-permute-start | bytes 786440 | tf_op jit(solution)/shard_map/ppermute | solution.py:237
  287.8 12.8 %collective-permute-start.27 = (bf16[8,64,256]{2,1,0:T(8,128)(2,1)S(1)}, bf16[8,64,256]{2,1,0:T(8,128)(2,1)S(1)}, u32[]{:S(2)}, u32[]{:S(2)}) collective-permute-start(bf16[8,64,256]{2,1,0:T(8,128)(2,1)S(1)} %get-tuple-element.156), channel_id=1, source_target_pairs={{0,8},{2,10},{4,12},{6,14},{8,16},{10,18},{12,20},{14,22},{16,24},... | collective-permute-start | bytes 786440 | tf_op jit(solution)/shard_map/ppermute | solution.py:236
  292.2 9.8 %collective-permute-start.28 = (bf16[8,64,256]{2,1,0:T(8,128)(2,1)S(1)}, bf16[8,64,256]{2,1,0:T(8,128)(2,1)S(1)}, u32[]{:S(2)}, u32[]{:S(2)}) collective-permute-start(bf16[8,64,256]{2,1,0:T(8,128)(2,1)S(1)} %get-tuple-element.155), channel_id=1, source_target_pairs={{30,22},{28,20},{26,18},{24,16},{22,14},{20,12},{18,10},{16,8},{14... | collective-permute-start | bytes 786440 | tf_op jit(solution)/shard_map/ppermute | solution.py:237
  293.7 32.4 %copy-start.29 = (bf16[8,64,256]{2,1,0:T(8,128)(2,1)S(1)}, bf16[8,64,256]{2,1,0:T(8,128)(2,1)}, u32[]{:S(2)}) copy-start(bf16[8,64,256]{2,1,0:T(8,128)(2,1)} %copy-done.28) | copy-start | bytes 786436
  293.7 10.0 %collective-permute-start.29 = (bf16[8,64,256]{2,1,0:T(8,128)(2,1)S(1)}, bf16[8,64,256]{2,1,0:T(8,128)(2,1)S(1)}, u32[]{:S(2)}, u32[]{:S(2)}) collective-permute-start(bf16[8,64,256]{2,1,0:T(8,128)(2,1)S(1)} %get-tuple-element.154), channel_id=1, source_target_pairs={{0,8},{2,10},{4,12},{6,14},{8,16},{10,18},{12,20},{14,22},{1,9},{3... | collective-permute-start | bytes 786440 | tf_op jit(solution)/shard_map/ppermute | solution.py:236
  299.9 3.9 %collective-permute-start.30 = (bf16[8,64,256]{2,1,0:T(8,128)(2,1)S(1)}, bf16[8,64,256]{2,1,0:T(8,128)(2,1)S(1)}, u32[]{:S(2)}, u32[]{:S(2)}) collective-permute-start(bf16[8,64,256]{2,1,0:T(8,128)(2,1)S(1)} %get-tuple-element.153), channel_id=1, source_target_pairs={{30,22},{28,20},{26,18},{24,16},{22,14},{20,12},{18,10},{16,8},{31... | collective-permute-start | bytes 786440 | tf_op jit(solution)/shard_map/ppermute | solution.py:237
  301.9 2.8 copy-start.30
  304.7 12.5 %collective-permute-start.31 = (bf16[8,64,256]{2,1,0:T(8,128)(2,1)}, bf16[8,64,256]{2,1,0:T(8,128)(2,1)}, u32[]{:S(2)}, u32[]{:S(2)}) collective-permute-start(bf16[8,64,256]{2,1,0:T(8,128)(2,1)} %get-tuple-element.152), channel_id=1, source_target_pairs={{0,8},{2,10},{4,12},{6,14},{8,16},{10,18},{12,20},{14,22},{16,24},... | collective-permute-start | bytes 786440 | tf_op jit(solution)/shard_map/ppermute | solution.py:236
  313.7 8.6 %collective-permute-start.32 = (bf16[8,64,256]{2,1,0:T(8,128)(2,1)}, bf16[8,64,256]{2,1,0:T(8,128)(2,1)}, u32[]{:S(2)}, u32[]{:S(2)}) collective-permute-start(bf16[8,64,256]{2,1,0:T(8,128)(2,1)} %get-tuple-element.151), channel_id=1, source_target_pairs={{30,22},{28,20},{26,18},{24,16},{22,14},{20,12},{18,10},{16,8},{14... | collective-permute-start | bytes 786440 | tf_op jit(solution)/shard_map/ppermute | solution.py:237
  326.2 3.8 %collective-permute-start.33 = (f32[16,256]{1,0:T(8,128)S(1)}, f32[16,256]{1,0:T(8,128)S(1)}, u32[]{:S(2)}, u32[]{:S(2)}) collective-permute-start(f32[16,256]{1,0:T(8,128)S(1)} %dynamic-slice_bitcast_fusion.4), channel_id=1, source_target_pairs={{0,1},{1,0},{2,3},{3,2},{4,5},{5,4},{6,7},{7,6},{8,9},{9,8},{10,11... | collective-permute-start | bytes 49160 | tf_op jit(solution)/shard_map/ppermute | solution.py:267
  (6 other events, 12.7 us)

commit v3 on v2

--- a/solution.py
+++ b/solution.py
@@ -10,8 +10,8 @@
 
 NFFT = 1024
 HALF = NFFT // 2
-PARTS = 4
 ROWS = 16
+SPREAD = 24
 
 wavenumber = 2.0
 height = 0.5
@@ -19,7 +19,7 @@
 
 def cos_of_turns(count):
     quarter = NFFT // 4
-    quadrant = (count + quarter // 2) // quarter
+    quadrant = (count + quarter // 2) >> (quarter.bit_length() - 1)
     angle = (count - quadrant * quarter).astype(jnp.float32) * (2.0 * math.pi / NFFT)
     square = angle * angle
     sine = 1.0 / math.factorial(9)
@@ -31,18 +31,17 @@
         1.0
         + square * (-1.0 / 6 + square * (1.0 / 120 + square * (-1.0 / 5040 + square * sine)))
     )
-    value = jnp.where(quadrant % 2 == 0, cosine, sine)
-    turned = quadrant % 4
-    return jnp.where((turned == 1) | (turned == 2), -value, value)
+    value = jnp.where(quadrant & 1 == 0, cosine, sine)
+    return jnp.where((quadrant + 1) & 2 == 0, value, -value)
 
 
 def fourier_table():
     row = lax.broadcasted_iota(jnp.int32, (2 * HALF, NFFT), 0)
     sample = lax.broadcasted_iota(jnp.int32, (2 * HALF, NFFT), 1)
-    turns = (row // 2 * sample + row % 2 * (NFFT // 4)) % NFFT
+    turns = ((row >> 1) * sample + (row & 1) * (NFFT // 4)) & (NFFT - 1)
     window = 0.5 - 0.5 * cos_of_turns(lax.broadcasted_iota(jnp.int32, (1, NFFT), 1))
-    value = cos_of_turns(turns) * window
-    return (value / math.sqrt(3.0 * NFFT / 8.0)).astype(jnp.bfloat16)
+    window = lax.optimization_barrier(window * (1.0 / math.sqrt(3.0 * NFFT / 8.0)))
+    return (cos_of_turns(turns) * window).astype(jnp.bfloat16)
 
 
 def distances(index, radius, azimuth, total_mics):
@@ -86,16 +85,19 @@
             table_ref[...], virtual[pl.ds(start, NFFT), :], preferred_element_type=jnp.float32
         )
         for half in range(halves):
-            spread[half, pl.ds(segment, columns, stride=ROWS), :] = product[
+            spread[half, pl.ds(segment, columns, stride=SPREAD), :] = product[
                 :, half * lanes : (half + 1) * lanes
             ]
 
     for half in range(halves):
         for pad in range(segments, ROWS):
-            spread[half, pl.ds(pad, columns, stride=ROWS), :] = jnp.zeros(
+            spread[half, pl.ds(pad, columns, stride=SPREAD), :] = jnp.zeros(
                 (columns, lanes), jnp.float32
             )
-        out_ref[0, :, half * lanes : (half + 1) * lanes] = spread[half].astype(jnp.bfloat16)
+        rows = spread[half].reshape(columns, SPREAD, lanes)[:, :ROWS]
+        out_ref[0, :, half * lanes : (half + 1) * lanes] = rows.reshape(
+            columns * ROWS, lanes
+        ).astype(jnp.bfloat16)
 
 
 def spectra_of(signal, edge, weight, table):
@@ -116,7 +118,7 @@
         out_shape=jax.ShapeDtypeStruct((blocks, 2 * HALF * ROWS, mics), jnp.bfloat16),
         scratch_shapes=[
             pltpu.VMEM((length, mics), jnp.bfloat16),
-            pltpu.VMEM((mics // lanes, tile * ROWS, lanes), jnp.float32),
+            pltpu.VMEM((mics // lanes, tile * SPREAD, lanes), jnp.float32),
         ],
         compiler_params=pltpu.CompilerParams(vmem_limit_bytes=50 << 20),
         name="welch",
@@ -215,27 +217,17 @@
     return kept.astype(jnp.float32) + got.astype(jnp.float32)
 
 
-def fold_line(state, stride, step):
-    x, right, left = state
+def fold_line(x, stride):
     length = x.shape[0]
     place = lax.axis_index("sector") // stride
-
-    def entry(i):
-        return lax.dynamic_index_in_dim(x, jnp.clip(i, 0, length - 1), 0, keepdims=False)
-
-    def joined(entry, got):
-        return entry if got is None else entry + got.astype(jnp.float32)
-
-    if step == length:
-        return joined(joined(entry(place), right), left)
-    send_right = joined(entry(length - step + place), right).astype(jnp.bfloat16)
-    send_left = joined(entry(place + step - length), left).astype(jnp.bfloat16)
-    movers = [i for i in range(length - 1) if i < step]
-    pairs = [(i * stride + j, (i + 1) * stride + j) for i in movers for j in range(stride)]
-    last = stride * length - 1
-    right = lax.ppermute(send_right, "sector", pairs)
-    left = lax.ppermute(send_left, "sector", [(last - a, last - b) for a, b in pairs])
-    return x, right, left
+    total = lax.dynamic_index_in_dim(x, place, 0, keepdims=False)
+    devices = stride * length
+    for shift in range(1, length):
+        target = (place + shift) % length
+        sent = lax.dynamic_index_in_dim(x, target, 0, keepdims=False).astype(jnp.bfloat16)
+        pairs = [(i, (i + shift * stride) % devices) for i in range(devices)]
+        total += lax.ppermute(sent, "sector", pairs).astype(jnp.float32)
+    return total
 
 
 def fold_stages(sectors):
@@ -244,17 +236,14 @@
     while stride < 4 and sectors // stride % 2 == 0:
         stages.append(functools.partial(fold_pair, bit=stride))
         stride *= 2
-    length = sectors // stride
-    for step in range(1, length):
-        if step == 1:
-            stages.append(lambda x: fold_line((x, None, None), stride, 1))
-        else:
-            stages.append(functools.partial(fold_line, stride=stride, step=step))
-    if length > 1:
-        final = functools.partial(fold_line, stride=stride, step=length)
-    else:
-        final = lambda x: x[0]
-    return stages, final
+    stages.append(functools.partial(fold_line, stride=stride))
+    return stages
+
+
+def bin_chunks(band):
+    if band % 8:
+        return [1] * band
+    return [band // 4] * 3 + [band // 8] * 2
 
 
 def add_over_blk(power):
@@ -280,8 +269,6 @@
     spectra = spectra_of(signal, edge, fraction[:, None, :], fourier_table())
 
     band = HALF // sectors
-    bins = band // PARTS
-    spectra = spectra.reshape(blocks, sectors, PARTS, bins, 2 * ROWS, mics)
     index = (sector * mics + lax.iota(jnp.int32, mics)[None, :] - offsets[:, None]) % total_mics
     phase = wavenumber * distances(index, radius, azimuth, total_mics)
     one = lax.optimization_barrier((jnp.cos(phase), jnp.sin(phase)))
@@ -299,21 +286,21 @@
         return total
 
     step = power_of(band)
-    stages, final = fold_stages(sectors)
-    states = [None] * PARTS
-    for tick in range(PARTS + len(stages)):
-        for part in range(PARTS):
+    stages = fold_stages(sectors)
+    chunks = bin_chunks(band)
+    states = [None] * len(chunks)
+    for tick in range(len(chunks) + len(stages)):
+        for part, bins in enumerate(chunks):
             stage = tick - part
             if stage == 0:
-                first = power_of(part * bins) if part else ()
-                states[part] = beams(spectra, one + step + first, part)
+                start = sum(chunks[:part])
+                first = power_of(start) if start else ()
+                shaped = spectra.reshape(blocks, sectors, band // bins, bins, 2 * ROWS, mics)
+                states[part] = beams(shaped, one + step + first, start // bins)
             elif 0 < stage <= len(stages):
                 states[part] = stages[stage - 1](states[part])
         states, spectra = lax.optimization_barrier((states, spectra))
-    powers = []
-    for state in states:
-        total = final(state)
-        powers.append(jnp.sum(total * total, 1))
+    powers = [jnp.sum(total * total, 1) for total in states]
     scale = 1.0 / (total_mics * blocks * segments * lax.axis_size("blk"))
     return add_over_blk(jnp.concatenate(powers, 0) * scale)
 

time: 332 us -> 284 us (0.86)
  starting transfers between devices: 73 us -> 30.7 us
  waiting for transfers between devices: 42.1 us -> 60 us
  other arithmetic: 47.7 us -> 32.9 us
  Pallas kernels: 150 us -> 143 us
    ppermute x24 -> x15, starting transfers between devices: 60 us -> 17.4 us  [fold_line(): total += lax.ppermute(sent, 'sector', pairs).astype(jnp.float32)]
    ppermute x24 -> x15, waiting for transfers between devices: 13.9 us -> 49.9 us  [fold_line(): total += lax.ppermute(sent, 'sector', pairs).astype(jnp.float32)]
    ppermute x8 -> x10, waiting for transfers between devices: 25.9 us -> 7.85 us  [fold_pair(): got = lax.ppermute(sent, 'sector', [(i, i ^ bit) for i in range(sectors)])]
    convert_element_type x9 -> x1, other arithmetic: 18 us -> 6.43 us  [fourier_table(): return (cos_of_turns(turns) * window).astype(jnp.bfloat16)]
    pallas_call x1, Pallas kernels: 51.9 us -> 43.2 us  [spectra_of(): pl.pallas_call(functools.partial(spectra_kernel, segments), grid=(blocks,...]
    unnamed x72 -> x48, local copies, waits for them, and re-layouts: 6.28 us -> 0.68 us
    reduce_sum x4 -> x5, other arithmetic: 3.87 us -> 0.23 us  [local(): powers = [jnp.sum(total * total, 1) for total in states]]
    pallas_call x4 -> x5, Pallas kernels: 97.7 us -> 100 us  [beams(): pl.pallas_call(beam_kernel, grid=(1,), in_specs=[pl.BlockSpec((blocks, gr...]
  transfers between devices with their start and end apart: 34 -> 27, of which waited for: 10 -> 13; matrix products, arithmetic and copies ran while one was open for 12% -> 9% of each run, Pallas kernels for 22% -> 27%
where the time goes in v3:
time: 284 us
  Pallas kernels  143 us (50%)
  waiting for transfers between devices  60 us (21%)
  other arithmetic  32.9 us (12%)
  starting transfers between devices  30.7 us (11%)
  local copies, waits for them, and re-layouts  16.3 us (6%)
    pallas_call x5, Pallas kernels, beams(): pl.pallas_call(beam_kernel, grid=(1,), in_specs=[pl.BlockSpec((blocks, gr...  100 us
    ppermute x15, waiting for transfers between devices, fold_line(): total += lax.ppermute(sent, 'sector', pairs).astype(jnp.float32)  49.9 us
    pallas_call x1, Pallas kernels, spectra_of(): pl.pallas_call(functools.partial(spectra_kernel, segments), grid=(blocks,...  43.2 us
    ppermute x15, starting transfers between devices, fold_line(): total += lax.ppermute(sent, 'sector', pairs).astype(jnp.float32)  17.4 us
    add x10, other arithmetic, fold_pair(): return kept.astype(jnp.float32) + got.astype(jnp.float32)  16.3 us
    ppermute x10, waiting for transfers between devices, fold_pair(): got = lax.ppermute(sent, 'sector', [(i, i ^ bit) for i in range(sectors)])  7.85 us
    squeeze x5, local copies, waits for them, and re-layouts, fold_pair(): lax.dynamic_index_in_dim(halves, 1 - mine, 1, keepdims=False)  7.39 us
    convert_element_type x1, other arithmetic, fourier_table(): return (cos_of_turns(turns) * window).astype(jnp.bfloat16)  6.43 us
  transfers between devices with their start and end apart: 27, of which 13 were waited for; matrix products, arithmetic and copies ran while one was open for 9% of the time, Pallas kernels for 27%

profile of v3, /device:TPU:0, one launch (start us, length us, event | category | flops | bytes accessed | tf_op | source)
XLA Modules:
  0.0 283.9 jit_solution(306265024717853990)
XLA Ops:
  0.0 1.0 slice.3
  1.0 5.5 %collective-permute-start = (bf16[2,1,8192]{2,1,0:T(2,128)(2,1)S(1)}, bf16[2,1,8192]{2,1,0:T(2,128)(2,1)S(1)}, u32[]{:S(2)}, u32[]{:S(2)}) collective-permute-start(bf16[2,1,8192]{2,1,0:T(2,128)(2,1)S(1)} %slice.3), channel_id=1, source_target_pairs={{0,30},{2,0},{4,2},{6,4},{8,6},{10,8},{12,10},{14,12},{16,14},{18,... | collective-permute-start | bytes 98312 | tf_op jit(solution)/shard_map/ppermute | solution.py:266
  6.5 0.7 cosine_multiply_fusion
  7.3 0.8 fusion.50
  8.1 2.3 fusion.20
  10.5 1.2 multiply_add_fusion
  11.8 6.4 %fusion.1.table_ref = bf16[1024,1024]{1,0:T(8,128)(2,1)S(1)} fusion(f32[1024]{0:T(1024)S(1)} %bitcast.158, s32[1024]{0:T(1024)S(1)} %get-tuple-element.114, s32[1024]{0:T(1024)S(1)} %get-tuple-element.113), kind=kLoop, calls=%fused_computation.2 | loop fusion | flops 40894464 | bytes 2109440 | tf_op jit(solution)/shard_map/convert_element_type | solution.py:44
  18.3 1.6 multiply_add_fusion.2
  20.0 43.2 %welch.1 = bf16[2,16384,256]{2,1,0:T(8,128)(2,1)} custom-call(bf16[2,256,8192]{2,1,0:T(8,128)(2,1)} %signal_ref.1, bf16[2,1,8192]{2,1,0:T(2,128)(2,1)S(1)} %collective-permute-done.edge_ref, f32[2,1,8192]{2,1,0:T(1,128)S(1)} %broadcast_in_dim.2.weight_ref, bf16[1024,1024]{1,0:T(8,128)(2,1)S(1)} %fusion.1.table_ref), custom_call_target="tpu_custom_call" | custom-call | tf_op jit(solution)/shard_map/welch/pallas_call | solution.py:108
  63.2 24.3 %beams.5 = bf16[16,8,2,32,256]{4,3,2,1,0:T(8,128)(2,1)} custom-call(bf16[2,16,4,8,32,256]{5,4,3,2,1,0:T(8,128)(2,1)} %bitcast.135, f32[2,256,256]{2,1,0:T(8,128)S(1)} %get-tuple-element.41.refs_1_, f32[2,256,256]{2,1,0:T(8,128)S(1)} %get-tuple-element.42.refs_2_, f32[2,256,256]{2,1,0:T(8,128)S(1)} %copy-done.12, f32[2,256,256]{2,1,0:T(8,128)S(1)} %copy-done.10), custom_call_target="tpu_custom_call" | custom-call | flops 17179869184 | bytes 8388608 | tf_op jit(solution)/shard_map/beams/pallas_call | solution.py:185
  87.5 3.3 %dynamic-slice_bitcast_fusion.2 = bf16[8,8,64,256]{3,2,1,0:T(8,128)(2,1)} fusion(bf16[8,2,8,64,256]{4,3,2,1,0:T(8,128)(2,1)} %bitcast.154, s32[]{:T(128)S(6)} %select_n.206), kind=kLoop, calls=%fused_computation.32 | loop fusion | bytes 4194308 | tf_op jit(solution)/shard_map/jit(dynamic_index_in_dim)/squeeze | solution.py:214
  90.9 24.5 %beams.6 = bf16[16,8,2,32,256]{4,3,2,1,0:T(8,128)(2,1)} custom-call(bf16[2,16,4,8,32,256]{5,4,3,2,1,0:T(8,128)(2,1)} %bitcast.136, f32[2,256,256]{2,1,0:T(8,128)S(1)} %get-tuple-element.41.refs_1_, f32[2,256,256]{2,1,0:T(8,128)S(1)} %get-tuple-element.42.refs_2_, f32[2,256,256]{2,1,0:T(8,128)S(1)} %copy-done.13, f32[2,256,256]{2,1,0:T(8,128)S(1)} %copy-done.11, ...), custom_call_target="tpu_custom_call" | custom-call | flops 17179869184 | bytes 8388608 | tf_op jit(solution)/shard_map/beams/pallas_call | solution.py:185
  115.4 4.6 %convert_add_fusion.2 = f32[8,8,64,256]{3,2,1,0:T(8,128)} fusion(bf16[8,8,64,256]{3,2,1,0:T(8,128)(2,1)} %collective-permute-done.1, bf16[8,2,8,64,256]{4,3,2,1,0:T(8,128)(2,1)S(1)} %bitcast.155, s32[]{:T(128)S(6)} %select_n.205), kind=kLoop, calls=%fused_computation.5 | loop fusion | flops 3145728 | bytes 8388612 | tf_op jit(solution)/shard_map/add | solution.py:217
  120.0 1.5 dynamic-slice_bitcast_fusion.1
  121.5 0.5 collective-permute-start.3
  122.0 1.7 fusion.9
  123.8 24.5 %beams.7 = bf16[16,8,2,32,256]{4,3,2,1,0:T(8,128)(2,1)} custom-call(bf16[2,16,4,8,32,256]{5,4,3,2,1,0:T(8,128)(2,1)} %bitcast.137, f32[2,256,256]{2,1,0:T(8,128)S(1)} %get-tuple-element.41.refs_1_, f32[2,256,256]{2,1,0:T(8,128)S(1)} %get-tuple-element.42.refs_2_, f32[2,256,256]{2,1,0:T(8,128)S(1)} %copy-done.13, f32[2,256,256]{2,1,0:T(8,128)S(1)} %copy-done.11, ...), custom_call_target="tpu_custom_call" | custom-call | flops 17179869184 | bytes 8388608 | tf_op jit(solution)/shard_map/beams/pallas_call | solution.py:185
  148.3 0.6 collective-permute-done.2
  148.9 1.7 bitcast_add_fusion.2
  150.6 0.6 copy-done.21
  151.2 4.7 %convert_add_fusion.1 = f32[8,8,64,256]{3,2,1,0:T(8,128)} fusion(bf16[8,8,64,256]{3,2,1,0:T(8,128)(2,1)} %collective-permute-done.3, bf16[8,2,8,64,256]{4,3,2,1,0:T(8,128)(2,1)S(1)} %bitcast.153, s32[]{:T(128)S(6)} %select_n.205), kind=kLoop, calls=%fused_computation.4 | loop fusion | flops 3145728 | bytes 8388612 | tf_op jit(solution)/shard_map/add | solution.py:217
  155.9 1.4 dynamic-slice_bitcast_fusion
  157.4 1.5 fusion.22
  158.9 1.3 collective-permute-start.6
  160.2 1.0 collective-permute-start.4
  161.2 1.7 fusion.10
  163.0 1.8 collective-permute-start.7
  164.8 13.5 %beams.8 = bf16[16,4,2,32,256]{4,3,2,1,0:T(8,128)(2,1)S(1)} custom-call(bf16[2,16,8,4,32,256]{5,4,3,2,1,0:T(8,128)(2,1)} %bitcast.138, f32[2,256,256]{2,1,0:T(8,128)S(1)} %get-tuple-element.41.refs_1_, f32[2,256,256]{2,1,0:T(8,128)S(1)} %get-tuple-element.42.refs_2_, f32[2,256,256]{2,1,0:T(8,128)S(1)} %copy-done.13, f32[2,256,256]{2,1,0:T(8,128)S(1)} %copy-done.11, ...), custom_call_target="tpu_custom_call" | custom-call | flops 8589934592 | bytes 4194304 | tf_op jit(solution)/shard_map/beams/pallas_call | solution.py:185
  178.3 4.7 %collective-permute-done.5 = bf16[8,64,256]{2,1,0:T(8,128)(2,1)S(1)} collective-permute-done((bf16[8,64,256]{2,1,0:T(8,128)(2,1)S(1)}, bf16[8,64,256]{2,1,0:T(8,128)(2,1)S(1)}, u32[]{:S(2)}, u32[]{:S(2)}) %collective-permute-start.5) | collective-permute-done | bytes 262176 | tf_op jit(solution)/shard_map/ppermute | solution.py:229
  183.0 1.2 fusion.19
  184.2 3.8 %collective-permute-done.7 = bf16[4,8,64,256]{3,2,1,0:T(8,128)(2,1)S(1)} collective-permute-done((bf16[4,8,64,256]{3,2,1,0:T(8,128)(2,1)S(1)}, bf16[4,8,64,256]{3,2,1,0:T(8,128)(2,1)S(1)}, u32[]{:S(2)}, u32[]{:S(2)}) %collective-permute-start.7) | collective-permute-done | bytes 1048608 | tf_op jit(solution)/shard_map/ppermute | solution.py:216
  188.0 0.4 bitcast_add_fusion.1
  188.4 2.4 convert_add_fusion
  190.9 2.7 collective-permute-start.11
  193.6 0.8 collective-permute-start.10
  194.5 1.2 collective-permute-start.9
  195.7 1.2 fusion.11
  196.8 1.7 collective-permute-start.12
  198.5 1.1 dynamic-slice_bitcast_fusion.4
  199.6 13.4 %beams.9 = bf16[16,4,2,32,256]{4,3,2,1,0:T(8,128)(2,1)S(1)} custom-call(bf16[2,16,8,4,32,256]{5,4,3,2,1,0:T(8,128)(2,1)} %bitcast.139, f32[2,256,256]{2,1,0:T(8,128)S(1)} %get-tuple-element.41.refs_1_, f32[2,256,256]{2,1,0:T(8,128)S(1)} %get-tuple-element.42.refs_2_, f32[2,256,256]{2,1,0:T(8,128)S(1)} %copy-done.13, f32[2,256,256]{2,1,0:T(8,128)S(1)} %copy-done.11, ...), custom_call_target="tpu_custom_call" | custom-call | flops 8589934592 | bytes 4194304 | tf_op jit(solution)/shard_map/beams/pallas_call | solution.py:185
  213.1 3.0 %collective-permute-done.10 = bf16[8,64,256]{2,1,0:T(8,128)(2,1)S(1)} collective-permute-done((bf16[8,64,256]{2,1,0:T(8,128)(2,1)S(1)}, bf16[8,64,256]{2,1,0:T(8,128)(2,1)S(1)}, u32[]{:S(2)}, u32[]{:S(2)}) %collective-permute-start.10) | collective-permute-done | bytes 262176 | tf_op jit(solution)/shard_map/ppermute | solution.py:229
  216.1 1.1 fusion.17
  217.1 3.3 %collective-permute-done.12 = bf16[4,8,64,256]{3,2,1,0:T(8,128)(2,1)} collective-permute-done((bf16[4,8,64,256]{3,2,1,0:T(8,128)(2,1)}, bf16[4,8,64,256]{3,2,1,0:T(8,128)(2,1)}, u32[]{:S(2)}, u32[]{:S(2)}) %collective-permute-start.12) | collective-permute-done | bytes 1048608 | tf_op jit(solution)/shard_map/ppermute | solution.py:216
  220.4 1.5 bitcast_add_fusion
  221.9 0.4 convert_add_fusion.4
  222.6 1.5 collective-permute-start.17
  224.2 2.3 collective-permute-start.16
  226.5 0.7 collective-permute-start.15
  227.5 5.8 %collective-permute-done.16 = bf16[8,64,256]{2,1,0:T(8,128)(2,1)S(1)} collective-permute-done((bf16[8,64,256]{2,1,0:T(8,128)(2,1)S(1)}, bf16[8,64,256]{2,1,0:T(8,128)(2,1)S(1)}, u32[]{:S(2)}, u32[]{:S(2)}) %collective-permute-start.16) | collective-permute-done | bytes 262176 | tf_op jit(solution)/shard_map/ppermute | solution.py:229
  233.3 17.2 %collective-permute-done.15 = bf16[8,64,256]{2,1,0:T(8,128)(2,1)S(1)} collective-permute-done((bf16[8,64,256]{2,1,0:T(8,128)(2,1)S(1)}, bf16[8,64,256]{2,1,0:T(8,128)(2,1)S(1)}, u32[]{:S(2)}, u32[]{:S(2)}) %collective-permute-start.15) | collective-permute-done | bytes 262176 | tf_op jit(solution)/shard_map/ppermute | solution.py:229
  250.8 0.4 convert_add_fusion.3
  251.2 0.4 collective-permute-start.22
  251.7 1.6 collective-permute-start.20
  253.4 1.9 collective-permute-start.19
  255.3 2.0 collective-permute-done.21
  257.3 7.0 %collective-permute-done.20 = bf16[4,64,256]{2,1,0:T(8,128)(2,1)S(1)} collective-permute-done((bf16[4,64,256]{2,1,0:T(8,128)(2,1)S(1)}, bf16[4,64,256]{2,1,0:T(8,128)(2,1)S(1)}, u32[]{:S(2)}, u32[]{:S(2)}) %collective-permute-start.20) | collective-permute-done | bytes 131104 | tf_op jit(solution)/shard_map/ppermute | solution.py:229
  264.6 0.7 fusion.38
  265.4 1.4 collective-permute-start.24
  266.8 2.0 collective-permute-start.23
  268.8 2.2 collective-permute-done.25
  271.0 8.1 %collective-permute-done.24 = bf16[4,64,256]{2,1,0:T(8,128)(2,1)S(1)} collective-permute-done((bf16[4,64,256]{2,1,0:T(8,128)(2,1)S(1)}, bf16[4,64,256]{2,1,0:T(8,128)(2,1)S(1)}, u32[]{:S(2)}, u32[]{:S(2)}) %collective-permute-start.24) | collective-permute-done | bytes 131104 | tf_op jit(solution)/shard_map/ppermute | solution.py:229
  279.5 1.6 collective-permute-start.26
  281.1 2.2 collective-permute-done.26
  283.3 0.6 bitcast_add_fusion.10
  (95 shorter events, 2.4 us)
Async XLA Ops:
  1.0 19.0 %collective-permute-start = (bf16[2,1,8192]{2,1,0:T(2,128)(2,1)S(1)}, bf16[2,1,8192]{2,1,0:T(2,128)(2,1)S(1)}, u32[]{:S(2)}, u32[]{:S(2)}) collective-permute-start(bf16[2,1,8192]{2,1,0:T(2,128)(2,1)S(1)} %slice.3), channel_id=1, source_target_pairs={{0,30},{2,0},{4,2},{6,4},{8,6},{10,8},{12,10},{14,12},{16,14},{18,... | collective-permute-start | bytes 98312 | tf_op jit(solution)/shard_map/ppermute | solution.py:266
  11.8 6.5 %copy-start = (f32[2,256,256]{2,1,0:T(8,128)}, f32[2,256,256]{2,1,0:T(8,128)S(1)}, u32[]{:S(2)}) copy-start(f32[2,256,256]{2,1,0:T(8,128)S(1)} %get-tuple-element.80.refs_5_) | copy-start | bytes 1572868
  11.8 6.5 %copy-start.2 = (f32[2,256,256]{2,1,0:T(8,128)}, f32[2,256,256]{2,1,0:T(8,128)S(1)}, u32[]{:S(2)}) copy-start(f32[2,256,256]{2,1,0:T(8,128)S(1)} %get-tuple-element.81.refs_6_) | copy-start | bytes 1572868
  11.8 6.5 %copy-start.4 = (f32[2,256,256]{2,1,0:T(8,128)}, f32[2,256,256]{2,1,0:T(8,128)S(1)}, u32[]{:S(2)}) copy-start(f32[2,256,256]{2,1,0:T(8,128)S(1)} %get-tuple-element.82.refs_6_) | copy-start | bytes 1572868
  11.8 6.5 %copy-start.6 = (f32[2,256,256]{2,1,0:T(8,128)}, f32[2,256,256]{2,1,0:T(8,128)S(1)}, u32[]{:S(2)}) copy-start(f32[2,256,256]{2,1,0:T(8,128)S(1)} %get-tuple-element.83.refs_5_) | copy-start | bytes 1572868
  11.8 8.1 %copy-start.23 = (f32[2,8192]{1,0:T(2,128)S(1)}, f32[2,8192]{1,0:T(2,128)}, u32[]{:S(2)}) copy-start(f32[2,8192]{1,0:T(2,128)} %param.7) | copy-start | bytes 196612
  19.9 43.2 %copy-start.10 = (f32[2,256,256]{2,1,0:T(8,128)S(1)}, f32[2,256,256]{2,1,0:T(8,128)}, u32[]{:S(2)}) copy-start(f32[2,256,256]{2,1,0:T(8,128)} %get-tuple-element.102.refs_4_) | copy-start | bytes 1572868
  20.0 43.2 %copy-start.12 = (f32[2,256,256]{2,1,0:T(8,128)S(1)}, f32[2,256,256]{2,1,0:T(8,128)}, u32[]{:S(2)}) copy-start(f32[2,256,256]{2,1,0:T(8,128)} %get-tuple-element.103.refs_3_) | copy-start | bytes 1572868
  87.5 3.3 %copy-start.5 = (f32[2,256,256]{2,1,0:T(8,128)S(1)}, f32[2,256,256]{2,1,0:T(8,128)}, u32[]{:S(2)}) copy-start(f32[2,256,256]{2,1,0:T(8,128)} %copy-done.4) | copy-start | bytes 1572868
  87.5 3.3 %copy-start.7 = (f32[2,256,256]{2,1,0:T(8,128)S(1)}, f32[2,256,256]{2,1,0:T(8,128)}, u32[]{:S(2)}) copy-start(f32[2,256,256]{2,1,0:T(8,128)} %copy-done.6) | copy-start | bytes 1572868
  87.5 3.3 %copy-start.11 = (f32[2,256,256]{2,1,0:T(8,128)S(1)}, f32[2,256,256]{2,1,0:T(8,128)}, u32[]{:S(2)}) copy-start(f32[2,256,256]{2,1,0:T(8,128)} %get-tuple-element.102.refs_4_) | copy-start | bytes 1572868
  87.5 3.3 %copy-start.13 = (f32[2,256,256]{2,1,0:T(8,128)S(1)}, f32[2,256,256]{2,1,0:T(8,128)}, u32[]{:S(2)}) copy-start(f32[2,256,256]{2,1,0:T(8,128)} %get-tuple-element.103.refs_3_) | copy-start | bytes 1572868
  90.8 24.6 %collective-permute-start.1 = (bf16[8,8,64,256]{3,2,1,0:T(8,128)(2,1)}, bf16[8,8,64,256]{3,2,1,0:T(8,128)(2,1)}, u32[]{:S(2)}, u32[]{:S(2)}) collective-permute-start(bf16[8,8,64,256]{3,2,1,0:T(8,128)(2,1)} %dynamic-slice_bitcast_fusion.2), channel_id=1, source_target_pairs={{0,2},{2,0},{4,6},{6,4},{8,10},{10,8},{12,14},{14,12},{16,18},{18,... | collective-permute-start | bytes 6291464 | tf_op jit(solution)/shard_map/ppermute | solution.py:216
  90.8 24.5 %copy-start.22 = (bf16[16,8,2,32,256]{4,3,2,1,0:T(8,128)(2,1)S(1)}, bf16[16,8,2,32,256]{4,3,2,1,0:T(8,128)(2,1)}, u32[]{:S(2)}) copy-start(bf16[16,8,2,32,256]{4,3,2,1,0:T(8,128)(2,1)} %beams.5) | copy-start | bytes 12582916
  115.4 4.7 %copy-start.20 = (bf16[16,8,2,32,256]{4,3,2,1,0:T(8,128)(2,1)S(1)}, bf16[16,8,2,32,256]{4,3,2,1,0:T(8,128)(2,1)}, u32[]{:S(2)}) copy-start(bf16[16,8,2,32,256]{4,3,2,1,0:T(8,128)(2,1)} %beams.6) | copy-start | bytes 12582916
  120.0 3.8 %copy-start.1 = (f32[2,256,256]{2,1,0:T(8,128)S(1)}, f32[2,256,256]{2,1,0:T(8,128)}, u32[]{:S(2)}) copy-start(f32[2,256,256]{2,1,0:T(8,128)} %copy-done) | copy-start | bytes 1572868
  120.0 3.8 %copy-start.3 = (f32[2,256,256]{2,1,0:T(8,128)S(1)}, f32[2,256,256]{2,1,0:T(8,128)}, u32[]{:S(2)}) copy-start(f32[2,256,256]{2,1,0:T(8,128)} %copy-done.2) | copy-start | bytes 1572868
  121.5 29.1 %collective-permute-start.3 = (bf16[8,8,64,256]{3,2,1,0:T(8,128)(2,1)}, bf16[8,8,64,256]{3,2,1,0:T(8,128)(2,1)}, u32[]{:S(2)}, u32[]{:S(2)}) collective-permute-start(bf16[8,8,64,256]{3,2,1,0:T(8,128)(2,1)} %dynamic-slice_bitcast_fusion.1), channel_id=1, source_target_pairs={{0,2},{2,0},{4,6},{6,4},{8,10},{10,8},{12,14},{14,12},{16,18},{18,... | collective-permute-start | bytes 6291464 | tf_op jit(solution)/shard_map/ppermute | solution.py:216
  123.7 25.1 %collective-permute-start.2 = (bf16[4,8,64,256]{3,2,1,0:T(8,128)(2,1)S(1)}, bf16[4,8,64,256]{3,2,1,0:T(8,128)(2,1)S(1)}, u32[]{:S(2)}, u32[]{:S(2)}) collective-permute-start(bf16[4,8,64,256]{3,2,1,0:T(8,128)(2,1)S(1)} %fusion.9), channel_id=1, source_target_pairs={{0,4},{2,6},{4,0},{6,2},{8,12},{10,14},{12,8},{14,10},{16,20},{18,... | collective-permute-start | bytes 3145736 | tf_op jit(solution)/shard_map/ppermute | solution.py:216
  123.8 25.1 %copy-start.17 = (f32[8,8,64,256]{3,2,1,0:T(8,128)S(1)}, f32[8,8,64,256]{3,2,1,0:T(8,128)}, u32[]{:S(2)}) copy-start(f32[8,8,64,256]{3,2,1,0:T(8,128)} %convert_add_fusion.2) | copy-start | bytes 12582916
  148.3 2.9 %copy-start.21 = (bf16[16,8,2,32,256]{4,3,2,1,0:T(8,128)(2,1)S(1)}, bf16[16,8,2,32,256]{4,3,2,1,0:T(8,128)(2,1)}, u32[]{:S(2)}) copy-start(bf16[16,8,2,32,256]{4,3,2,1,0:T(8,128)(2,1)} %beams.6) | copy-start | bytes 12582916
  150.6 5.3 %copy-start.18 = (bf16[16,8,2,32,256]{4,3,2,1,0:T(8,128)(2,1)S(1)}, bf16[16,8,2,32,256]{4,3,2,1,0:T(8,128)(2,1)}, u32[]{:S(2)}) copy-start(bf16[16,8,2,32,256]{4,3,2,1,0:T(8,128)(2,1)} %beams.7) | copy-start | bytes 12582916
  155.9 8.9 %copy-start.14 = (f32[2,256,256]{2,1,0:T(8,128)S(1)}, f32[2,256,256]{2,1,0:T(8,128)}, u32[]{:S(2)}) copy-start(f32[2,256,256]{2,1,0:T(8,128)} %get-tuple-element.90.refs_6_) | copy-start | bytes 1572868
  155.9 8.9 %copy-start.15 = (f32[2,256,256]{2,1,0:T(8,128)S(1)}, f32[2,256,256]{2,1,0:T(8,128)}, u32[]{:S(2)}) copy-start(f32[2,256,256]{2,1,0:T(8,128)} %get-tuple-element.91.refs_5_) | copy-start | bytes 1572868
  157.3 31.1 %collective-permute-start.8 = (bf16[8,8,64,256]{3,2,1,0:T(8,128)(2,1)}, bf16[8,8,64,256]{3,2,1,0:T(8,128)(2,1)}, u32[]{:S(2)}, u32[]{:S(2)}) collective-permute-start(bf16[8,8,64,256]{3,2,1,0:T(8,128)(2,1)} %dynamic-slice_bitcast_fusion), channel_id=1, source_target_pairs={{0,2},{2,0},{4,6},{6,4},{8,10},{10,8},{12,14},{14,12},{16,18},{18,... | collective-permute-start | bytes 6291464 | tf_op jit(solution)/shard_map/ppermute | solution.py:216
  158.9 19.4 %collective-permute-start.6 = (bf16[8,64,256]{2,1,0:T(8,128)(2,1)S(1)}, bf16[8,64,256]{2,1,0:T(8,128)(2,1)S(1)}, u32[]{:S(2)}, u32[]{:S(2)}) collective-permute-start(bf16[8,64,256]{2,1,0:T(8,128)(2,1)S(1)} %get-tuple-element.93), channel_id=1, source_target_pairs={{0,24},{2,26},{4,28},{6,30},{8,0},{10,2},{12,4},{14,6},{16,8},{18,... | collective-permute-start | bytes 786440 | tf_op jit(solution)/shard_map/ppermute | solution.py:229
  160.2 22.8 %collective-permute-start.5 = (bf16[8,64,256]{2,1,0:T(8,128)(2,1)S(1)}, bf16[8,64,256]{2,1,0:T(8,128)(2,1)S(1)}, u32[]{:S(2)}, u32[]{:S(2)}) collective-permute-start(bf16[8,64,256]{2,1,0:T(8,128)(2,1)S(1)} %get-tuple-element.94), channel_id=1, source_target_pairs={{0,16},{2,18},{4,20},{6,22},{8,24},{10,26},{12,28},{14,30},{16,0},... | collective-permute-start | bytes 786440 | tf_op jit(solution)/shard_map/ppermute | solution.py:229
  160.2 22.8 %collective-permute-start.4 = (bf16[8,64,256]{2,1,0:T(8,128)(2,1)S(1)}, bf16[8,64,256]{2,1,0:T(8,128)(2,1)S(1)}, u32[]{:S(2)}, u32[]{:S(2)}) collective-permute-start(bf16[8,64,256]{2,1,0:T(8,128)(2,1)S(1)} %get-tuple-element.92), channel_id=1, source_target_pairs={{0,8},{2,10},{4,12},{6,14},{8,16},{10,18},{12,20},{14,22},{16,24},... | collective-permute-start | bytes 786440 | tf_op jit(solution)/shard_map/ppermute | solution.py:229
  163.0 25.0 %collective-permute-start.7 = (bf16[4,8,64,256]{3,2,1,0:T(8,128)(2,1)S(1)}, bf16[4,8,64,256]{3,2,1,0:T(8,128)(2,1)S(1)}, u32[]{:S(2)}, u32[]{:S(2)}) collective-permute-start(bf16[4,8,64,256]{3,2,1,0:T(8,128)(2,1)S(1)} %fusion.10), channel_id=1, source_target_pairs={{0,4},{2,6},{4,0},{6,2},{8,12},{10,14},{12,8},{14,10},{16,20},{18,... | collective-permute-start | bytes 3145736 | tf_op jit(solution)/shard_map/ppermute | solution.py:216
  164.8 23.3 %copy-start.16 = (f32[8,8,64,256]{3,2,1,0:T(8,128)S(1)}, f32[8,8,64,256]{3,2,1,0:T(8,128)}, u32[]{:S(2)}) copy-start(f32[8,8,64,256]{3,2,1,0:T(8,128)} %convert_add_fusion.1) | copy-start | bytes 12582916
  178.3 10.1 %copy-start.19 = (bf16[16,8,2,32,256]{4,3,2,1,0:T(8,128)(2,1)S(1)}, bf16[16,8,2,32,256]{4,3,2,1,0:T(8,128)(2,1)}, u32[]{:S(2)}) copy-start(bf16[16,8,2,32,256]{4,3,2,1,0:T(8,128)(2,1)} %beams.7) | copy-start | bytes 12582916
  190.8 8.8 %copy-start.8 = (f32[2,256,256]{2,1,0:T(8,128)S(1)}, f32[2,256,256]{2,1,0:T(8,128)}, u32[]{:S(2)}) copy-start(f32[2,256,256]{2,1,0:T(8,128)} %get-tuple-element.77.refs_6_) | copy-start | bytes 1572868
  190.8 8.8 %copy-start.9 = (f32[2,256,256]{2,1,0:T(8,128)S(1)}, f32[2,256,256]{2,1,0:T(8,128)}, u32[]{:S(2)}) copy-start(f32[2,256,256]{2,1,0:T(8,128)} %get-tuple-element.101.refs_5_) | copy-start | bytes 1572868
  190.9 22.1 %collective-permute-start.11 = (bf16[8,64,256]{2,1,0:T(8,128)(2,1)S(1)}, bf16[8,64,256]{2,1,0:T(8,128)(2,1)S(1)}, u32[]{:S(2)}, u32[]{:S(2)}) collective-permute-start(bf16[8,64,256]{2,1,0:T(8,128)(2,1)S(1)} %get-tuple-element.88), channel_id=1, source_target_pairs={{0,24},{2,26},{4,28},{6,30},{8,0},{10,2},{12,4},{14,6},{16,8},{18,... | collective-permute-start | bytes 786440 | tf_op jit(solution)/shard_map/ppermute | solution.py:229
  193.6 22.4 %collective-permute-start.10 = (bf16[8,64,256]{2,1,0:T(8,128)(2,1)S(1)}, bf16[8,64,256]{2,1,0:T(8,128)(2,1)S(1)}, u32[]{:S(2)}, u32[]{:S(2)}) collective-permute-start(bf16[8,64,256]{2,1,0:T(8,128)(2,1)S(1)} %get-tuple-element.89), channel_id=1, source_target_pairs={{0,16},{2,18},{4,20},{6,22},{8,24},{10,26},{12,28},{14,30},{16,0},... | collective-permute-start | bytes 786440 | tf_op jit(solution)/shard_map/ppermute | solution.py:229
  194.5 21.6 %collective-permute-start.9 = (bf16[8,64,256]{2,1,0:T(8,128)(2,1)S(1)}, bf16[8,64,256]{2,1,0:T(8,128)(2,1)}, u32[]{:S(2)}, u32[]{:S(2)}) collective-permute-start(bf16[8,64,256]{2,1,0:T(8,128)(2,1)S(1)} %get-tuple-element.87), channel_id=1, source_target_pairs={{0,8},{2,10},{4,12},{6,14},{8,16},{10,18},{12,20},{14,22},{16,24},... | collective-permute-start | bytes 786440 | tf_op jit(solution)/shard_map/ppermute | solution.py:229
  196.8 23.6 %collective-permute-start.12 = (bf16[4,8,64,256]{3,2,1,0:T(8,128)(2,1)}, bf16[4,8,64,256]{3,2,1,0:T(8,128)(2,1)}, u32[]{:S(2)}, u32[]{:S(2)}) collective-permute-start(bf16[4,8,64,256]{3,2,1,0:T(8,128)(2,1)} %fusion.11), channel_id=1, source_target_pairs={{0,4},{2,6},{4,0},{6,2},{8,12},{10,14},{12,8},{14,10},{16,20},{18,... | collective-permute-start | bytes 3145736 | tf_op jit(solution)/shard_map/ppermute | solution.py:216
  199.6 22.3 %collective-permute-start.13 = (bf16[8,4,64,256]{3,2,1,0:T(8,128)(2,1)}, bf16[8,4,64,256]{3,2,1,0:T(8,128)(2,1)S(1)}, u32[]{:S(2)}, u32[]{:S(2)}) collective-permute-start(bf16[8,4,64,256]{3,2,1,0:T(8,128)(2,1)} %dynamic-slice_bitcast_fusion.4), channel_id=1, source_target_pairs={{0,2},{2,0},{4,6},{6,4},{8,10},{10,8},{12,14},{14,12},{16,18},{18,... | collective-permute-start | bytes 3145736 | tf_op jit(solution)/shard_map/ppermute | solution.py:216
  222.4 28.4 %collective-permute-start.18 = (bf16[8,4,64,256]{3,2,1,0:T(8,128)(2,1)S(1)}, bf16[8,4,64,256]{3,2,1,0:T(8,128)(2,1)S(1)}, u32[]{:S(2)}, u32[]{:S(2)}) collective-permute-start(bf16[8,4,64,256]{3,2,1,0:T(8,128)(2,1)S(1)} %dynamic-slice_bitcast_fusion.3), channel_id=1, source_target_pairs={{0,2},{2,0},{4,6},{6,4},{8,10},{10,8},{12,14},{14,12},{16,18},{18,... | collective-permute-start | bytes 3145736 | tf_op jit(solution)/shard_map/ppermute | solution.py:216
  222.6 28.1 %collective-permute-start.17 = (bf16[4,4,64,256]{3,2,1,0:T(8,128)(2,1)S(1)}, bf16[4,4,64,256]{3,2,1,0:T(8,128)(2,1)S(1)}, u32[]{:S(2)}, u32[]{:S(2)}) collective-permute-start(bf16[4,4,64,256]{3,2,1,0:T(8,128)(2,1)S(1)} %fusion.12), channel_id=1, source_target_pairs={{0,4},{2,6},{4,0},{6,2},{8,12},{10,14},{12,8},{14,10},{16,20},{18,... | collective-permute-start | bytes 1572872 | tf_op jit(solution)/shard_map/ppermute | solution.py:216
  224.2 9.1 %collective-permute-start.16 = (bf16[8,64,256]{2,1,0:T(8,128)(2,1)S(1)}, bf16[8,64,256]{2,1,0:T(8,128)(2,1)S(1)}, u32[]{:S(2)}, u32[]{:S(2)}) collective-permute-start(bf16[8,64,256]{2,1,0:T(8,128)(2,1)S(1)} %get-tuple-element.85), channel_id=1, source_target_pairs={{0,24},{2,26},{4,28},{6,30},{8,0},{10,2},{12,4},{14,6},{16,8},{18,... | collective-permute-start | bytes 786440 | tf_op jit(solution)/shard_map/ppermute | solution.py:229
  226.5 24.0 %collective-permute-start.15 = (bf16[8,64,256]{2,1,0:T(8,128)(2,1)S(1)}, bf16[8,64,256]{2,1,0:T(8,128)(2,1)S(1)}, u32[]{:S(2)}, u32[]{:S(2)}) collective-permute-start(bf16[8,64,256]{2,1,0:T(8,128)(2,1)S(1)} %get-tuple-element.86), channel_id=1, source_target_pairs={{0,16},{2,18},{4,20},{6,22},{8,24},{10,26},{12,28},{14,30},{16,0},... | collective-permute-start | bytes 786440 | tf_op jit(solution)/shard_map/ppermute | solution.py:229
  227.2 23.2 %collective-permute-start.14 = (bf16[8,64,256]{2,1,0:T(8,128)(2,1)S(1)}, bf16[8,64,256]{2,1,0:T(8,128)(2,1)S(1)}, u32[]{:S(2)}, u32[]{:S(2)}) collective-permute-start(bf16[8,64,256]{2,1,0:T(8,128)(2,1)S(1)} %get-tuple-element.84), channel_id=1, source_target_pairs={{0,8},{2,10},{4,12},{6,14},{8,16},{10,18},{12,20},{14,22},{16,24},... | collective-permute-start | bytes 786440 | tf_op jit(solution)/shard_map/ppermute | solution.py:229
  251.2 13.3 %collective-permute-start.22 = (bf16[4,4,64,256]{3,2,1,0:T(8,128)(2,1)S(1)}, bf16[4,4,64,256]{3,2,1,0:T(8,128)(2,1)S(1)}, u32[]{:S(2)}, u32[]{:S(2)}) collective-permute-start(bf16[4,4,64,256]{3,2,1,0:T(8,128)(2,1)S(1)} %fusion.13), channel_id=1, source_target_pairs={{0,4},{2,6},{4,0},{6,2},{8,12},{10,14},{12,8},{14,10},{16,20},{18,... | collective-permute-start | bytes 1572872 | tf_op jit(solution)/shard_map/ppermute | solution.py:216
  251.7 5.6 %collective-permute-start.21 = (bf16[4,64,256]{2,1,0:T(8,128)(2,1)S(1)}, bf16[4,64,256]{2,1,0:T(8,128)(2,1)S(1)}, u32[]{:S(2)}, u32[]{:S(2)}) collective-permute-start(bf16[4,64,256]{2,1,0:T(8,128)(2,1)S(1)} %get-tuple-element.99), channel_id=1, source_target_pairs={{0,24},{2,26},{4,28},{6,30},{8,0},{10,2},{12,4},{14,6},{16,8},{18,... | collective-permute-start | bytes 393224 | tf_op jit(solution)/shard_map/ppermute | solution.py:229
  251.7 12.5 %collective-permute-start.20 = (bf16[4,64,256]{2,1,0:T(8,128)(2,1)S(1)}, bf16[4,64,256]{2,1,0:T(8,128)(2,1)S(1)}, u32[]{:S(2)}, u32[]{:S(2)}) collective-permute-start(bf16[4,64,256]{2,1,0:T(8,128)(2,1)S(1)} %get-tuple-element.100), channel_id=1, source_target_pairs={{0,16},{2,18},{4,20},{6,22},{8,24},{10,26},{12,28},{14,30},{16,0},... | collective-permute-start | bytes 393224 | tf_op jit(solution)/shard_map/ppermute | solution.py:229
  253.4 10.9 %collective-permute-start.19 = (bf16[4,64,256]{2,1,0:T(8,128)(2,1)S(1)}, bf16[4,64,256]{2,1,0:T(8,128)(2,1)S(1)}, u32[]{:S(2)}, u32[]{:S(2)}) collective-permute-start(bf16[4,64,256]{2,1,0:T(8,128)(2,1)S(1)} %get-tuple-element.98), channel_id=1, source_target_pairs={{0,8},{2,10},{4,12},{6,14},{8,16},{10,18},{12,20},{14,22},{16,24},... | collective-permute-start | bytes 393224 | tf_op jit(solution)/shard_map/ppermute | solution.py:229
  265.4 5.6 %collective-permute-start.25 = (bf16[4,64,256]{2,1,0:T(8,128)(2,1)}, bf16[4,64,256]{2,1,0:T(8,128)(2,1)S(1)}, u32[]{:S(2)}, u32[]{:S(2)}) collective-permute-start(bf16[4,64,256]{2,1,0:T(8,128)(2,1)} %get-tuple-element.96), channel_id=1, source_target_pairs={{0,24},{2,26},{4,28},{6,30},{8,0},{10,2},{12,4},{14,6},{16,8},{18,... | collective-permute-start | bytes 393224 | tf_op jit(solution)/shard_map/ppermute | solution.py:229
  265.4 13.7 %collective-permute-start.24 = (bf16[4,64,256]{2,1,0:T(8,128)(2,1)S(1)}, bf16[4,64,256]{2,1,0:T(8,128)(2,1)S(1)}, u32[]{:S(2)}, u32[]{:S(2)}) collective-permute-start(bf16[4,64,256]{2,1,0:T(8,128)(2,1)S(1)} %get-tuple-element.97), channel_id=1, source_target_pairs={{0,16},{2,18},{4,20},{6,22},{8,24},{10,26},{12,28},{14,30},{16,0},... | collective-permute-start | bytes 393224 | tf_op jit(solution)/shard_map/ppermute | solution.py:229
  266.8 12.3 %collective-permute-start.23 = (bf16[4,64,256]{2,1,0:T(8,128)(2,1)S(1)}, bf16[4,64,256]{2,1,0:T(8,128)(2,1)S(1)}, u32[]{:S(2)}, u32[]{:S(2)}) collective-permute-start(bf16[4,64,256]{2,1,0:T(8,128)(2,1)S(1)} %get-tuple-element.95), channel_id=1, source_target_pairs={{0,8},{2,10},{4,12},{6,14},{8,16},{10,18},{12,20},{14,22},{16,24},... | collective-permute-start | bytes 393224 | tf_op jit(solution)/shard_map/ppermute | solution.py:229
  279.5 3.8 %collective-permute-start.26 = (f32[16,256]{1,0:T(8,128)S(1)}, f32[16,256]{1,0:T(8,128)S(1)}, u32[]{:S(2)}, u32[]{:S(2)}) collective-permute-start(f32[16,256]{1,0:T(8,128)S(1)} %dynamic-slice_bitcast_fusion.5), channel_id=1, source_target_pairs={{0,1},{1,0},{2,3},{3,2},{4,5},{5,4},{6,7},{7,6},{8,9},{9,8},{10,11... | collective-permute-start | bytes 49160 | tf_op jit(solution)/shard_map/ppermute | solution.py:256

commit v4 on v3

--- a/solution.py
+++ b/solution.py
@@ -78,7 +78,7 @@
             mixed = (1.0 - weight) * lower + weight * upper
             virtual[where, :] = mixed.T.astype(jnp.bfloat16)
 
-    @pl.loop(0, segments)
+    @pl.loop(0, segments, unroll=3 if segments % 3 == 0 else 1)
     def _(segment):
         start = pl.multiple_of(segment * HALF, HALF)
         product = jnp.dot(
@@ -132,32 +132,42 @@
     mics = one_cos.shape[1]
     units = blocks * groups
 
-    def generate(unit, steer):
+    def generate(unit, steer, tile):
         block = unit // groups
-        for tile in range(mics // ROWS):
-            rows = pl.ds(tile * ROWS, ROWS)
-            cos0, sin0 = now[0, rows], now[1, rows]
-            cos1, sin1 = one_cos[block, rows], one_sin[block, rows]
-            next_cos = cos0 * cos1 - sin0 * sin1
-            next_sin = sin0 * cos1 + cos0 * sin1
-            double = cos1 + cos1
-            turn_cos, turn_sin = step_cos[block, rows], step_sin[block, rows]
-            now[0, rows] = cos0 * turn_cos - sin0 * turn_sin
-            now[1, rows] = sin0 * turn_cos + cos0 * turn_sin
-            for place in range(bins):
-                steer[place, 0, rows] = cos0.astype(jnp.bfloat16)
-                steer[place, 1, rows] = sin0.astype(jnp.bfloat16)
-                cos0, next_cos = next_cos, double * next_cos - cos0
-                sin0, next_sin = next_sin, double * next_sin - sin0
-
-    def multiply(unit, steer):
+        rows = pl.ds(tile * ROWS, ROWS)
+        sin_rows = pl.ds(mics + tile * ROWS, ROWS)
+        cos0, sin0 = now[0, rows], now[1, rows]
+        cos1, sin1 = one_cos[block, rows], one_sin[block, rows]
+        next_cos = cos0 * cos1 - sin0 * sin1
+        next_sin = sin0 * cos1 + cos0 * sin1
+        double = cos1 + cos1
+        turn_cos, turn_sin = step_cos[block, rows], step_sin[block, rows]
+        now[0, rows] = cos0 * turn_cos - sin0 * turn_sin
+        now[1, rows] = sin0 * turn_cos + cos0 * turn_sin
+        for place in range(bins):
+            steer[place, rows] = cos0.astype(jnp.bfloat16)
+            steer[place, sin_rows] = sin0.astype(jnp.bfloat16)
+            cos0, next_cos = next_cos, double * next_cos - cos0
+            sin0, next_sin = next_sin, double * next_sin - sin0
+
+    def multiply(unit, steer, place):
         block, group = unit // groups, unit % groups
-        for place in range(bins):
-            rows = spectra_ref[block, group, 0, place]
-            turned = jnp.concatenate([rows[ROWS:], -rows[:ROWS]], 0)
-            product = jnp.dot(rows, steer[place, 0], preferred_element_type=jnp.float32)
-            product += jnp.dot(turned, steer[place, 1], preferred_element_type=jnp.float32)
-            out_ref[group, place, block] = product.astype(jnp.bfloat16)
+        rows = spectra_ref[block, group, 0, place]
+        turned = jnp.concatenate([rows[ROWS:], -rows[:ROWS]], 0)
+        if mics % 128 == 0:
+            both = jnp.concatenate([rows, turned], 1)
+            product = jnp.dot(both, steer[place], preferred_element_type=jnp.float32)
+        else:
+            product = jnp.dot(rows, steer[place, :mics], preferred_element_type=jnp.float32)
+            product += jnp.dot(turned, steer[place, mics:], preferred_element_type=jnp.float32)
+        out_ref[group, place, block] = product.astype(jnp.bfloat16)
+
+    def both(made, steer, used, other):
+        tiles = mics // ROWS
+        for tile in range(tiles):
+            for place in range(tile * bins // tiles, (tile + 1) * bins // tiles):
+                multiply(used, other, place)
+            generate(made, steer, tile)
 
     @pl.loop(0, units // 2)
     def _(pair):
@@ -170,12 +180,11 @@
                 now[0] = jnp.ones(now.shape[1:], jnp.float32)
                 now[1] = jnp.zeros(now.shape[1:], jnp.float32)
 
-        multiply(jnp.maximum(2 * pair - 1, 0), odd)
-        generate(2 * pair, even)
-        multiply(2 * pair, even)
-        generate(2 * pair + 1, odd)
-
-    multiply(units - 1, odd)
+        both(2 * pair, even, jnp.maximum(2 * pair - 1, 0), odd)
+        both(2 * pair + 1, odd, 2 * pair, even)
+
+    for place in range(bins):
+        multiply(units - 1, odd, place)
 
 
 def beams(spectra, waves, part):
@@ -193,8 +202,8 @@
         out_shape=jax.ShapeDtypeStruct((groups, bins, blocks, rows, points), jnp.bfloat16),
         scratch_shapes=[
             pltpu.VMEM((2, mics, points), jnp.float32),
-            pltpu.VMEM((bins, 2, mics, points), jnp.bfloat16),
-            pltpu.VMEM((bins, 2, mics, points), jnp.bfloat16),
+            pltpu.VMEM((bins, 2 * mics, points), jnp.bfloat16),
+            pltpu.VMEM((bins, 2 * mics, points), jnp.bfloat16),
         ],
         compiler_params=pltpu.CompilerParams(vmem_limit_bytes=48 << 20),
         cost_estimate=pl.CostEstimate(
@@ -207,20 +216,20 @@
     return out.reshape(groups, bins, blocks * rows, points)
 
 
-def fold_pair(x, bit):
+def fold_pair(x, bit, kind):
     sectors = lax.axis_size("sector")
     mine = lax.axis_index("sector") // bit % 2
     halves = x.reshape((x.shape[0] // 2, 2) + x.shape[1:])
     sent = lax.dynamic_index_in_dim(halves, 1 - mine, 1, keepdims=False).astype(jnp.bfloat16)
     kept = lax.dynamic_index_in_dim(halves, mine, 1, keepdims=False)
     got = lax.ppermute(sent, "sector", [(i, i ^ bit) for i in range(sectors)])
-    return kept.astype(jnp.float32) + got.astype(jnp.float32)
+    return (kept.astype(jnp.float32) + got.astype(jnp.float32)).astype(kind)
 
 
 def fold_line(x, stride):
     length = x.shape[0]
     place = lax.axis_index("sector") // stride
-    total = lax.dynamic_index_in_dim(x, place, 0, keepdims=False)
+    total = lax.dynamic_index_in_dim(x, place, 0, keepdims=False).astype(jnp.float32)
     devices = stride * length
     for shift in range(1, length):
         target = (place + shift) % length
@@ -234,7 +243,8 @@
     stages = []
     stride = 1
     while stride < 4 and sectors // stride % 2 == 0:
-        stages.append(functools.partial(fold_pair, bit=stride))
+        kind = jnp.bfloat16 if stride == 1 else jnp.float32
+        stages.append(functools.partial(fold_pair, bit=stride, kind=kind))
         stride *= 2
     stages.append(functools.partial(fold_line, stride=stride))
     return stages

time: 284 us -> 278 us (0.979)
    add x10 -> x5, other arithmetic: 16.3 us -> 2.87 us  [fold_pair(): return (kept.astype(jnp.float32) + got.astype(jnp.float32)).astype(kind)]
    convert_element_type x0 -> x5, other arithmetic: none -> 12.7 us  [fold_pair(): return (kept.astype(jnp.float32) + got.astype(jnp.float32)).astype(kind)]
    pallas_call x1, Pallas kernels: 43.2 us -> 36.5 us  [spectra_of(): pl.pallas_call(functools.partial(spectra_kernel, segments), grid=(blocks,...]
    convert_element_type x5 -> x0, local copies, waits for them, and re-layouts: 4.75 us -> none  [fold_pair(): lax.dynamic_index_in_dim(halves, 1 - mine, 1, keepdims=False)]
    pallas_call x5, Pallas kernels: 100 us -> 104 us  [beams(): pl.pallas_call(beam_kernel, grid=(1,), in_specs=[pl.BlockSpec((blocks, gr...]
    squeeze x5 -> x10, local copies, waits for them, and re-layouts: 7.39 us -> 9.29 us  [fold_pair(): lax.dynamic_index_in_dim(halves, 1 - mine, 1, keepdims=False)]
  transfers between devices with their start and end apart: 27 -> 27, of which waited for: 13 -> 12; matrix products, arithmetic and copies ran while one was open for 9% -> 8% of each run, Pallas kernels for 27% -> 28%
where the time goes in v4:
time: 278 us; the launch traced here: 277 us
  Pallas kernels  141 us (51%)
  waiting for transfers between devices  59.1 us (21%)
  other arithmetic  32.3 us (12%)
  starting transfers between devices  30.7 us (11%)
  local copies, waits for them, and re-layouts  14 us (5%)
    pallas_call x5, Pallas kernels, beams(): pl.pallas_call(beam_kernel, grid=(1,), in_specs=[pl.BlockSpec((blocks, gr...  104 us
    ppermute x15, waiting for transfers between devices, fold_line(): total += lax.ppermute(sent, 'sector', pairs).astype(jnp.float32)  51.3 us
    pallas_call x1, Pallas kernels, spectra_of(): pl.pallas_call(functools.partial(spectra_kernel, segments), grid=(blocks,...  36.5 us
    ppermute x15, starting transfers between devices, fold_line(): total += lax.ppermute(sent, 'sector', pairs).astype(jnp.float32)  17.5 us
    convert_element_type x5, other arithmetic, fold_pair(): return (kept.astype(jnp.float32) + got.astype(jnp.float32)).astype(kind)  12.7 us
    squeeze x10, local copies, waits for them, and re-layouts, fold_pair(): lax.dynamic_index_in_dim(halves, 1 - mine, 1, keepdims=False)  9.29 us
    convert_element_type x1, other arithmetic, fourier_table(): return (cos_of_turns(turns) * window).astype(jnp.bfloat16)  6.43 us
    ppermute x10, starting transfers between devices, fold_pair(): got = lax.ppermute(sent, 'sector', [(i, i ^ bit) for i in range(sectors)])  6.24 us
  transfers between devices with their start and end apart: 27, of which 12 were waited for; matrix products, arithmetic and copies ran while one was open for 8% of the time, Pallas kernels for 28%

profile of v4, /device:TPU:0, one launch (start us, length us, event | category | flops | bytes accessed | tf_op | source)
XLA Modules:
  0.0 277.3 jit_solution(4425312608012866802)
XLA Ops:
  0.0 1.0 slice.3
  1.0 5.5 %collective-permute-start = (bf16[2,1,8192]{2,1,0:T(2,128)(2,1)S(1)}, bf16[2,1,8192]{2,1,0:T(2,128)(2,1)S(1)}, u32[]{:S(2)}, u32[]{:S(2)}) collective-permute-start(bf16[2,1,8192]{2,1,0:T(2,128)(2,1)S(1)} %slice.3), channel_id=1, source_target_pairs={{0,30},{2,0},{4,2},{6,4},{8,6},{10,8},{12,10},{14,12},{16,14},{18,... | collective-permute-start | bytes 98312 | tf_op jit(solution)/shard_map/ppermute | solution.py:276
  6.5 0.7 cosine_multiply_fusion
  7.3 0.8 fusion.50
  8.1 2.3 fusion.20
  10.3 0.2 multiply_subtract_fusion.6
  10.5 1.2 multiply_add_fusion
  11.8 6.4 %fusion.1.table_ref = bf16[1024,1024]{1,0:T(8,128)(2,1)S(1)} fusion(f32[1024]{0:T(1024)S(1)} %bitcast.163, s32[1024]{0:T(1024)S(1)} %get-tuple-element.114, s32[1024]{0:T(1024)S(1)} %get-tuple-element.113), kind=kLoop, calls=%fused_computation.2 | loop fusion | flops 40894464 | bytes 2109440 | tf_op jit(solution)/shard_map/convert_element_type | solution.py:44
  18.3 1.7 multiply_add_fusion.2
  20.0 36.5 %welch.1 = bf16[2,16384,256]{2,1,0:T(8,128)(2,1)} custom-call(bf16[2,256,8192]{2,1,0:T(8,128)(2,1)} %signal_ref.1, bf16[2,1,8192]{2,1,0:T(2,128)(2,1)S(1)} %collective-permute-done.edge_ref, f32[2,1,8192]{2,1,0:T(1,128)S(1)} %broadcast_in_dim.2.weight_ref, bf16[1024,1024]{1,0:T(8,128)(2,1)S(1)} %fusion.1.table_ref), custom_call_target="tpu_custom_call" | custom-call | tf_op jit(solution)/shard_map/welch/pallas_call | solution.py:108
  56.6 25.3 %beams.5 = bf16[16,8,2,32,256]{4,3,2,1,0:T(8,128)(2,1)} custom-call(bf16[2,16,4,8,32,256]{5,4,3,2,1,0:T(8,128)(2,1)} %bitcast.140, f32[2,256,256]{2,1,0:T(8,128)S(1)} %get-tuple-element.41.refs_1_, f32[2,256,256]{2,1,0:T(8,128)S(1)} %get-tuple-element.42.refs_2_, f32[2,256,256]{2,1,0:T(8,128)S(1)} %copy-done.12, f32[2,256,256]{2,1,0:T(8,128)S(1)} %copy-done.10), custom_call_target="tpu_custom_call" | custom-call | flops 17179869184 | bytes 8388608 | tf_op jit(solution)/shard_map/beams/pallas_call | solution.py:194
  81.9 3.3 %dynamic-slice_bitcast_fusion.2 = bf16[8,8,64,256]{3,2,1,0:T(8,128)(2,1)} fusion(bf16[8,2,8,64,256]{4,3,2,1,0:T(8,128)(2,1)} %bitcast.155, s32[]{:T(128)S(6)} %select_n.206), kind=kLoop, calls=%fused_computation.34 | loop fusion | bytes 4194308 | tf_op jit(solution)/shard_map/jit(dynamic_index_in_dim)/squeeze | solution.py:223
  85.3 25.5 %beams.6 = bf16[16,8,2,32,256]{4,3,2,1,0:T(8,128)(2,1)} custom-call(bf16[2,16,4,8,32,256]{5,4,3,2,1,0:T(8,128)(2,1)} %bitcast.141, f32[2,256,256]{2,1,0:T(8,128)S(1)} %get-tuple-element.41.refs_1_, f32[2,256,256]{2,1,0:T(8,128)S(1)} %get-tuple-element.42.refs_2_, f32[2,256,256]{2,1,0:T(8,128)S(1)} %copy-done.13, f32[2,256,256]{2,1,0:T(8,128)S(1)} %copy-done.11, ...), custom_call_target="tpu_custom_call" | custom-call | flops 17179869184 | bytes 8388608 | tf_op jit(solution)/shard_map/beams/pallas_call | solution.py:194
  110.8 4.1 %fusion.4 = bf16[8,8,64,256]{3,2,1,0:T(8,128)(2,1)} fusion(bf16[8,8,64,256]{3,2,1,0:T(8,128)(2,1)} %collective-permute-done.1, bf16[8,2,8,64,256]{4,3,2,1,0:T(8,128)(2,1)S(1)} %bitcast.156, s32[]{:T(128)S(6)} %select_n.205), kind=kLoop, calls=%fused_computation.8 | loop fusion | flops 4194304 | bytes 6291460 | tf_op jit(solution)/shard_map/convert_element_type | solution.py:226
  114.9 1.5 dynamic-slice_bitcast_fusion.1
  116.4 0.5 collective-permute-start.3
  116.9 1.3 dynamic-slice_bitcast_fusion.7
  118.3 25.5 %beams.7 = bf16[16,8,2,32,256]{4,3,2,1,0:T(8,128)(2,1)} custom-call(bf16[2,16,4,8,32,256]{5,4,3,2,1,0:T(8,128)(2,1)} %bitcast.142, f32[2,256,256]{2,1,0:T(8,128)S(1)} %get-tuple-element.41.refs_1_, f32[2,256,256]{2,1,0:T(8,128)S(1)} %get-tuple-element.42.refs_2_, f32[2,256,256]{2,1,0:T(8,128)S(1)} %copy-done.13, f32[2,256,256]{2,1,0:T(8,128)S(1)} %copy-done.11, ...), custom_call_target="tpu_custom_call" | custom-call | flops 17179869184 | bytes 8388608 | tf_op jit(solution)/shard_map/beams/pallas_call | solution.py:194
  143.8 1.8 convert_add_fusion.7
  145.6 1.1 copy-done.21
  146.7 4.1 %fusion.3 = bf16[8,8,64,256]{3,2,1,0:T(8,128)(2,1)} fusion(bf16[8,8,64,256]{3,2,1,0:T(8,128)(2,1)} %collective-permute-done.3, bf16[8,2,8,64,256]{4,3,2,1,0:T(8,128)(2,1)S(1)} %bitcast.154, s32[]{:T(128)S(6)} %select_n.205), kind=kLoop, calls=%fused_computation.6 | loop fusion | flops 4194304 | bytes 6291460 | tf_op jit(solution)/shard_map/convert_element_type | solution.py:226
  150.8 1.4 dynamic-slice_bitcast_fusion
  152.3 1.5 fusion.22
  153.7 1.4 collective-permute-start.6
  155.1 1.0 collective-permute-start.4
  156.1 1.3 dynamic-slice_bitcast_fusion.6
  157.4 1.8 collective-permute-start.7
  159.2 14.0 %beams.8 = bf16[16,4,2,32,256]{4,3,2,1,0:T(8,128)(2,1)S(1)} custom-call(bf16[2,16,8,4,32,256]{5,4,3,2,1,0:T(8,128)(2,1)} %bitcast.143, f32[2,256,256]{2,1,0:T(8,128)S(1)} %get-tuple-element.41.refs_1_, f32[2,256,256]{2,1,0:T(8,128)S(1)} %get-tuple-element.42.refs_2_, f32[2,256,256]{2,1,0:T(8,128)S(1)} %copy-done.13, f32[2,256,256]{2,1,0:T(8,128)S(1)} %copy-done.11, ...), custom_call_target="tpu_custom_call" | custom-call | flops 8589934592 | bytes 4194304 | tf_op jit(solution)/shard_map/beams/pallas_call | solution.py:194
  173.2 4.6 %collective-permute-done.5 = bf16[8,64,256]{2,1,0:T(8,128)(2,1)S(1)} collective-permute-done((bf16[8,64,256]{2,1,0:T(8,128)(2,1)S(1)}, bf16[8,64,256]{2,1,0:T(8,128)(2,1)S(1)}, u32[]{:S(2)}, u32[]{:S(2)}) %collective-permute-start.5) | collective-permute-done | bytes 262176 | tf_op jit(solution)/shard_map/ppermute | solution.py:238
  177.9 1.2 fusion.19
  179.0 3.4 %collective-permute-done.7 = bf16[4,8,64,256]{3,2,1,0:T(8,128)(2,1)S(1)} collective-permute-done((bf16[4,8,64,256]{3,2,1,0:T(8,128)(2,1)S(1)}, bf16[4,8,64,256]{3,2,1,0:T(8,128)(2,1)S(1)}, u32[]{:S(2)}, u32[]{:S(2)}) %collective-permute-start.7) | collective-permute-done | bytes 1048608 | tf_op jit(solution)/shard_map/ppermute | solution.py:225
  182.4 0.4 convert_add_fusion.6
  182.9 2.5 fusion.2
  185.5 2.7 collective-permute-start.11
  188.2 0.8 collective-permute-start.10
  189.1 1.2 collective-permute-start.9
  190.4 1.8 collective-permute-start.12
  192.4 13.9 %beams.9 = bf16[16,4,2,32,256]{4,3,2,1,0:T(8,128)(2,1)S(1)} custom-call(bf16[2,16,8,4,32,256]{5,4,3,2,1,0:T(8,128)(2,1)} %bitcast.144, f32[2,256,256]{2,1,0:T(8,128)S(1)} %get-tuple-element.41.refs_1_, f32[2,256,256]{2,1,0:T(8,128)S(1)} %get-tuple-element.42.refs_2_, f32[2,256,256]{2,1,0:T(8,128)S(1)} %copy-done.13, f32[2,256,256]{2,1,0:T(8,128)S(1)} %copy-done.11, ...), custom_call_target="tpu_custom_call" | custom-call | flops 8589934592 | bytes 4194304 | tf_op jit(solution)/shard_map/beams/pallas_call | solution.py:194
  206.2 4.4 %collective-permute-done.10 = bf16[8,64,256]{2,1,0:T(8,128)(2,1)S(1)} collective-permute-done((bf16[8,64,256]{2,1,0:T(8,128)(2,1)S(1)}, bf16[8,64,256]{2,1,0:T(8,128)(2,1)S(1)}, u32[]{:S(2)}, u32[]{:S(2)}) %collective-permute-start.10) | collective-permute-done | bytes 262176 | tf_op jit(solution)/shard_map/ppermute | solution.py:238
  210.7 1.1 fusion.17
  211.7 2.0 collective-permute-done.12
  213.7 0.4 convert_add_fusion.5
  214.1 1.6 fusion.13
  216.0 1.5 collective-permute-start.17
  217.6 2.3 collective-permute-start.16
  219.9 0.7 collective-permute-start.15
  220.6 0.3 collective-permute-start.14
  220.9 5.8 %collective-permute-done.16 = bf16[8,64,256]{2,1,0:T(8,128)(2,1)S(1)} collective-permute-done((bf16[8,64,256]{2,1,0:T(8,128)(2,1)S(1)}, bf16[8,64,256]{2,1,0:T(8,128)(2,1)S(1)}, u32[]{:S(2)}, u32[]{:S(2)}) %collective-permute-start.16) | collective-permute-done | bytes 262176 | tf_op jit(solution)/shard_map/ppermute | solution.py:238
  226.7 17.2 %collective-permute-done.15 = bf16[8,64,256]{2,1,0:T(8,128)(2,1)S(1)} collective-permute-done((bf16[8,64,256]{2,1,0:T(8,128)(2,1)S(1)}, bf16[8,64,256]{2,1,0:T(8,128)(2,1)S(1)}, u32[]{:S(2)}, u32[]{:S(2)}) %collective-permute-start.15) | collective-permute-done | bytes 262176 | tf_op jit(solution)/shard_map/ppermute | solution.py:238
  244.2 0.4 fusion.12
  244.7 0.4 collective-permute-start.22
  245.2 1.6 collective-permute-start.20
  246.8 1.9 collective-permute-start.19
  248.8 2.0 collective-permute-done.21
  250.7 7.0 %collective-permute-done.20 = bf16[4,64,256]{2,1,0:T(8,128)(2,1)S(1)} collective-permute-done((bf16[4,64,256]{2,1,0:T(8,128)(2,1)S(1)}, bf16[4,64,256]{2,1,0:T(8,128)(2,1)S(1)}, u32[]{:S(2)}, u32[]{:S(2)}) %collective-permute-start.20) | collective-permute-done | bytes 131104 | tf_op jit(solution)/shard_map/ppermute | solution.py:238
  257.8 0.2 collective-permute-done.22
  258.1 0.7 fusion.38
  258.8 1.4 collective-permute-start.24
  260.2 2.0 collective-permute-start.23
  262.3 2.2 collective-permute-done.25
  264.4 8.1 %collective-permute-done.24 = bf16[4,64,256]{2,1,0:T(8,128)(2,1)S(1)} collective-permute-done((bf16[4,64,256]{2,1,0:T(8,128)(2,1)S(1)}, bf16[4,64,256]{2,1,0:T(8,128)(2,1)S(1)}, u32[]{:S(2)}, u32[]{:S(2)}) %collective-permute-start.24) | collective-permute-done | bytes 131104 | tf_op jit(solution)/shard_map/ppermute | solution.py:238
  272.9 1.6 collective-permute-start.26
  274.5 2.2 collective-permute-done.26
  276.7 0.6 bitcast_add_fusion.5
  (95 shorter events, 2.0 us)
Async XLA Ops:
  1.0 19.1 %collective-permute-start = (bf16[2,1,8192]{2,1,0:T(2,128)(2,1)S(1)}, bf16[2,1,8192]{2,1,0:T(2,128)(2,1)S(1)}, u32[]{:S(2)}, u32[]{:S(2)}) collective-permute-start(bf16[2,1,8192]{2,1,0:T(2,128)(2,1)S(1)} %slice.3), channel_id=1, source_target_pairs={{0,30},{2,0},{4,2},{6,4},{8,6},{10,8},{12,10},{14,12},{16,14},{18,... | collective-permute-start | bytes 98312 | tf_op jit(solution)/shard_map/ppermute | solution.py:276
  11.7 6.5 %copy-start = (f32[2,256,256]{2,1,0:T(8,128)}, f32[2,256,256]{2,1,0:T(8,128)S(1)}, u32[]{:S(2)}) copy-start(f32[2,256,256]{2,1,0:T(8,128)S(1)} %get-tuple-element.80.refs_5_) | copy-start | bytes 1572868
  11.8 6.5 %copy-start.2 = (f32[2,256,256]{2,1,0:T(8,128)}, f32[2,256,256]{2,1,0:T(8,128)S(1)}, u32[]{:S(2)}) copy-start(f32[2,256,256]{2,1,0:T(8,128)S(1)} %get-tuple-element.81.refs_6_) | copy-start | bytes 1572868
  11.8 6.5 %copy-start.4 = (f32[2,256,256]{2,1,0:T(8,128)}, f32[2,256,256]{2,1,0:T(8,128)S(1)}, u32[]{:S(2)}) copy-start(f32[2,256,256]{2,1,0:T(8,128)S(1)} %get-tuple-element.82.refs_6_) | copy-start | bytes 1572868
  11.8 6.5 %copy-start.6 = (f32[2,256,256]{2,1,0:T(8,128)}, f32[2,256,256]{2,1,0:T(8,128)S(1)}, u32[]{:S(2)}) copy-start(f32[2,256,256]{2,1,0:T(8,128)S(1)} %get-tuple-element.83.refs_5_) | copy-start | bytes 1572868
  11.8 8.2 %copy-start.23 = (f32[2,8192]{1,0:T(2,128)S(1)}, f32[2,8192]{1,0:T(2,128)}, u32[]{:S(2)}) copy-start(f32[2,8192]{1,0:T(2,128)} %param.7) | copy-start | bytes 196612
  20.0 36.6 %copy-start.10 = (f32[2,256,256]{2,1,0:T(8,128)S(1)}, f32[2,256,256]{2,1,0:T(8,128)}, u32[]{:S(2)}) copy-start(f32[2,256,256]{2,1,0:T(8,128)} %get-tuple-element.102.refs_4_) | copy-start | bytes 1572868
  20.0 36.5 %copy-start.12 = (f32[2,256,256]{2,1,0:T(8,128)S(1)}, f32[2,256,256]{2,1,0:T(8,128)}, u32[]{:S(2)}) copy-start(f32[2,256,256]{2,1,0:T(8,128)} %get-tuple-element.103.refs_3_) | copy-start | bytes 1572868
  81.9 3.3 %copy-start.5 = (f32[2,256,256]{2,1,0:T(8,128)S(1)}, f32[2,256,256]{2,1,0:T(8,128)}, u32[]{:S(2)}) copy-start(f32[2,256,256]{2,1,0:T(8,128)} %copy-done.4) | copy-start | bytes 1572868
  81.9 3.3 %copy-start.7 = (f32[2,256,256]{2,1,0:T(8,128)S(1)}, f32[2,256,256]{2,1,0:T(8,128)}, u32[]{:S(2)}) copy-start(f32[2,256,256]{2,1,0:T(8,128)} %copy-done.6) | copy-start | bytes 1572868
  81.9 3.3 %copy-start.11 = (f32[2,256,256]{2,1,0:T(8,128)S(1)}, f32[2,256,256]{2,1,0:T(8,128)}, u32[]{:S(2)}) copy-start(f32[2,256,256]{2,1,0:T(8,128)} %get-tuple-element.102.refs_4_) | copy-start | bytes 1572868
  81.9 3.4 %copy-start.13 = (f32[2,256,256]{2,1,0:T(8,128)S(1)}, f32[2,256,256]{2,1,0:T(8,128)}, u32[]{:S(2)}) copy-start(f32[2,256,256]{2,1,0:T(8,128)} %get-tuple-element.103.refs_3_) | copy-start | bytes 1572868
  85.3 25.5 %collective-permute-start.1 = (bf16[8,8,64,256]{3,2,1,0:T(8,128)(2,1)}, bf16[8,8,64,256]{3,2,1,0:T(8,128)(2,1)}, u32[]{:S(2)}, u32[]{:S(2)}) collective-permute-start(bf16[8,8,64,256]{3,2,1,0:T(8,128)(2,1)} %dynamic-slice_bitcast_fusion.2), channel_id=1, source_target_pairs={{0,2},{2,0},{4,6},{6,4},{8,10},{10,8},{12,14},{14,12},{16,18},{18,... | collective-permute-start | bytes 6291464 | tf_op jit(solution)/shard_map/ppermute | solution.py:225
  85.3 25.5 %copy-start.22 = (bf16[16,8,2,32,256]{4,3,2,1,0:T(8,128)(2,1)S(1)}, bf16[16,8,2,32,256]{4,3,2,1,0:T(8,128)(2,1)}, u32[]{:S(2)}) copy-start(bf16[16,8,2,32,256]{4,3,2,1,0:T(8,128)(2,1)} %beams.5) | copy-start | bytes 12582916
  110.8 4.1 %copy-start.20 = (bf16[16,8,2,32,256]{4,3,2,1,0:T(8,128)(2,1)S(1)}, bf16[16,8,2,32,256]{4,3,2,1,0:T(8,128)(2,1)}, u32[]{:S(2)}) copy-start(bf16[16,8,2,32,256]{4,3,2,1,0:T(8,128)(2,1)} %beams.6) | copy-start | bytes 12582916
  114.9 3.4 %copy-start.1 = (f32[2,256,256]{2,1,0:T(8,128)S(1)}, f32[2,256,256]{2,1,0:T(8,128)}, u32[]{:S(2)}) copy-start(f32[2,256,256]{2,1,0:T(8,128)} %copy-done) | copy-start | bytes 1572868
  114.9 3.4 %copy-start.3 = (f32[2,256,256]{2,1,0:T(8,128)S(1)}, f32[2,256,256]{2,1,0:T(8,128)}, u32[]{:S(2)}) copy-start(f32[2,256,256]{2,1,0:T(8,128)} %copy-done.2) | copy-start | bytes 1572868
  116.4 29.2 %collective-permute-start.3 = (bf16[8,8,64,256]{3,2,1,0:T(8,128)(2,1)}, bf16[8,8,64,256]{3,2,1,0:T(8,128)(2,1)}, u32[]{:S(2)}, u32[]{:S(2)}) collective-permute-start(bf16[8,8,64,256]{3,2,1,0:T(8,128)(2,1)} %dynamic-slice_bitcast_fusion.1), channel_id=1, source_target_pairs={{0,2},{2,0},{4,6},{6,4},{8,10},{10,8},{12,14},{14,12},{16,18},{18,... | collective-permute-start | bytes 6291464 | tf_op jit(solution)/shard_map/ppermute | solution.py:225
  118.2 25.6 %collective-permute-start.2 = (bf16[4,8,64,256]{3,2,1,0:T(8,128)(2,1)S(1)}, bf16[4,8,64,256]{3,2,1,0:T(8,128)(2,1)S(1)}, u32[]{:S(2)}, u32[]{:S(2)}) collective-permute-start(bf16[4,8,64,256]{3,2,1,0:T(8,128)(2,1)S(1)} %dynamic-slice_bitcast_fusion.7), channel_id=1, source_target_pairs={{0,4},{2,6},{4,0},{6,2},{8,12},{10,14},{12,8},{14,10},{16,20},{18,... | collective-permute-start | bytes 3145736 | tf_op jit(solution)/shard_map/ppermute | solution.py:225
  118.3 25.5 %copy-start.17 = (bf16[8,8,64,256]{3,2,1,0:T(8,128)(2,1)S(1)}, bf16[8,8,64,256]{3,2,1,0:T(8,128)(2,1)}, u32[]{:S(2)}) copy-start(bf16[8,8,64,256]{3,2,1,0:T(8,128)(2,1)} %fusion.4) | copy-start | bytes 6291460
  143.8 2.9 %copy-start.21 = (bf16[16,8,2,32,256]{4,3,2,1,0:T(8,128)(2,1)S(1)}, bf16[16,8,2,32,256]{4,3,2,1,0:T(8,128)(2,1)}, u32[]{:S(2)}) copy-start(bf16[16,8,2,32,256]{4,3,2,1,0:T(8,128)(2,1)} %beams.6) | copy-start | bytes 12582916
  145.6 5.2 %copy-start.18 = (bf16[16,8,2,32,256]{4,3,2,1,0:T(8,128)(2,1)S(1)}, bf16[16,8,2,32,256]{4,3,2,1,0:T(8,128)(2,1)}, u32[]{:S(2)}) copy-start(bf16[16,8,2,32,256]{4,3,2,1,0:T(8,128)(2,1)} %beams.7) | copy-start | bytes 12582916
  150.8 8.4 %copy-start.14 = (f32[2,256,256]{2,1,0:T(8,128)S(1)}, f32[2,256,256]{2,1,0:T(8,128)}, u32[]{:S(2)}) copy-start(f32[2,256,256]{2,1,0:T(8,128)} %get-tuple-element.90.refs_6_) | copy-start | bytes 1572868
  150.8 8.4 %copy-start.15 = (f32[2,256,256]{2,1,0:T(8,128)S(1)}, f32[2,256,256]{2,1,0:T(8,128)}, u32[]{:S(2)}) copy-start(f32[2,256,256]{2,1,0:T(8,128)} %get-tuple-element.91.refs_5_) | copy-start | bytes 1572868
  152.2 30.6 %collective-permute-start.8 = (bf16[8,8,64,256]{3,2,1,0:T(8,128)(2,1)}, bf16[8,8,64,256]{3,2,1,0:T(8,128)(2,1)}, u32[]{:S(2)}, u32[]{:S(2)}) collective-permute-start(bf16[8,8,64,256]{3,2,1,0:T(8,128)(2,1)} %dynamic-slice_bitcast_fusion), channel_id=1, source_target_pairs={{0,2},{2,0},{4,6},{6,4},{8,10},{10,8},{12,14},{14,12},{16,18},{18,... | collective-permute-start | bytes 6291464 | tf_op jit(solution)/shard_map/ppermute | solution.py:225
  153.7 19.5 %collective-permute-start.6 = (bf16[8,64,256]{2,1,0:T(8,128)(2,1)S(1)}, bf16[8,64,256]{2,1,0:T(8,128)(2,1)S(1)}, u32[]{:S(2)}, u32[]{:S(2)}) collective-permute-start(bf16[8,64,256]{2,1,0:T(8,128)(2,1)S(1)} %get-tuple-element.93), channel_id=1, source_target_pairs={{0,24},{2,26},{4,28},{6,30},{8,0},{10,2},{12,4},{14,6},{16,8},{18,... | collective-permute-start | bytes 786440 | tf_op jit(solution)/shard_map/ppermute | solution.py:238
  155.1 22.8 %collective-permute-start.5 = (bf16[8,64,256]{2,1,0:T(8,128)(2,1)S(1)}, bf16[8,64,256]{2,1,0:T(8,128)(2,1)S(1)}, u32[]{:S(2)}, u32[]{:S(2)}) collective-permute-start(bf16[8,64,256]{2,1,0:T(8,128)(2,1)S(1)} %get-tuple-element.94), channel_id=1, source_target_pairs={{0,16},{2,18},{4,20},{6,22},{8,24},{10,26},{12,28},{14,30},{16,0},... | collective-permute-start | bytes 786440 | tf_op jit(solution)/shard_map/ppermute | solution.py:238
  155.1 22.8 %collective-permute-start.4 = (bf16[8,64,256]{2,1,0:T(8,128)(2,1)S(1)}, bf16[8,64,256]{2,1,0:T(8,128)(2,1)S(1)}, u32[]{:S(2)}, u32[]{:S(2)}) collective-permute-start(bf16[8,64,256]{2,1,0:T(8,128)(2,1)S(1)} %get-tuple-element.92), channel_id=1, source_target_pairs={{0,8},{2,10},{4,12},{6,14},{8,16},{10,18},{12,20},{14,22},{16,24},... | collective-permute-start | bytes 786440 | tf_op jit(solution)/shard_map/ppermute | solution.py:238
  157.4 25.0 %collective-permute-start.7 = (bf16[4,8,64,256]{3,2,1,0:T(8,128)(2,1)S(1)}, bf16[4,8,64,256]{3,2,1,0:T(8,128)(2,1)S(1)}, u32[]{:S(2)}, u32[]{:S(2)}) collective-permute-start(bf16[4,8,64,256]{3,2,1,0:T(8,128)(2,1)S(1)} %dynamic-slice_bitcast_fusion.6), channel_id=1, source_target_pairs={{0,4},{2,6},{4,0},{6,2},{8,12},{10,14},{12,8},{14,10},{16,20},{18,... | collective-permute-start | bytes 3145736 | tf_op jit(solution)/shard_map/ppermute | solution.py:225
  159.2 23.3 %copy-start.16 = (bf16[8,8,64,256]{3,2,1,0:T(8,128)(2,1)S(1)}, bf16[8,8,64,256]{3,2,1,0:T(8,128)(2,1)}, u32[]{:S(2)}) copy-start(bf16[8,8,64,256]{3,2,1,0:T(8,128)(2,1)} %fusion.3) | copy-start | bytes 6291460
  173.2 9.7 %copy-start.19 = (bf16[16,8,2,32,256]{4,3,2,1,0:T(8,128)(2,1)S(1)}, bf16[16,8,2,32,256]{4,3,2,1,0:T(8,128)(2,1)}, u32[]{:S(2)}) copy-start(bf16[16,8,2,32,256]{4,3,2,1,0:T(8,128)(2,1)} %beams.7) | copy-start | bytes 12582916
  185.4 7.0 %copy-start.8 = (f32[2,256,256]{2,1,0:T(8,128)S(1)}, f32[2,256,256]{2,1,0:T(8,128)}, u32[]{:S(2)}) copy-start(f32[2,256,256]{2,1,0:T(8,128)} %get-tuple-element.77.refs_6_) | copy-start | bytes 1572868
  185.4 7.0 %copy-start.9 = (f32[2,256,256]{2,1,0:T(8,128)S(1)}, f32[2,256,256]{2,1,0:T(8,128)}, u32[]{:S(2)}) copy-start(f32[2,256,256]{2,1,0:T(8,128)} %get-tuple-element.101.refs_5_) | copy-start | bytes 1572868
  185.5 20.7 %collective-permute-start.11 = (bf16[8,64,256]{2,1,0:T(8,128)(2,1)S(1)}, bf16[8,64,256]{2,1,0:T(8,128)(2,1)S(1)}, u32[]{:S(2)}, u32[]{:S(2)}) collective-permute-start(bf16[8,64,256]{2,1,0:T(8,128)(2,1)S(1)} %get-tuple-element.88), channel_id=1, source_target_pairs={{0,24},{2,26},{4,28},{6,30},{8,0},{10,2},{12,4},{14,6},{16,8},{18,... | collective-permute-start | bytes 786440 | tf_op jit(solution)/shard_map/ppermute | solution.py:238
  188.2 22.4 %collective-permute-start.10 = (bf16[8,64,256]{2,1,0:T(8,128)(2,1)S(1)}, bf16[8,64,256]{2,1,0:T(8,128)(2,1)S(1)}, u32[]{:S(2)}, u32[]{:S(2)}) collective-permute-start(bf16[8,64,256]{2,1,0:T(8,128)(2,1)S(1)} %get-tuple-element.89), channel_id=1, source_target_pairs={{0,16},{2,18},{4,20},{6,22},{8,24},{10,26},{12,28},{14,30},{16,0},... | collective-permute-start | bytes 786440 | tf_op jit(solution)/shard_map/ppermute | solution.py:238
  189.1 21.6 %collective-permute-start.9 = (bf16[8,64,256]{2,1,0:T(8,128)(2,1)S(1)}, bf16[8,64,256]{2,1,0:T(8,128)(2,1)}, u32[]{:S(2)}, u32[]{:S(2)}) collective-permute-start(bf16[8,64,256]{2,1,0:T(8,128)(2,1)S(1)} %get-tuple-element.87), channel_id=1, source_target_pairs={{0,8},{2,10},{4,12},{6,14},{8,16},{10,18},{12,20},{14,22},{16,24},... | collective-permute-start | bytes 786440 | tf_op jit(solution)/shard_map/ppermute | solution.py:238
  190.4 23.3 %collective-permute-start.12 = (bf16[4,8,64,256]{3,2,1,0:T(8,128)(2,1)S(1)}, bf16[4,8,64,256]{3,2,1,0:T(8,128)(2,1)S(1)}, u32[]{:S(2)}, u32[]{:S(2)}) collective-permute-start(bf16[4,8,64,256]{3,2,1,0:T(8,128)(2,1)S(1)} %dynamic-slice_bitcast_fusion.5), channel_id=1, source_target_pairs={{0,4},{2,6},{4,0},{6,2},{8,12},{10,14},{12,8},{14,10},{16,20},{18,... | collective-permute-start | bytes 3145736 | tf_op jit(solution)/shard_map/ppermute | solution.py:225
  192.3 21.8 %collective-permute-start.13 = (bf16[8,4,64,256]{3,2,1,0:T(8,128)(2,1)S(1)}, bf16[8,4,64,256]{3,2,1,0:T(8,128)(2,1)}, u32[]{:S(2)}, u32[]{:S(2)}) collective-permute-start(bf16[8,4,64,256]{3,2,1,0:T(8,128)(2,1)S(1)} %dynamic-slice_bitcast_fusion.4), channel_id=1, source_target_pairs={{0,2},{2,0},{4,6},{6,4},{8,10},{10,8},{12,14},{14,12},{16,18},{18,... | collective-permute-start | bytes 3145736 | tf_op jit(solution)/shard_map/ppermute | solution.py:225
  215.8 28.3 %collective-permute-start.18 = (bf16[8,4,64,256]{3,2,1,0:T(8,128)(2,1)S(1)}, bf16[8,4,64,256]{3,2,1,0:T(8,128)(2,1)S(1)}, u32[]{:S(2)}, u32[]{:S(2)}) collective-permute-start(bf16[8,4,64,256]{3,2,1,0:T(8,128)(2,1)S(1)} %dynamic-slice_bitcast_fusion.3), channel_id=1, source_target_pairs={{0,2},{2,0},{4,6},{6,4},{8,10},{10,8},{12,14},{14,12},{16,18},{18,... | collective-permute-start | bytes 3145736 | tf_op jit(solution)/shard_map/ppermute | solution.py:225
  216.0 28.0 %collective-permute-start.17 = (bf16[4,4,64,256]{3,2,1,0:T(8,128)(2,1)S(1)}, bf16[4,4,64,256]{3,2,1,0:T(8,128)(2,1)S(1)}, u32[]{:S(2)}, u32[]{:S(2)}) collective-permute-start(bf16[4,4,64,256]{3,2,1,0:T(8,128)(2,1)S(1)} %dynamic-slice_bitcast_fusion.9), channel_id=1, source_target_pairs={{0,4},{2,6},{4,0},{6,2},{8,12},{10,14},{12,8},{14,10},{16,20},{18,... | collective-permute-start | bytes 1572872 | tf_op jit(solution)/shard_map/ppermute | solution.py:225
  217.6 9.1 %collective-permute-start.16 = (bf16[8,64,256]{2,1,0:T(8,128)(2,1)S(1)}, bf16[8,64,256]{2,1,0:T(8,128)(2,1)S(1)}, u32[]{:S(2)}, u32[]{:S(2)}) collective-permute-start(bf16[8,64,256]{2,1,0:T(8,128)(2,1)S(1)} %get-tuple-element.85), channel_id=1, source_target_pairs={{0,24},{2,26},{4,28},{6,30},{8,0},{10,2},{12,4},{14,6},{16,8},{18,... | collective-permute-start | bytes 786440 | tf_op jit(solution)/shard_map/ppermute | solution.py:238
  219.9 24.0 %collective-permute-start.15 = (bf16[8,64,256]{2,1,0:T(8,128)(2,1)S(1)}, bf16[8,64,256]{2,1,0:T(8,128)(2,1)S(1)}, u32[]{:S(2)}, u32[]{:S(2)}) collective-permute-start(bf16[8,64,256]{2,1,0:T(8,128)(2,1)S(1)} %get-tuple-element.86), channel_id=1, source_target_pairs={{0,16},{2,18},{4,20},{6,22},{8,24},{10,26},{12,28},{14,30},{16,0},... | collective-permute-start | bytes 786440 | tf_op jit(solution)/shard_map/ppermute | solution.py:238
  220.6 23.2 %collective-permute-start.14 = (bf16[8,64,256]{2,1,0:T(8,128)(2,1)S(1)}, bf16[8,64,256]{2,1,0:T(8,128)(2,1)S(1)}, u32[]{:S(2)}, u32[]{:S(2)}) collective-permute-start(bf16[8,64,256]{2,1,0:T(8,128)(2,1)S(1)} %get-tuple-element.84), channel_id=1, source_target_pairs={{0,8},{2,10},{4,12},{6,14},{8,16},{10,18},{12,20},{14,22},{16,24},... | collective-permute-start | bytes 786440 | tf_op jit(solution)/shard_map/ppermute | solution.py:238
  244.7 13.3 %collective-permute-start.22 = (bf16[4,4,64,256]{3,2,1,0:T(8,128)(2,1)S(1)}, bf16[4,4,64,256]{3,2,1,0:T(8,128)(2,1)S(1)}, u32[]{:S(2)}, u32[]{:S(2)}) collective-permute-start(bf16[4,4,64,256]{3,2,1,0:T(8,128)(2,1)S(1)} %dynamic-slice_bitcast_fusion.8), channel_id=1, source_target_pairs={{0,4},{2,6},{4,0},{6,2},{8,12},{10,14},{12,8},{14,10},{16,20},{18,... | collective-permute-start | bytes 1572872 | tf_op jit(solution)/shard_map/ppermute | solution.py:225
  245.1 5.6 %collective-permute-start.21 = (bf16[4,64,256]{2,1,0:T(8,128)(2,1)S(1)}, bf16[4,64,256]{2,1,0:T(8,128)(2,1)S(1)}, u32[]{:S(2)}, u32[]{:S(2)}) collective-permute-start(bf16[4,64,256]{2,1,0:T(8,128)(2,1)S(1)} %get-tuple-element.99), channel_id=1, source_target_pairs={{0,24},{2,26},{4,28},{6,30},{8,0},{10,2},{12,4},{14,6},{16,8},{18,... | collective-permute-start | bytes 393224 | tf_op jit(solution)/shard_map/ppermute | solution.py:238
  245.2 12.5 %collective-permute-start.20 = (bf16[4,64,256]{2,1,0:T(8,128)(2,1)S(1)}, bf16[4,64,256]{2,1,0:T(8,128)(2,1)S(1)}, u32[]{:S(2)}, u32[]{:S(2)}) collective-permute-start(bf16[4,64,256]{2,1,0:T(8,128)(2,1)S(1)} %get-tuple-element.100), channel_id=1, source_target_pairs={{0,16},{2,18},{4,20},{6,22},{8,24},{10,26},{12,28},{14,30},{16,0},... | collective-permute-start | bytes 393224 | tf_op jit(solution)/shard_map/ppermute | solution.py:238
  246.8 10.9 %collective-permute-start.19 = (bf16[4,64,256]{2,1,0:T(8,128)(2,1)S(1)}, bf16[4,64,256]{2,1,0:T(8,128)(2,1)S(1)}, u32[]{:S(2)}, u32[]{:S(2)}) collective-permute-start(bf16[4,64,256]{2,1,0:T(8,128)(2,1)S(1)} %get-tuple-element.98), channel_id=1, source_target_pairs={{0,8},{2,10},{4,12},{6,14},{8,16},{10,18},{12,20},{14,22},{16,24},... | collective-permute-start | bytes 393224 | tf_op jit(solution)/shard_map/ppermute | solution.py:238
  258.8 5.6 %collective-permute-start.25 = (bf16[4,64,256]{2,1,0:T(8,128)(2,1)}, bf16[4,64,256]{2,1,0:T(8,128)(2,1)S(1)}, u32[]{:S(2)}, u32[]{:S(2)}) collective-permute-start(bf16[4,64,256]{2,1,0:T(8,128)(2,1)} %get-tuple-element.96), channel_id=1, source_target_pairs={{0,24},{2,26},{4,28},{6,30},{8,0},{10,2},{12,4},{14,6},{16,8},{18,... | collective-permute-start | bytes 393224 | tf_op jit(solution)/shard_map/ppermute | solution.py:238
  258.8 13.7 %collective-permute-start.24 = (bf16[4,64,256]{2,1,0:T(8,128)(2,1)S(1)}, bf16[4,64,256]{2,1,0:T(8,128)(2,1)S(1)}, u32[]{:S(2)}, u32[]{:S(2)}) collective-permute-start(bf16[4,64,256]{2,1,0:T(8,128)(2,1)S(1)} %get-tuple-element.97), channel_id=1, source_target_pairs={{0,16},{2,18},{4,20},{6,22},{8,24},{10,26},{12,28},{14,30},{16,0},... | collective-permute-start | bytes 393224 | tf_op jit(solution)/shard_map/ppermute | solution.py:238
  260.2 12.3 %collective-permute-start.23 = (bf16[4,64,256]{2,1,0:T(8,128)(2,1)S(1)}, bf16[4,64,256]{2,1,0:T(8,128)(2,1)S(1)}, u32[]{:S(2)}, u32[]{:S(2)}) collective-permute-start(bf16[4,64,256]{2,1,0:T(8,128)(2,1)S(1)} %get-tuple-element.95), channel_id=1, source_target_pairs={{0,8},{2,10},{4,12},{6,14},{8,16},{10,18},{12,20},{14,22},{16,24},... | collective-permute-start | bytes 393224 | tf_op jit(solution)/shard_map/ppermute | solution.py:238
  272.9 3.8 %collective-permute-start.26 = (f32[16,256]{1,0:T(8,128)S(1)}, f32[16,256]{1,0:T(8,128)S(1)}, u32[]{:S(2)}, u32[]{:S(2)}) collective-permute-start(f32[16,256]{1,0:T(8,128)S(1)} %dynamic-slice_bitcast_fusion.10), channel_id=1, source_target_pairs={{0,1},{1,0},{2,3},{3,2},{4,5},{5,4},{6,7},{7,6},{8,9},{9,8},{10,11... | collective-permute-start | bytes 49160 | tf_op jit(solution)/shard_map/ppermute | solution.py:266

commit v5 on v4

--- a/solution.py
+++ b/solution.py
@@ -154,19 +154,14 @@
         block, group = unit // groups, unit % groups
         rows = spectra_ref[block, group, 0, place]
         turned = jnp.concatenate([rows[ROWS:], -rows[:ROWS]], 0)
-        if mics % 128 == 0:
-            both = jnp.concatenate([rows, turned], 1)
-            product = jnp.dot(both, steer[place], preferred_element_type=jnp.float32)
-        else:
-            product = jnp.dot(rows, steer[place, :mics], preferred_element_type=jnp.float32)
-            product += jnp.dot(turned, steer[place, mics:], preferred_element_type=jnp.float32)
+        product = jnp.dot(rows, steer[place, :mics], preferred_element_type=jnp.float32)
+        product += jnp.dot(turned, steer[place, mics:], preferred_element_type=jnp.float32)
         out_ref[group, place, block] = product.astype(jnp.bfloat16)
 
     def both(made, steer, used, other):
-        tiles = mics // ROWS
-        for tile in range(tiles):
-            for place in range(tile * bins // tiles, (tile + 1) * bins // tiles):
-                multiply(used, other, place)
+        for place in range(bins):
+            multiply(used, other, place)
+        for tile in range(mics // ROWS):
             generate(made, steer, tile)
 
     @pl.loop(0, units // 2)

time: 278 us -> 275 us (0.989)
  Pallas kernels: 141 us -> 137 us
    pallas_call x5, Pallas kernels: 104 us -> 100 us  [beams(): pl.pallas_call(beam_kernel, grid=(1,), in_specs=[pl.BlockSpec((blocks, gr...]
  transfers between devices with their start and end apart: 27 -> 27, of which waited for: 12 -> 13; matrix products, arithmetic and copies ran while one was open for 8% -> 8% of each run, Pallas kernels for 28% -> 28%
where the time goes in v5:
time: 275 us; the launch traced here: 274 us
  Pallas kernels  137 us (50%)
  waiting for transfers between devices  60.5 us (22%)
  other arithmetic  32.2 us (12%)
  starting transfers between devices  30.8 us (11%)
  local copies, waits for them, and re-layouts  13.5 us (5%)
    pallas_call x5, Pallas kernels, beams(): pl.pallas_call(beam_kernel, grid=(1,), in_specs=[pl.BlockSpec((blocks, gr...  100 us
    ppermute x15, waiting for transfers between devices, fold_line(): total += lax.ppermute(sent, 'sector', pairs).astype(jnp.float32)  52.2 us
    pallas_call x1, Pallas kernels, spectra_of(): pl.pallas_call(functools.partial(spectra_kernel, segments), grid=(blocks,...  36.5 us
    ppermute x15, starting transfers between devices, fold_line(): total += lax.ppermute(sent, 'sector', pairs).astype(jnp.float32)  17.4 us
    convert_element_type x5, other arithmetic, fold_pair(): return (kept.astype(jnp.float32) + got.astype(jnp.float32)).astype(kind)  12.7 us
    squeeze x10, local copies, waits for them, and re-layouts, fold_pair(): lax.dynamic_index_in_dim(halves, 1 - mine, 1, keepdims=False)  9.29 us
    convert_element_type x1, other arithmetic, fourier_table(): return (cos_of_turns(turns) * window).astype(jnp.bfloat16)  6.43 us
    ppermute x10, starting transfers between devices, fold_pair(): got = lax.ppermute(sent, 'sector', [(i, i ^ bit) for i in range(sectors)])  6.26 us
  transfers between devices with their start and end apart: 27, of which 13 were waited for; matrix products, arithmetic and copies ran while one was open for 8% of the time, Pallas kernels for 28%

profile of v5, /device:TPU:0, one launch (start us, length us, event | category | flops | bytes accessed | tf_op | source)
XLA Modules:
  0.0 274.5 jit_solution(1778817807070650068)
XLA Ops:
  0.0 1.0 slice.3
  1.0 5.5 %collective-permute-start = (bf16[2,1,8192]{2,1,0:T(2,128)(2,1)S(1)}, bf16[2,1,8192]{2,1,0:T(2,128)(2,1)S(1)}, u32[]{:S(2)}, u32[]{:S(2)}) collective-permute-start(bf16[2,1,8192]{2,1,0:T(2,128)(2,1)S(1)} %slice.3), channel_id=1, source_target_pairs={{0,30},{2,0},{4,2},{6,4},{8,6},{10,8},{12,10},{14,12},{16,14},{18,... | collective-permute-start | bytes 98312 | tf_op jit(solution)/shard_map/ppermute | solution.py:271
  6.5 0.7 cosine_multiply_fusion
  7.3 0.8 fusion.50
  8.1 2.3 fusion.20
  10.3 0.2 multiply_subtract_fusion.6
  10.5 1.2 multiply_add_fusion
  11.8 6.4 %fusion.1.table_ref = bf16[1024,1024]{1,0:T(8,128)(2,1)S(1)} fusion(f32[1024]{0:T(1024)S(1)} %bitcast.163, s32[1024]{0:T(1024)S(1)} %get-tuple-element.114, s32[1024]{0:T(1024)S(1)} %get-tuple-element.113), kind=kLoop, calls=%fused_computation.2 | loop fusion | flops 40894464 | bytes 2109440 | tf_op jit(solution)/shard_map/convert_element_type | solution.py:44
  18.3 1.7 multiply_add_fusion.2
  20.0 36.5 %welch.1 = bf16[2,16384,256]{2,1,0:T(8,128)(2,1)} custom-call(bf16[2,256,8192]{2,1,0:T(8,128)(2,1)} %signal_ref.1, bf16[2,1,8192]{2,1,0:T(2,128)(2,1)S(1)} %collective-permute-done.edge_ref, f32[2,1,8192]{2,1,0:T(1,128)S(1)} %broadcast_in_dim.2.weight_ref, bf16[1024,1024]{1,0:T(8,128)(2,1)S(1)} %fusion.1.table_ref), custom_call_target="tpu_custom_call" | custom-call | tf_op jit(solution)/shard_map/welch/pallas_call | solution.py:108
  56.6 24.4 %beams.5 = bf16[16,8,2,32,256]{4,3,2,1,0:T(8,128)(2,1)} custom-call(bf16[2,16,4,8,32,256]{5,4,3,2,1,0:T(8,128)(2,1)} %bitcast.140, f32[2,256,256]{2,1,0:T(8,128)S(1)} %get-tuple-element.41.refs_1_, f32[2,256,256]{2,1,0:T(8,128)S(1)} %get-tuple-element.42.refs_2_, f32[2,256,256]{2,1,0:T(8,128)S(1)} %copy-done.12, f32[2,256,256]{2,1,0:T(8,128)S(1)} %copy-done.10), custom_call_target="tpu_custom_call" | custom-call | flops 17179869184 | bytes 8388608 | tf_op jit(solution)/shard_map/beams/pallas_call | solution.py:189
  81.0 3.3 %dynamic-slice_bitcast_fusion.2 = bf16[8,8,64,256]{3,2,1,0:T(8,128)(2,1)} fusion(bf16[8,2,8,64,256]{4,3,2,1,0:T(8,128)(2,1)} %bitcast.155, s32[]{:T(128)S(6)} %select_n.206), kind=kLoop, calls=%fused_computation.34 | loop fusion | bytes 4194308 | tf_op jit(solution)/shard_map/jit(dynamic_index_in_dim)/squeeze | solution.py:218
  84.4 24.5 %beams.6 = bf16[16,8,2,32,256]{4,3,2,1,0:T(8,128)(2,1)} custom-call(bf16[2,16,4,8,32,256]{5,4,3,2,1,0:T(8,128)(2,1)} %bitcast.141, f32[2,256,256]{2,1,0:T(8,128)S(1)} %get-tuple-element.41.refs_1_, f32[2,256,256]{2,1,0:T(8,128)S(1)} %get-tuple-element.42.refs_2_, f32[2,256,256]{2,1,0:T(8,128)S(1)} %copy-done.13, f32[2,256,256]{2,1,0:T(8,128)S(1)} %copy-done.11, ...), custom_call_target="tpu_custom_call" | custom-call | flops 17179869184 | bytes 8388608 | tf_op jit(solution)/shard_map/beams/pallas_call | solution.py:189
  108.9 4.1 %fusion.4 = bf16[8,8,64,256]{3,2,1,0:T(8,128)(2,1)} fusion(bf16[8,8,64,256]{3,2,1,0:T(8,128)(2,1)} %collective-permute-done.1, bf16[8,2,8,64,256]{4,3,2,1,0:T(8,128)(2,1)S(1)} %bitcast.156, s32[]{:T(128)S(6)} %select_n.205), kind=kLoop, calls=%fused_computation.8 | loop fusion | flops 4194304 | bytes 6291460 | tf_op jit(solution)/shard_map/convert_element_type | solution.py:221
  113.0 1.5 dynamic-slice_bitcast_fusion.1
  114.5 0.5 collective-permute-start.3
  115.0 1.3 dynamic-slice_bitcast_fusion.7
  116.4 24.5 %beams.7 = bf16[16,8,2,32,256]{4,3,2,1,0:T(8,128)(2,1)} custom-call(bf16[2,16,4,8,32,256]{5,4,3,2,1,0:T(8,128)(2,1)} %bitcast.142, f32[2,256,256]{2,1,0:T(8,128)S(1)} %get-tuple-element.41.refs_1_, f32[2,256,256]{2,1,0:T(8,128)S(1)} %get-tuple-element.42.refs_2_, f32[2,256,256]{2,1,0:T(8,128)S(1)} %copy-done.13, f32[2,256,256]{2,1,0:T(8,128)S(1)} %copy-done.11, ...), custom_call_target="tpu_custom_call" | custom-call | flops 17179869184 | bytes 8388608 | tf_op jit(solution)/shard_map/beams/pallas_call | solution.py:189
  140.9 0.5 collective-permute-done.2
  141.5 1.8 convert_add_fusion.7
  143.3 0.6 copy-done.21
  143.9 4.0 %fusion.3 = bf16[8,8,64,256]{3,2,1,0:T(8,128)(2,1)} fusion(bf16[8,8,64,256]{3,2,1,0:T(8,128)(2,1)} %collective-permute-done.3, bf16[8,2,8,64,256]{4,3,2,1,0:T(8,128)(2,1)S(1)} %bitcast.154, s32[]{:T(128)S(6)} %select_n.205), kind=kLoop, calls=%fused_computation.6 | loop fusion | flops 4194304 | bytes 6291460 | tf_op jit(solution)/shard_map/convert_element_type | solution.py:221
  147.9 1.4 dynamic-slice_bitcast_fusion
  149.4 1.5 fusion.22
  150.9 1.4 collective-permute-start.6
  152.2 1.0 collective-permute-start.4
  153.2 1.3 dynamic-slice_bitcast_fusion.6
  154.6 1.8 collective-permute-start.7
  156.3 13.5 %beams.8 = bf16[16,4,2,32,256]{4,3,2,1,0:T(8,128)(2,1)S(1)} custom-call(bf16[2,16,8,4,32,256]{5,4,3,2,1,0:T(8,128)(2,1)} %bitcast.143, f32[2,256,256]{2,1,0:T(8,128)S(1)} %get-tuple-element.41.refs_1_, f32[2,256,256]{2,1,0:T(8,128)S(1)} %get-tuple-element.42.refs_2_, f32[2,256,256]{2,1,0:T(8,128)S(1)} %copy-done.13, f32[2,256,256]{2,1,0:T(8,128)S(1)} %copy-done.11, ...), custom_call_target="tpu_custom_call" | custom-call | flops 8589934592 | bytes 4194304 | tf_op jit(solution)/shard_map/beams/pallas_call | solution.py:189
  169.9 5.1 %collective-permute-done.5 = bf16[8,64,256]{2,1,0:T(8,128)(2,1)S(1)} collective-permute-done((bf16[8,64,256]{2,1,0:T(8,128)(2,1)S(1)}, bf16[8,64,256]{2,1,0:T(8,128)(2,1)S(1)}, u32[]{:S(2)}, u32[]{:S(2)}) %collective-permute-start.5) | collective-permute-done | bytes 262176 | tf_op jit(solution)/shard_map/ppermute | solution.py:233
  175.0 1.2 fusion.19
  176.2 3.4 %collective-permute-done.7 = bf16[4,8,64,256]{3,2,1,0:T(8,128)(2,1)S(1)} collective-permute-done((bf16[4,8,64,256]{3,2,1,0:T(8,128)(2,1)S(1)}, bf16[4,8,64,256]{3,2,1,0:T(8,128)(2,1)S(1)}, u32[]{:S(2)}, u32[]{:S(2)}) %collective-permute-start.7) | collective-permute-done | bytes 1048608 | tf_op jit(solution)/shard_map/ppermute | solution.py:220
  179.6 0.4 convert_add_fusion.6
  180.0 2.5 fusion.2
  182.7 2.7 collective-permute-start.11
  185.4 0.8 collective-permute-start.10
  186.2 1.2 collective-permute-start.9
  187.5 1.8 collective-permute-start.12
  189.5 13.4 %beams.9 = bf16[16,4,2,32,256]{4,3,2,1,0:T(8,128)(2,1)S(1)} custom-call(bf16[2,16,8,4,32,256]{5,4,3,2,1,0:T(8,128)(2,1)} %bitcast.144, f32[2,256,256]{2,1,0:T(8,128)S(1)} %get-tuple-element.41.refs_1_, f32[2,256,256]{2,1,0:T(8,128)S(1)} %get-tuple-element.42.refs_2_, f32[2,256,256]{2,1,0:T(8,128)S(1)} %copy-done.13, f32[2,256,256]{2,1,0:T(8,128)S(1)} %copy-done.11, ...), custom_call_target="tpu_custom_call" | custom-call | flops 8589934592 | bytes 4194304 | tf_op jit(solution)/shard_map/beams/pallas_call | solution.py:189
  202.9 4.9 %collective-permute-done.10 = bf16[8,64,256]{2,1,0:T(8,128)(2,1)S(1)} collective-permute-done((bf16[8,64,256]{2,1,0:T(8,128)(2,1)S(1)}, bf16[8,64,256]{2,1,0:T(8,128)(2,1)S(1)}, u32[]{:S(2)}, u32[]{:S(2)}) %collective-permute-start.10) | collective-permute-done | bytes 262176 | tf_op jit(solution)/shard_map/ppermute | solution.py:233
  207.8 1.1 fusion.17
  208.9 2.0 collective-permute-done.12
  210.8 0.4 convert_add_fusion.5
  211.2 1.6 fusion.13
  213.1 1.5 collective-permute-start.17
  214.8 2.3 collective-permute-start.16
  217.1 0.7 collective-permute-start.15
  217.8 0.3 collective-permute-start.14
  218.1 5.8 %collective-permute-done.16 = bf16[8,64,256]{2,1,0:T(8,128)(2,1)S(1)} collective-permute-done((bf16[8,64,256]{2,1,0:T(8,128)(2,1)S(1)}, bf16[8,64,256]{2,1,0:T(8,128)(2,1)S(1)}, u32[]{:S(2)}, u32[]{:S(2)}) %collective-permute-start.16) | collective-permute-done | bytes 262176 | tf_op jit(solution)/shard_map/ppermute | solution.py:233
  223.8 17.2 %collective-permute-done.15 = bf16[8,64,256]{2,1,0:T(8,128)(2,1)S(1)} collective-permute-done((bf16[8,64,256]{2,1,0:T(8,128)(2,1)S(1)}, bf16[8,64,256]{2,1,0:T(8,128)(2,1)S(1)}, u32[]{:S(2)}, u32[]{:S(2)}) %collective-permute-start.15) | collective-permute-done | bytes 262176 | tf_op jit(solution)/shard_map/ppermute | solution.py:233
  241.3 0.4 fusion.12
  241.8 0.4 collective-permute-start.22
  242.3 1.6 collective-permute-start.20
  244.0 1.9 collective-permute-start.19
  245.9 2.0 collective-permute-done.21
  247.9 7.0 %collective-permute-done.20 = bf16[4,64,256]{2,1,0:T(8,128)(2,1)S(1)} collective-permute-done((bf16[4,64,256]{2,1,0:T(8,128)(2,1)S(1)}, bf16[4,64,256]{2,1,0:T(8,128)(2,1)S(1)}, u32[]{:S(2)}, u32[]{:S(2)}) %collective-permute-start.20) | collective-permute-done | bytes 131104 | tf_op jit(solution)/shard_map/ppermute | solution.py:233
  255.2 0.7 fusion.38
  256.0 1.4 collective-permute-start.24
  257.4 2.0 collective-permute-start.23
  259.4 2.2 collective-permute-done.25
  261.6 8.1 %collective-permute-done.24 = bf16[4,64,256]{2,1,0:T(8,128)(2,1)S(1)} collective-permute-done((bf16[4,64,256]{2,1,0:T(8,128)(2,1)S(1)}, bf16[4,64,256]{2,1,0:T(8,128)(2,1)S(1)}, u32[]{:S(2)}, u32[]{:S(2)}) %collective-permute-start.24) | collective-permute-done | bytes 131104 | tf_op jit(solution)/shard_map/ppermute | solution.py:233
  270.1 1.6 collective-permute-start.26
  271.7 2.2 collective-permute-done.26
  273.9 0.6 bitcast_add_fusion.5
  (95 shorter events, 2.2 us)
Async XLA Ops:
  1.0 19.1 %collective-permute-start = (bf16[2,1,8192]{2,1,0:T(2,128)(2,1)S(1)}, bf16[2,1,8192]{2,1,0:T(2,128)(2,1)S(1)}, u32[]{:S(2)}, u32[]{:S(2)}) collective-permute-start(bf16[2,1,8192]{2,1,0:T(2,128)(2,1)S(1)} %slice.3), channel_id=1, source_target_pairs={{0,30},{2,0},{4,2},{6,4},{8,6},{10,8},{12,10},{14,12},{16,14},{18,... | collective-permute-start | bytes 98312 | tf_op jit(solution)/shard_map/ppermute | solution.py:271
  11.7 6.5 %copy-start = (f32[2,256,256]{2,1,0:T(8,128)}, f32[2,256,256]{2,1,0:T(8,128)S(1)}, u32[]{:S(2)}) copy-start(f32[2,256,256]{2,1,0:T(8,128)S(1)} %get-tuple-element.80.refs_5_) | copy-start | bytes 1572868
  11.8 6.5 %copy-start.2 = (f32[2,256,256]{2,1,0:T(8,128)}, f32[2,256,256]{2,1,0:T(8,128)S(1)}, u32[]{:S(2)}) copy-start(f32[2,256,256]{2,1,0:T(8,128)S(1)} %get-tuple-element.81.refs_6_) | copy-start | bytes 1572868
  11.8 6.5 %copy-start.4 = (f32[2,256,256]{2,1,0:T(8,128)}, f32[2,256,256]{2,1,0:T(8,128)S(1)}, u32[]{:S(2)}) copy-start(f32[2,256,256]{2,1,0:T(8,128)S(1)} %get-tuple-element.82.refs_6_) | copy-start | bytes 1572868
  11.8 6.5 %copy-start.6 = (f32[2,256,256]{2,1,0:T(8,128)}, f32[2,256,256]{2,1,0:T(8,128)S(1)}, u32[]{:S(2)}) copy-start(f32[2,256,256]{2,1,0:T(8,128)S(1)} %get-tuple-element.83.refs_5_) | copy-start | bytes 1572868
  11.8 8.2 %copy-start.23 = (f32[2,8192]{1,0:T(2,128)S(1)}, f32[2,8192]{1,0:T(2,128)}, u32[]{:S(2)}) copy-start(f32[2,8192]{1,0:T(2,128)} %param.7) | copy-start | bytes 196612
  20.0 36.6 %copy-start.10 = (f32[2,256,256]{2,1,0:T(8,128)S(1)}, f32[2,256,256]{2,1,0:T(8,128)}, u32[]{:S(2)}) copy-start(f32[2,256,256]{2,1,0:T(8,128)} %get-tuple-element.102.refs_4_) | copy-start | bytes 1572868
  20.0 36.5 %copy-start.12 = (f32[2,256,256]{2,1,0:T(8,128)S(1)}, f32[2,256,256]{2,1,0:T(8,128)}, u32[]{:S(2)}) copy-start(f32[2,256,256]{2,1,0:T(8,128)} %get-tuple-element.103.refs_3_) | copy-start | bytes 1572868
  81.0 3.3 %copy-start.5 = (f32[2,256,256]{2,1,0:T(8,128)S(1)}, f32[2,256,256]{2,1,0:T(8,128)}, u32[]{:S(2)}) copy-start(f32[2,256,256]{2,1,0:T(8,128)} %copy-done.4) | copy-start | bytes 1572868
  81.0 3.3 %copy-start.7 = (f32[2,256,256]{2,1,0:T(8,128)S(1)}, f32[2,256,256]{2,1,0:T(8,128)}, u32[]{:S(2)}) copy-start(f32[2,256,256]{2,1,0:T(8,128)} %copy-done.6) | copy-start | bytes 1572868
  81.0 3.3 %copy-start.11 = (f32[2,256,256]{2,1,0:T(8,128)S(1)}, f32[2,256,256]{2,1,0:T(8,128)}, u32[]{:S(2)}) copy-start(f32[2,256,256]{2,1,0:T(8,128)} %get-tuple-element.102.refs_4_) | copy-start | bytes 1572868
  81.0 3.4 %copy-start.13 = (f32[2,256,256]{2,1,0:T(8,128)S(1)}, f32[2,256,256]{2,1,0:T(8,128)}, u32[]{:S(2)}) copy-start(f32[2,256,256]{2,1,0:T(8,128)} %get-tuple-element.103.refs_3_) | copy-start | bytes 1572868
  84.3 24.6 %collective-permute-start.1 = (bf16[8,8,64,256]{3,2,1,0:T(8,128)(2,1)}, bf16[8,8,64,256]{3,2,1,0:T(8,128)(2,1)}, u32[]{:S(2)}, u32[]{:S(2)}) collective-permute-start(bf16[8,8,64,256]{3,2,1,0:T(8,128)(2,1)} %dynamic-slice_bitcast_fusion.2), channel_id=1, source_target_pairs={{0,2},{2,0},{4,6},{6,4},{8,10},{10,8},{12,14},{14,12},{16,18},{18,... | collective-permute-start | bytes 6291464 | tf_op jit(solution)/shard_map/ppermute | solution.py:220
  84.3 24.6 %copy-start.22 = (bf16[16,8,2,32,256]{4,3,2,1,0:T(8,128)(2,1)S(1)}, bf16[16,8,2,32,256]{4,3,2,1,0:T(8,128)(2,1)}, u32[]{:S(2)}) copy-start(bf16[16,8,2,32,256]{4,3,2,1,0:T(8,128)(2,1)} %beams.5) | copy-start | bytes 12582916
  108.9 4.1 %copy-start.20 = (bf16[16,8,2,32,256]{4,3,2,1,0:T(8,128)(2,1)S(1)}, bf16[16,8,2,32,256]{4,3,2,1,0:T(8,128)(2,1)}, u32[]{:S(2)}) copy-start(bf16[16,8,2,32,256]{4,3,2,1,0:T(8,128)(2,1)} %beams.6) | copy-start | bytes 12582916
  113.0 3.4 %copy-start.1 = (f32[2,256,256]{2,1,0:T(8,128)S(1)}, f32[2,256,256]{2,1,0:T(8,128)}, u32[]{:S(2)}) copy-start(f32[2,256,256]{2,1,0:T(8,128)} %copy-done) | copy-start | bytes 1572868
  113.0 3.4 %copy-start.3 = (f32[2,256,256]{2,1,0:T(8,128)S(1)}, f32[2,256,256]{2,1,0:T(8,128)}, u32[]{:S(2)}) copy-start(f32[2,256,256]{2,1,0:T(8,128)} %copy-done.2) | copy-start | bytes 1572868
  114.5 28.8 %collective-permute-start.3 = (bf16[8,8,64,256]{3,2,1,0:T(8,128)(2,1)}, bf16[8,8,64,256]{3,2,1,0:T(8,128)(2,1)}, u32[]{:S(2)}, u32[]{:S(2)}) collective-permute-start(bf16[8,8,64,256]{3,2,1,0:T(8,128)(2,1)} %dynamic-slice_bitcast_fusion.1), channel_id=1, source_target_pairs={{0,2},{2,0},{4,6},{6,4},{8,10},{10,8},{12,14},{14,12},{16,18},{18,... | collective-permute-start | bytes 6291464 | tf_op jit(solution)/shard_map/ppermute | solution.py:220
  116.3 25.1 %collective-permute-start.2 = (bf16[4,8,64,256]{3,2,1,0:T(8,128)(2,1)S(1)}, bf16[4,8,64,256]{3,2,1,0:T(8,128)(2,1)S(1)}, u32[]{:S(2)}, u32[]{:S(2)}) collective-permute-start(bf16[4,8,64,256]{3,2,1,0:T(8,128)(2,1)S(1)} %dynamic-slice_bitcast_fusion.7), channel_id=1, source_target_pairs={{0,4},{2,6},{4,0},{6,2},{8,12},{10,14},{12,8},{14,10},{16,20},{18,... | collective-permute-start | bytes 3145736 | tf_op jit(solution)/shard_map/ppermute | solution.py:220
  116.4 25.1 %copy-start.17 = (bf16[8,8,64,256]{3,2,1,0:T(8,128)(2,1)S(1)}, bf16[8,8,64,256]{3,2,1,0:T(8,128)(2,1)}, u32[]{:S(2)}) copy-start(bf16[8,8,64,256]{3,2,1,0:T(8,128)(2,1)} %fusion.4) | copy-start | bytes 6291460
  140.9 2.9 %copy-start.21 = (bf16[16,8,2,32,256]{4,3,2,1,0:T(8,128)(2,1)S(1)}, bf16[16,8,2,32,256]{4,3,2,1,0:T(8,128)(2,1)}, u32[]{:S(2)}) copy-start(bf16[16,8,2,32,256]{4,3,2,1,0:T(8,128)(2,1)} %beams.6) | copy-start | bytes 12582916
  143.3 4.6 %copy-start.18 = (bf16[16,8,2,32,256]{4,3,2,1,0:T(8,128)(2,1)S(1)}, bf16[16,8,2,32,256]{4,3,2,1,0:T(8,128)(2,1)}, u32[]{:S(2)}) copy-start(bf16[16,8,2,32,256]{4,3,2,1,0:T(8,128)(2,1)} %beams.7) | copy-start | bytes 12582916
  147.9 8.4 %copy-start.14 = (f32[2,256,256]{2,1,0:T(8,128)S(1)}, f32[2,256,256]{2,1,0:T(8,128)}, u32[]{:S(2)}) copy-start(f32[2,256,256]{2,1,0:T(8,128)} %get-tuple-element.90.refs_6_) | copy-start | bytes 1572868
  147.9 8.4 %copy-start.15 = (f32[2,256,256]{2,1,0:T(8,128)S(1)}, f32[2,256,256]{2,1,0:T(8,128)}, u32[]{:S(2)}) copy-start(f32[2,256,256]{2,1,0:T(8,128)} %get-tuple-element.91.refs_5_) | copy-start | bytes 1572868
  149.4 30.6 %collective-permute-start.8 = (bf16[8,8,64,256]{3,2,1,0:T(8,128)(2,1)}, bf16[8,8,64,256]{3,2,1,0:T(8,128)(2,1)}, u32[]{:S(2)}, u32[]{:S(2)}) collective-permute-start(bf16[8,8,64,256]{3,2,1,0:T(8,128)(2,1)} %dynamic-slice_bitcast_fusion), channel_id=1, source_target_pairs={{0,2},{2,0},{4,6},{6,4},{8,10},{10,8},{12,14},{14,12},{16,18},{18,... | collective-permute-start | bytes 6291464 | tf_op jit(solution)/shard_map/ppermute | solution.py:220
  150.9 19.0 %collective-permute-start.6 = (bf16[8,64,256]{2,1,0:T(8,128)(2,1)S(1)}, bf16[8,64,256]{2,1,0:T(8,128)(2,1)S(1)}, u32[]{:S(2)}, u32[]{:S(2)}) collective-permute-start(bf16[8,64,256]{2,1,0:T(8,128)(2,1)S(1)} %get-tuple-element.93), channel_id=1, source_target_pairs={{0,24},{2,26},{4,28},{6,30},{8,0},{10,2},{12,4},{14,6},{16,8},{18,... | collective-permute-start | bytes 786440 | tf_op jit(solution)/shard_map/ppermute | solution.py:233
  152.2 22.8 %collective-permute-start.5 = (bf16[8,64,256]{2,1,0:T(8,128)(2,1)S(1)}, bf16[8,64,256]{2,1,0:T(8,128)(2,1)S(1)}, u32[]{:S(2)}, u32[]{:S(2)}) collective-permute-start(bf16[8,64,256]{2,1,0:T(8,128)(2,1)S(1)} %get-tuple-element.94), channel_id=1, source_target_pairs={{0,16},{2,18},{4,20},{6,22},{8,24},{10,26},{12,28},{14,30},{16,0},... | collective-permute-start | bytes 786440 | tf_op jit(solution)/shard_map/ppermute | solution.py:233
  152.2 22.8 %collective-permute-start.4 = (bf16[8,64,256]{2,1,0:T(8,128)(2,1)S(1)}, bf16[8,64,256]{2,1,0:T(8,128)(2,1)S(1)}, u32[]{:S(2)}, u32[]{:S(2)}) collective-permute-start(bf16[8,64,256]{2,1,0:T(8,128)(2,1)S(1)} %get-tuple-element.92), channel_id=1, source_target_pairs={{0,8},{2,10},{4,12},{6,14},{8,16},{10,18},{12,20},{14,22},{16,24},... | collective-permute-start | bytes 786440 | tf_op jit(solution)/shard_map/ppermute | solution.py:233
  154.6 25.0 %collective-permute-start.7 = (bf16[4,8,64,256]{3,2,1,0:T(8,128)(2,1)S(1)}, bf16[4,8,64,256]{3,2,1,0:T(8,128)(2,1)S(1)}, u32[]{:S(2)}, u32[]{:S(2)}) collective-permute-start(bf16[4,8,64,256]{3,2,1,0:T(8,128)(2,1)S(1)} %dynamic-slice_bitcast_fusion.6), channel_id=1, source_target_pairs={{0,4},{2,6},{4,0},{6,2},{8,12},{10,14},{12,8},{14,10},{16,20},{18,... | collective-permute-start | bytes 3145736 | tf_op jit(solution)/shard_map/ppermute | solution.py:220
  156.3 23.3 %copy-start.16 = (bf16[8,8,64,256]{3,2,1,0:T(8,128)(2,1)S(1)}, bf16[8,8,64,256]{3,2,1,0:T(8,128)(2,1)}, u32[]{:S(2)}) copy-start(bf16[8,8,64,256]{3,2,1,0:T(8,128)(2,1)} %fusion.3) | copy-start | bytes 6291460
  169.9 10.1 %copy-start.19 = (bf16[16,8,2,32,256]{4,3,2,1,0:T(8,128)(2,1)S(1)}, bf16[16,8,2,32,256]{4,3,2,1,0:T(8,128)(2,1)}, u32[]{:S(2)}) copy-start(bf16[16,8,2,32,256]{4,3,2,1,0:T(8,128)(2,1)} %beams.7) | copy-start | bytes 12582916
  182.5 7.0 %copy-start.8 = (f32[2,256,256]{2,1,0:T(8,128)S(1)}, f32[2,256,256]{2,1,0:T(8,128)}, u32[]{:S(2)}) copy-start(f32[2,256,256]{2,1,0:T(8,128)} %get-tuple-element.77.refs_6_) | copy-start | bytes 1572868
  182.6 7.0 %copy-start.9 = (f32[2,256,256]{2,1,0:T(8,128)S(1)}, f32[2,256,256]{2,1,0:T(8,128)}, u32[]{:S(2)}) copy-start(f32[2,256,256]{2,1,0:T(8,128)} %get-tuple-element.101.refs_5_) | copy-start | bytes 1572868
  182.7 20.2 %collective-permute-start.11 = (bf16[8,64,256]{2,1,0:T(8,128)(2,1)S(1)}, bf16[8,64,256]{2,1,0:T(8,128)(2,1)S(1)}, u32[]{:S(2)}, u32[]{:S(2)}) collective-permute-start(bf16[8,64,256]{2,1,0:T(8,128)(2,1)S(1)} %get-tuple-element.88), channel_id=1, source_target_pairs={{0,24},{2,26},{4,28},{6,30},{8,0},{10,2},{12,4},{14,6},{16,8},{18,... | collective-permute-start | bytes 786440 | tf_op jit(solution)/shard_map/ppermute | solution.py:233
  185.4 22.4 %collective-permute-start.10 = (bf16[8,64,256]{2,1,0:T(8,128)(2,1)S(1)}, bf16[8,64,256]{2,1,0:T(8,128)(2,1)S(1)}, u32[]{:S(2)}, u32[]{:S(2)}) collective-permute-start(bf16[8,64,256]{2,1,0:T(8,128)(2,1)S(1)} %get-tuple-element.89), channel_id=1, source_target_pairs={{0,16},{2,18},{4,20},{6,22},{8,24},{10,26},{12,28},{14,30},{16,0},... | collective-permute-start | bytes 786440 | tf_op jit(solution)/shard_map/ppermute | solution.py:233
  186.2 21.6 %collective-permute-start.9 = (bf16[8,64,256]{2,1,0:T(8,128)(2,1)S(1)}, bf16[8,64,256]{2,1,0:T(8,128)(2,1)}, u32[]{:S(2)}, u32[]{:S(2)}) collective-permute-start(bf16[8,64,256]{2,1,0:T(8,128)(2,1)S(1)} %get-tuple-element.87), channel_id=1, source_target_pairs={{0,8},{2,10},{4,12},{6,14},{8,16},{10,18},{12,20},{14,22},{16,24},... | collective-permute-start | bytes 786440 | tf_op jit(solution)/shard_map/ppermute | solution.py:233
  187.5 23.3 %collective-permute-start.12 = (bf16[4,8,64,256]{3,2,1,0:T(8,128)(2,1)S(1)}, bf16[4,8,64,256]{3,2,1,0:T(8,128)(2,1)S(1)}, u32[]{:S(2)}, u32[]{:S(2)}) collective-permute-start(bf16[4,8,64,256]{3,2,1,0:T(8,128)(2,1)S(1)} %dynamic-slice_bitcast_fusion.5), channel_id=1, source_target_pairs={{0,4},{2,6},{4,0},{6,2},{8,12},{10,14},{12,8},{14,10},{16,20},{18,... | collective-permute-start | bytes 3145736 | tf_op jit(solution)/shard_map/ppermute | solution.py:220
  189.4 21.8 %collective-permute-start.13 = (bf16[8,4,64,256]{3,2,1,0:T(8,128)(2,1)S(1)}, bf16[8,4,64,256]{3,2,1,0:T(8,128)(2,1)}, u32[]{:S(2)}, u32[]{:S(2)}) collective-permute-start(bf16[8,4,64,256]{3,2,1,0:T(8,128)(2,1)S(1)} %dynamic-slice_bitcast_fusion.4), channel_id=1, source_target_pairs={{0,2},{2,0},{4,6},{6,4},{8,10},{10,8},{12,14},{14,12},{16,18},{18,... | collective-permute-start | bytes 3145736 | tf_op jit(solution)/shard_map/ppermute | solution.py:220
  213.0 28.3 %collective-permute-start.18 = (bf16[8,4,64,256]{3,2,1,0:T(8,128)(2,1)S(1)}, bf16[8,4,64,256]{3,2,1,0:T(8,128)(2,1)S(1)}, u32[]{:S(2)}, u32[]{:S(2)}) collective-permute-start(bf16[8,4,64,256]{3,2,1,0:T(8,128)(2,1)S(1)} %dynamic-slice_bitcast_fusion.3), channel_id=1, source_target_pairs={{0,2},{2,0},{4,6},{6,4},{8,10},{10,8},{12,14},{14,12},{16,18},{18,... | collective-permute-start | bytes 3145736 | tf_op jit(solution)/shard_map/ppermute | solution.py:220
  213.1 28.0 %collective-permute-start.17 = (bf16[4,4,64,256]{3,2,1,0:T(8,128)(2,1)S(1)}, bf16[4,4,64,256]{3,2,1,0:T(8,128)(2,1)S(1)}, u32[]{:S(2)}, u32[]{:S(2)}) collective-permute-start(bf16[4,4,64,256]{3,2,1,0:T(8,128)(2,1)S(1)} %dynamic-slice_bitcast_fusion.9), channel_id=1, source_target_pairs={{0,4},{2,6},{4,0},{6,2},{8,12},{10,14},{12,8},{14,10},{16,20},{18,... | collective-permute-start | bytes 1572872 | tf_op jit(solution)/shard_map/ppermute | solution.py:220
  214.8 9.1 %collective-permute-start.16 = (bf16[8,64,256]{2,1,0:T(8,128)(2,1)S(1)}, bf16[8,64,256]{2,1,0:T(8,128)(2,1)S(1)}, u32[]{:S(2)}, u32[]{:S(2)}) collective-permute-start(bf16[8,64,256]{2,1,0:T(8,128)(2,1)S(1)} %get-tuple-element.85), channel_id=1, source_target_pairs={{0,24},{2,26},{4,28},{6,30},{8,0},{10,2},{12,4},{14,6},{16,8},{18,... | collective-permute-start | bytes 786440 | tf_op jit(solution)/shard_map/ppermute | solution.py:233
  217.1 24.0 %collective-permute-start.15 = (bf16[8,64,256]{2,1,0:T(8,128)(2,1)S(1)}, bf16[8,64,256]{2,1,0:T(8,128)(2,1)S(1)}, u32[]{:S(2)}, u32[]{:S(2)}) collective-permute-start(bf16[8,64,256]{2,1,0:T(8,128)(2,1)S(1)} %get-tuple-element.86), channel_id=1, source_target_pairs={{0,16},{2,18},{4,20},{6,22},{8,24},{10,26},{12,28},{14,30},{16,0},... | collective-permute-start | bytes 786440 | tf_op jit(solution)/shard_map/ppermute | solution.py:233
  217.8 23.2 %collective-permute-start.14 = (bf16[8,64,256]{2,1,0:T(8,128)(2,1)S(1)}, bf16[8,64,256]{2,1,0:T(8,128)(2,1)S(1)}, u32[]{:S(2)}, u32[]{:S(2)}) collective-permute-start(bf16[8,64,256]{2,1,0:T(8,128)(2,1)S(1)} %get-tuple-element.84), channel_id=1, source_target_pairs={{0,8},{2,10},{4,12},{6,14},{8,16},{10,18},{12,20},{14,22},{16,24},... | collective-permute-start | bytes 786440 | tf_op jit(solution)/shard_map/ppermute | solution.py:233
  241.8 13.3 %collective-permute-start.22 = (bf16[4,4,64,256]{3,2,1,0:T(8,128)(2,1)S(1)}, bf16[4,4,64,256]{3,2,1,0:T(8,128)(2,1)S(1)}, u32[]{:S(2)}, u32[]{:S(2)}) collective-permute-start(bf16[4,4,64,256]{3,2,1,0:T(8,128)(2,1)S(1)} %dynamic-slice_bitcast_fusion.8), channel_id=1, source_target_pairs={{0,4},{2,6},{4,0},{6,2},{8,12},{10,14},{12,8},{14,10},{16,20},{18,... | collective-permute-start | bytes 1572872 | tf_op jit(solution)/shard_map/ppermute | solution.py:220
  242.3 5.6 %collective-permute-start.21 = (bf16[4,64,256]{2,1,0:T(8,128)(2,1)S(1)}, bf16[4,64,256]{2,1,0:T(8,128)(2,1)S(1)}, u32[]{:S(2)}, u32[]{:S(2)}) collective-permute-start(bf16[4,64,256]{2,1,0:T(8,128)(2,1)S(1)} %get-tuple-element.99), channel_id=1, source_target_pairs={{0,24},{2,26},{4,28},{6,30},{8,0},{10,2},{12,4},{14,6},{16,8},{18,... | collective-permute-start | bytes 393224 | tf_op jit(solution)/shard_map/ppermute | solution.py:233
  242.3 12.5 %collective-permute-start.20 = (bf16[4,64,256]{2,1,0:T(8,128)(2,1)S(1)}, bf16[4,64,256]{2,1,0:T(8,128)(2,1)S(1)}, u32[]{:S(2)}, u32[]{:S(2)}) collective-permute-start(bf16[4,64,256]{2,1,0:T(8,128)(2,1)S(1)} %get-tuple-element.100), channel_id=1, source_target_pairs={{0,16},{2,18},{4,20},{6,22},{8,24},{10,26},{12,28},{14,30},{16,0},... | collective-permute-start | bytes 393224 | tf_op jit(solution)/shard_map/ppermute | solution.py:233
  244.0 10.9 %collective-permute-start.19 = (bf16[4,64,256]{2,1,0:T(8,128)(2,1)S(1)}, bf16[4,64,256]{2,1,0:T(8,128)(2,1)S(1)}, u32[]{:S(2)}, u32[]{:S(2)}) collective-permute-start(bf16[4,64,256]{2,1,0:T(8,128)(2,1)S(1)} %get-tuple-element.98), channel_id=1, source_target_pairs={{0,8},{2,10},{4,12},{6,14},{8,16},{10,18},{12,20},{14,22},{16,24},... | collective-permute-start | bytes 393224 | tf_op jit(solution)/shard_map/ppermute | solution.py:233
  256.0 5.6 %collective-permute-start.25 = (bf16[4,64,256]{2,1,0:T(8,128)(2,1)}, bf16[4,64,256]{2,1,0:T(8,128)(2,1)S(1)}, u32[]{:S(2)}, u32[]{:S(2)}) collective-permute-start(bf16[4,64,256]{2,1,0:T(8,128)(2,1)} %get-tuple-element.96), channel_id=1, source_target_pairs={{0,24},{2,26},{4,28},{6,30},{8,0},{10,2},{12,4},{14,6},{16,8},{18,... | collective-permute-start | bytes 393224 | tf_op jit(solution)/shard_map/ppermute | solution.py:233
  256.0 13.7 %collective-permute-start.24 = (bf16[4,64,256]{2,1,0:T(8,128)(2,1)S(1)}, bf16[4,64,256]{2,1,0:T(8,128)(2,1)S(1)}, u32[]{:S(2)}, u32[]{:S(2)}) collective-permute-start(bf16[4,64,256]{2,1,0:T(8,128)(2,1)S(1)} %get-tuple-element.97), channel_id=1, source_target_pairs={{0,16},{2,18},{4,20},{6,22},{8,24},{10,26},{12,28},{14,30},{16,0},... | collective-permute-start | bytes 393224 | tf_op jit(solution)/shard_map/ppermute | solution.py:233
  257.4 12.3 %collective-permute-start.23 = (bf16[4,64,256]{2,1,0:T(8,128)(2,1)S(1)}, bf16[4,64,256]{2,1,0:T(8,128)(2,1)S(1)}, u32[]{:S(2)}, u32[]{:S(2)}) collective-permute-start(bf16[4,64,256]{2,1,0:T(8,128)(2,1)S(1)} %get-tuple-element.95), channel_id=1, source_target_pairs={{0,8},{2,10},{4,12},{6,14},{8,16},{10,18},{12,20},{14,22},{16,24},... | collective-permute-start | bytes 393224 | tf_op jit(solution)/shard_map/ppermute | solution.py:233
  270.1 3.8 %collective-permute-start.26 = (f32[16,256]{1,0:T(8,128)S(1)}, f32[16,256]{1,0:T(8,128)S(1)}, u32[]{:S(2)}, u32[]{:S(2)}) collective-permute-start(f32[16,256]{1,0:T(8,128)S(1)} %dynamic-slice_bitcast_fusion.10), channel_id=1, source_target_pairs={{0,1},{1,0},{2,3},{3,2},{4,5},{5,4},{6,7},{7,6},{8,9},{9,8},{10,11... | collective-permute-start | bytes 49160 | tf_op jit(solution)/shard_map/ppermute | solution.py:261
